TPU v7x, 32 devices: a whole 2x2x4 slice. The times are simulated.
32 devices in a mesh: groups: 2 (over y), ex: 8 (over z, x), proj: 2 (over core).
Axes of the slice: x: 2, y: 2, z: 4, core: 2. Of those that a mesh axis runs over, the one named last changes fastest.
Arguments:
- train_factors: bfloat16 [16384, 4, 128], P(('groups', 'ex'), 'proj'), parts along dimension 0, may hold values from -600 to 600, as said below
- query_grads: float32 [256, 4, 4096], P(('groups', 'ex'), 'proj'), parts along dimension 0, may hold values from -600 to 600, as said below
Outputs:
- scores: float32 [16384, 128], P(('groups', 'ex'), 'proj'), parts along dimension 0
There are 2 independent parts, one for each index of `groups`. A program takes and returns all parts, laid end to end along the dimension named above; each array names one. Nothing has to cross between parts.
Inputs may be any that keep to these rules, and one draw needn't show every extreme that they name: `train_factors`: real-valued projected factors of mixed scale. `query_grads`: real-valued projected gradients of mixed scale.
All inputs are finite; a program needn't handle non-finite values.
Results may differ from a plain program's by a relative error of at most 0.005.
Values may be sent and summed in bfloat16 or wider, within the bound.
No kernel may reach another device: no remote copies, remote signals or barrier semaphores. Data moves between devices by JAX's collectives and lax.ppermute only.
A program may use at most 64 MiB of HBM per device.

v0:
```python
import math

import jax
import jax.numpy as jnp
from jax import lax
from jax.sharding import PartitionSpec as P

epsilon = 1e-06


def contract_tokens(train_factors, query_rows):
    token_count, module_count, doubled = train_factors.shape
    rank = doubled // 2
    query_count = query_rows.shape[0]
    query_mats = query_rows.reshape(query_count, module_count, rank, rank)
    block_rows = math.gcd(token_count, max(8, 16384 // query_count))
    blocks = train_factors.reshape(token_count // block_rows, block_rows, module_count, doubled)

    def one_block(rows):
        act_rows = rows[:, :, :rank]
        grad_rows = rows[:, :, rank:]
        inner = jnp.einsum(
            "tmj,qmij->tmqi", grad_rows, query_mats, preferred_element_type=jnp.float32
        )
        inner = inner.astype(jnp.bfloat16)
        return jnp.einsum("tmi,tmqi->tq", act_rows, inner, preferred_element_type=jnp.float32)

    return lax.map(one_block, blocks).reshape(token_count, query_count)


def local(train_factors, query_grads):
    rank = train_factors.shape[2] // 2
    full_width = train_factors.shape[1] * lax.axis_size("proj") * rank * rank
    act_all = train_factors[:, :, :rank].astype(jnp.float32)
    grad_all = train_factors[:, :, rank:].astype(jnp.float32)
    train_part = jnp.sum(
        jnp.sum(act_all * act_all, axis=2) * jnp.sum(grad_all * grad_all, axis=2), axis=1
    )
    query_part = jnp.sum(query_grads * query_grads, axis=(1, 2))
    train_sq, query_sq = lax.psum((train_part, query_part), "proj")
    query_unit = (query_grads * lax.rsqrt(query_sq / full_width + epsilon)[:, None, None]).astype(
        jnp.bfloat16
    )
    block_scores = contract_tokens(
        train_factors, lax.all_gather(query_unit, "ex", axis=0, tiled=True)
    )
    summed = lax.psum_scatter(block_scores, "proj", scatter_dimension=1, tiled=True)
    train_scale = lax.rsqrt(train_sq / full_width + epsilon) / jnp.sqrt(jnp.float32(full_width))
    return summed * train_scale[:, None]


def solution(mesh):
    return jax.shard_map(
        local,
        mesh=mesh,
        in_specs=(P(("groups", "ex"), "proj", None), P(("groups", "ex"), "proj", None)),
        out_specs=P(("groups", "ex"), "proj"),
        check_vma=False,
    )
```

profile of v0, /device:TPU:1, one launch (start us, length us, event | category | flops | bytes accessed | tf_op | source)
XLA Modules:
  0.0 133.1 jit_solution(10443118995358652625)
XLA Ops:
  6.5 0.0 all-gather.2.cloned.1.call-start
  6.5 4.2 %multiply_reduce_fusion.1 = (f32[1024,2]{1,0:T(8,128)S(1)}, f32[1024,2]{1,0:T(8,128)S(1)}) fusion(bf16[1024,2,128]{2,1,0:T(2,128)(2,1)} %param.4), kind=kLoop, calls=%fused_computation.6 | loop fusion | flops 782336 | bytes 540672 | tf_op jit(solution)/shard_map/reduce_sum | solution.py:37
  10.7 1.4 %multiply_reduce_fusion.4 = f32[16]{0:T(128)S(1)} fusion(f32[16,2,4096]{2,1,0:T(2,128)} %param.5), kind=kLoop, calls=%fused_computation.10 | loop fusion | flops 262128 | bytes 524352 | tf_op jit(solution)/shard_map/reduce_sum | solution.py:39
  12.1 0.2 multiply_reduce_fusion.3
  12.3 2.5 %all-reduce = (f32[16]{0:T(128)S(1)}, f32[1024]{0:T(1024)S(1)}) all-reduce(f32[16]{0:T(128)S(1)} %multiply_reduce_fusion.4, f32[1024]{0:T(1024)S(1)} %multiply_reduce_fusion.3), channel_id=1, replica_groups=mesh['groups'=2,'ex'=8,'proj'=2] {'proj'}, use_global_device_ids=true, to_apply=%region_1.0 | all-reduce | flops 1040 | bytes 8320 | tf_op jit(solution)/shard_map/psum | solution.py:40
  14.8 2.0 %multiply_convert_fusion = bf16[16,2,4096]{2,1,0:T(2,128)(2,1)} fusion(f32[16,2,4096]{2,1,0:T(2,128)} %param.5, f32[16]{0:T(128)S(1)} %add_rsqrt_fusion), kind=kLoop, calls=%fused_computation.9 | loop fusion | flops 262144 | bytes 786496 | tf_op jit(solution)/shard_map/convert_element_type | solution.py:41
  16.8 0.0 all-gather.2.cloned.1.call-update
  16.9 0.0 reduce-scatter.2.cloned.1.call-start
  16.9 50.3 %all-gather.2.cloned.1.call-done = bf16[128,2,4096]{2,1,0:T(2,128)(2,1)} async-done(((bf16[16,2,4096]{2,1,0:T(2,128)(2,1)}), bf16[128,2,4096]{2,1,0:T(2,128)(2,1)}) %all-gather.2.cloned.1.call-update) | async-done | bytes 2097168 | tf_op jit(solution)/shard_map/all_gather | solution.py:45
  67.3 4.9 %copy.22 = bf16[128,2,4096]{0,2,1:T(8,128)(2,1)S(1)} copy(bf16[128,2,4096]{2,1,0:T(2,128)(2,1)} %all-gather.2.cloned.1.call-done) | data formatting | bytes 4194304 | tf_op jit(solution)/shard_map/all_gather | solution.py:45
  72.2 6.5 %copy.24 = bf16[128,2,64,64]{3,2,0,1:T(8,128)(2,1)} copy(bf16[128,2,64,64]{0,3,2,1:T(8,128)(2,1)S(1)} %bitcast.32) | data formatting | bytes 4194304 | tf_op jit(solution)/shard_map/while | solution.py:28
  78.6 36.8 %while.10 = (s32[]{:T(128)}, f32[8,128,128]{2,1,0:T(8,128)S(1)}, bf16[8,128,2,128]{3,2,1,0:T(2,128)(2,1)}, bf16[128,2,64,64]{3,2,0,1:T(8,128)(2,1)}, s32[]{:T(128)}) while((s32[]{:T(128)}, f32[8,128,128]{2,1,0:T(8,128)S(1)}, bf16[8,128,2,128]{3,2,1,0:T(2,128)(2,1)}, bf16[128,2,64,64]{3,2,0,1:T(8,128)(2,1)}, s32[]{:T(128)}) %tuple.31), condition=%wide.region_3.0_spmd, body=%wide.region_2.0_spmd.sunk | while | flops 276824064 | bytes 2883653 | solution.py:28
  78.6 0.9 constant_dynamic-slice_fusion.2
  79.5 0.1 copy.44
  79.7 3.4 %multiply_reduce_fusion.6 = f32[128,128]{0,1:T(8,128)S(1)} fusion(f32[128,64,2]{0,1,2:T(8,128)S(1)} %fusion.5, bf16[128,2,64,64]{3,2,0,1:T(8,128)(2,1)} %get-tuple-element.98, bf16[128,2,128]{0,2,1:T(8,128)(2,1)S(1)} %bitcast.34), kind=kOutput, calls=%fused_computation.clone.1 | convolution fusion | flops 276807680 | bytes 2260992 | tf_op jit(solution)/shard_map/while/body/eval_jaxpr/tmj,qmij->tmqi/dot_general | solution.py:22
  83.1 0.1 copy.45
  83.2 0.9 constant_dynamic-slice_fusion.2
  84.1 0.1 copy.44
  84.3 3.4 %multiply_reduce_fusion.6 = f32[128,128]{0,1:T(8,128)S(1)} fusion(f32[128,64,2]{0,1,2:T(8,128)S(1)} %fusion.5, bf16[128,2,64,64]{3,2,0,1:T(8,128)(2,1)} %get-tuple-element.98, bf16[128,2,128]{0,2,1:T(8,128)(2,1)S(1)} %bitcast.34), kind=kOutput, calls=%fused_computation.clone.1 | convolution fusion | flops 276807680 | bytes 2260992 | tf_op jit(solution)/shard_map/while/body/eval_jaxpr/tmj,qmij->tmqi/dot_general | solution.py:22
  87.7 0.1 copy.45
  87.9 0.9 constant_dynamic-slice_fusion.2
  88.7 0.1 copy.44
  88.9 3.4 %multiply_reduce_fusion.6 = f32[128,128]{0,1:T(8,128)S(1)} fusion(f32[128,64,2]{0,1,2:T(8,128)S(1)} %fusion.5, bf16[128,2,64,64]{3,2,0,1:T(8,128)(2,1)} %get-tuple-element.98, bf16[128,2,128]{0,2,1:T(8,128)(2,1)S(1)} %bitcast.34), kind=kOutput, calls=%fused_computation.clone.1 | convolution fusion | flops 276807680 | bytes 2260992 | tf_op jit(solution)/shard_map/while/body/eval_jaxpr/tmj,qmij->tmqi/dot_general | solution.py:22
  92.3 0.1 copy.45
  92.5 0.9 constant_dynamic-slice_fusion.2
  93.4 0.1 copy.44
  93.5 3.4 %multiply_reduce_fusion.6 = f32[128,128]{0,1:T(8,128)S(1)} fusion(f32[128,64,2]{0,1,2:T(8,128)S(1)} %fusion.5, bf16[128,2,64,64]{3,2,0,1:T(8,128)(2,1)} %get-tuple-element.98, bf16[128,2,128]{0,2,1:T(8,128)(2,1)S(1)} %bitcast.34), kind=kOutput, calls=%fused_computation.clone.1 | convolution fusion | flops 276807680 | bytes 2260992 | tf_op jit(solution)/shard_map/while/body/eval_jaxpr/tmj,qmij->tmqi/dot_general | solution.py:22
  96.9 0.1 copy.45
  97.1 0.9 constant_dynamic-slice_fusion.2
  98.0 0.1 copy.44
  98.1 3.4 %multiply_reduce_fusion.6 = f32[128,128]{0,1:T(8,128)S(1)} fusion(f32[128,64,2]{0,1,2:T(8,128)S(1)} %fusion.5, bf16[128,2,64,64]{3,2,0,1:T(8,128)(2,1)} %get-tuple-element.98, bf16[128,2,128]{0,2,1:T(8,128)(2,1)S(1)} %bitcast.34), kind=kOutput, calls=%fused_computation.clone.1 | convolution fusion | flops 276807680 | bytes 2260992 | tf_op jit(solution)/shard_map/while/body/eval_jaxpr/tmj,qmij->tmqi/dot_general | solution.py:22
  101.5 0.1 copy.45
  101.7 0.9 constant_dynamic-slice_fusion.2
  102.6 0.1 copy.44
  102.7 3.4 %multiply_reduce_fusion.6 = f32[128,128]{0,1:T(8,128)S(1)} fusion(f32[128,64,2]{0,1,2:T(8,128)S(1)} %fusion.5, bf16[128,2,64,64]{3,2,0,1:T(8,128)(2,1)} %get-tuple-element.98, bf16[128,2,128]{0,2,1:T(8,128)(2,1)S(1)} %bitcast.34), kind=kOutput, calls=%fused_computation.clone.1 | convolution fusion | flops 276807680 | bytes 2260992 | tf_op jit(solution)/shard_map/while/body/eval_jaxpr/tmj,qmij->tmqi/dot_general | solution.py:22
  106.1 0.1 copy.45
  106.3 0.9 constant_dynamic-slice_fusion.2
  107.2 0.1 copy.44
  107.3 3.4 %multiply_reduce_fusion.6 = f32[128,128]{0,1:T(8,128)S(1)} fusion(f32[128,64,2]{0,1,2:T(8,128)S(1)} %fusion.5, bf16[128,2,64,64]{3,2,0,1:T(8,128)(2,1)} %get-tuple-element.98, bf16[128,2,128]{0,2,1:T(8,128)(2,1)S(1)} %bitcast.34), kind=kOutput, calls=%fused_computation.clone.1 | convolution fusion | flops 276807680 | bytes 2260992 | tf_op jit(solution)/shard_map/while/body/eval_jaxpr/tmj,qmij->tmqi/dot_general | solution.py:22
  110.8 0.1 copy.45
  110.9 0.9 constant_dynamic-slice_fusion.2
  111.8 0.1 copy.44
  111.9 3.4 %multiply_reduce_fusion.6 = f32[128,128]{0,1:T(8,128)S(1)} fusion(f32[128,64,2]{0,1,2:T(8,128)S(1)} %fusion.5, bf16[128,2,64,64]{3,2,0,1:T(8,128)(2,1)} %get-tuple-element.98, bf16[128,2,128]{0,2,1:T(8,128)(2,1)S(1)} %bitcast.34), kind=kOutput, calls=%fused_computation.clone.1 | convolution fusion | flops 276807680 | bytes 2260992 | tf_op jit(solution)/shard_map/while/body/eval_jaxpr/tmj,qmij->tmqi/dot_general | solution.py:22
  115.4 0.1 copy.45
  115.5 1.0 copy.37
  116.5 0.0 reduce-scatter.2.cloned.1.call-update
  116.5 8.0 %reduce-scatter.2.cloned.1.call-done = f32[1024,64]{0,1:T(8,128)} async-done(((f32[1024,128]{0,1:T(8,128)}), f32[1024,64]{0,1:T(8,128)}) %reduce-scatter.2.cloned.1.call-update) | async-done | bytes 262160 | tf_op jit(solution)/shard_map/reduce_scatter | solution.py:47
  124.6 1.7 %broadcast_multiply_fusion = f32[1024,64]{0,1:T(8,128)} fusion(f32[1024,64]{0,1:T(8,128)} %reduce-scatter.2.cloned.1.call-done, f32[1024]{0:T(1024)S(1)} %rsqrt_multiply_fusion), kind=kLoop, calls=%fused_computation.11 | loop fusion | flops 65536 | bytes 528384 | tf_op jit(solution)/shard_map/mul | solution.py:49
  (19 shorter events, 0.2 us)
Async XLA Ops:
  6.5 60.7 %all-gather.2.cloned.1.call-start = ((), (), s32[]{:S(2)}) async-start(), calls=%async_computation.1 | async-start | bytes 2359296 | tf_op jit(solution)/shard_map/all_gather | solution.py:45
  16.9 107.7 %reduce-scatter.2.cloned.1.call-start = ((), (), s32[]{:S(2)}) async-start(), calls=%async_computation.2 | async-start | bytes 786432 | tf_op jit(solution)/shard_map/reduce_scatter | solution.py:47
Sparse Core Ops, SparseCore 0:
  17.0 50.2 all-gather.1
  116.6 7.8 reduce-scatter.1
where the time goes:
time: 134 us; the launch traced here: 133 us
  waiting for transfers between devices  58.4 us (44%)
  matrix products  27.5 us (21%)
  local copies, waits for them, and re-layouts  21.2 us (16%)
  between operations  13.4 us (10%)
  other arithmetic  9.53 us (7%)
  blocking collectives  2.51 us (2%)
    all_gather x1, waiting for transfers between devices, local(): lax.all_gather(query_unit, 'ex', axis=0, tiled=True)  50.3 us
    dot_general x8, matrix products, one_block(): jnp.einsum('tmj,qmij->tmqi', grad_rows, query_mats, preferred_element_typ...  27.5 us
    dynamic_slice x16, local copies, waits for them, and re-layouts, contract_tokens(): return lax.map(one_block, blocks).reshape(token_count, query_count)  8.08 us
    reduce_scatter x1, waiting for transfers between devices, local(): lax.psum_scatter(block_scores, 'proj', scatter_dimension=1, tiled=True)  8.04 us
    while x1, local copies, waits for them, and re-layouts, contract_tokens(): return lax.map(one_block, blocks).reshape(token_count, query_count)  6.47 us
    all_gather x1, local copies, waits for them, and re-layouts, local(): lax.all_gather(query_unit, 'ex', axis=0, tiled=True)  4.88 us
    reduce_sum x1, other arithmetic, local(): jnp.sum(grad_all * grad_all, axis=2)  4.18 us
  transfers between devices with their start and end apart: 2, of which 2 were waited for; matrix products, arithmetic and copies ran while one was open for 0% of the time, Pallas kernels for 0%

commit v1 on v0

v1 whole, which is shorter than its diff:
```python
import functools

import jax
import jax.numpy as jnp
from jax import lax
from jax.experimental import pallas as pl
from jax.experimental.pallas import tpu as pltpu
from jax.sharding import PartitionSpec as P

epsilon = 1e-06
LANES = 128
GROUP = 16
VMEM = pl.BlockSpec(memory_space=pltpu.VMEM)
PARAMS = pltpu.CompilerParams(vmem_limit_bytes=32 * 1024 * 1024)


def query_kernel(modules, pairs, x_ref, o_ref):
    queries = o_ref.shape[1]
    for m in range(modules):
        for i in range(pairs):
            rows = x_ref[pl.ds(i * modules + m, queries, stride=pairs * modules), :]
            o_ref[m * pairs + i] = rows.astype(jnp.bfloat16)


def token_kernel(modules, rank, x_ref, w_ref, a_ref, n_ref, wide):
    tokens = x_ref.shape[0] // modules
    wide[...] = x_ref[...].astype(jnp.float32)
    norm = jnp.zeros((1, tokens), jnp.float32)
    for m in range(modules):
        turned = wide[pl.ds(m, tokens, stride=modules), :].T
        act, grad = turned[:rank], turned[rank:]
        norm += jnp.sum(act * act, axis=0, keepdims=True) * jnp.sum(
            grad * grad, axis=0, keepdims=True
        )
        grad = grad.astype(jnp.bfloat16)
        w_ref[m, :rank] = grad
        w_ref[m, rank : 2 * rank] = jnp.zeros_like(grad)
        w_ref[m, 2 * rank :] = grad
        a_ref[m] = act
    n_ref[...] = jnp.broadcast_to(norm, n_ref.shape)


def score_kernel(count, modules, rank, *refs):
    blocks, w_ref, a_ref, o_ref = refs[:count], refs[count], refs[count + 1], refs[count + 2]
    tokens = w_ref.shape[2]
    pairs = rank // 2
    tile = 256 if tokens % 256 == 0 else tokens
    step = 8
    for b in range(count):
        total = jnp.zeros((GROUP, LANES), jnp.float32)
        for k in range(modules * pairs):
            v = blocks[b][k].astype(jnp.float32)
            total += v * v
        o_ref[b * GROUP : (b + 1) * GROUP, tokens:] = total

    @pl.loop(0, tokens // tile)
    def _(t):
        lanes = pl.ds(pl.multiple_of(t * tile, tile), tile)
        acc = [jnp.zeros((GROUP, tile), jnp.float32) for _ in range(count)]
        for m in range(modules):
            for odd in range(2):
                w = w_ref[m, odd * rank : (odd + 2) * rank, lanes]
                for b in range(count):
                    for i in range(0, pairs, step):
                        k = m * pairs + i
                        left = blocks[b][k : k + step].reshape(step * GROUP, LANES)
                        inner = jnp.dot(left, w, preferred_element_type=jnp.float32)
                        for s in range(step):
                            act = a_ref[m, pl.ds(2 * (i + s) + odd, 1), lanes]
                            acc[b] += inner[s * GROUP : (s + 1) * GROUP] * act
        for b in range(count):
            o_ref[b * GROUP : (b + 1) * GROUP, lanes] = acc[b]


def finish_kernel(count, width, slot_ref, *refs):
    own, far = refs[:count], refs[count : 2 * count]
    norm_ref, far_norm_ref, o_ref, both = refs[2 * count :]
    tokens = o_ref.shape[1]
    at = 0
    for mine, other in zip(own, far):
        rows = mine.shape[0]
        both[at : at + rows] = mine[...] + other[...]
        at += rows
    norm = norm_ref[:1] + far_norm_ref[:1]
    token_scale = lax.rsqrt(norm / width + epsilon) / jnp.sqrt(jnp.float32(width))
    for j in range(o_ref.shape[0] // GROUP):
        got = both[pl.ds(pl.multiple_of(slot_ref[j] * GROUP, GROUP), GROUP), :]
        square = jnp.sum(got[:, tokens:], axis=1, keepdims=True)
        query_scale = lax.rsqrt(square / width + epsilon)
        o_ref[j * GROUP : (j + 1) * GROUP] = got[:, :tokens] * query_scale * token_scale


def local(train_factors, query_grads):
    tokens, modules, doubled = train_factors.shape
    rank = doubled // 2
    pairs = rank // 2
    ex, proj = lax.axis_size("ex"), lax.axis_size("proj")
    here, core = lax.axis_index("ex"), lax.axis_index("proj")
    queries = query_grads.shape[0]
    width = modules * proj * rank * rank
    swap = [(i, (i + 1) % proj) for i in range(proj)]

    token_rows = train_factors.reshape(tokens * modules, doubled)
    weights, acts, norm = pl.pallas_call(
        functools.partial(token_kernel, modules, rank),
        out_shape=(
            jax.ShapeDtypeStruct((modules, 3 * rank, tokens), jnp.bfloat16),
            jax.ShapeDtypeStruct((modules, rank, tokens), jnp.float32),
            jax.ShapeDtypeStruct((8, tokens), jnp.float32),
        ),
        in_specs=[VMEM],
        out_specs=(VMEM, VMEM, VMEM),
        scratch_shapes=[pltpu.VMEM((tokens * modules, doubled), jnp.float32)],
        compiler_params=PARAMS,
        name="tokens",
    )(token_rows)

    def score(*blocks):
        count = len(blocks)
        flops = 2 * count * GROUP * modules * rank * rank * tokens
        return pl.pallas_call(
            functools.partial(score_kernel, count, modules, rank),
            out_shape=jax.ShapeDtypeStruct((count * GROUP, tokens + LANES), jnp.float32),
            in_specs=[VMEM] * (count + 2),
            out_specs=VMEM,
            compiler_params=PARAMS,
            cost_estimate=pl.CostEstimate(
                flops=4 * flops, bytes_accessed=2 * 1024 * 1024, transcendentals=0
            ),
            name="scores",
        )(*blocks, weights, acts)

    def swapped(x):
        return lax.ppermute(x, "proj", swap)

    if queries % GROUP == 0 and ex % 2 == 0 and ex <= 16 and queries == GROUP:
        order = list(range(0, ex, 2)) + list(range(ex - 1, 0, -2))
        up = [(order[i], order[(i + 1) % ex]) for i in range(ex)]
        down = [(b, a) for a, b in up]
        rows = query_grads.reshape(queries, modules, pairs, LANES)
        rows = rows.transpose(0, 2, 1, 3).reshape(queries * pairs * modules, LANES)
        block = pl.pallas_call(
            functools.partial(query_kernel, modules, pairs),
            out_shape=jax.ShapeDtypeStruct((modules * pairs, queries, LANES), jnp.bfloat16),
            in_specs=[VMEM],
            out_specs=VMEM,
            compiler_params=PARAMS,
            name="queries",
        )(rows)
        half = modules * pairs // 2
        low = high = block
        own, far = [], []
        waiting = (block,)
        for step in range(1, ex // 2 + 1):
            if step < ex // 2:
                low = lax.ppermute(low, "ex", up)
                high = lax.ppermute(high, "ex", down)
                arrived = (low, high)
            else:
                first = lax.ppermute(low[:half], "ex", up)
                second = lax.ppermute(high[half:], "ex", down)
                arrived = (jnp.concatenate([first, second], axis=0),)
            own.append(score(*waiting))
            far.append(swapped(own[-1]))
            waiting = arrived
        own.append(score(*waiting))
        far.append(swapped(own[-1]))
        place = jnp.array([order.index(i) for i in range(ex)], jnp.int32)
        wanted = core * (ex // proj) + jnp.arange(ex // proj, dtype=jnp.int32)
        ahead = jnp.mod(place[wanted] - place[here], ex)
        slots = jnp.where(
            ahead == 0,
            0,
            jnp.where(
                ahead < ex // 2,
                2 * ahead,
                jnp.where(ahead > ex // 2, 2 * (ex - ahead) - 1, ex - 1),
            ),
        )
    else:
        gathered = lax.all_gather(query_grads.astype(jnp.bfloat16), "ex", axis=0, tiled=True)
        count = queries * ex // GROUP
        gathered = gathered.reshape(count, GROUP, modules * pairs, LANES).transpose(0, 2, 1, 3)
        own = [score(gathered[i]) for i in range(count)]
        far = [swapped(x) for x in own]
        slots = core * (count // proj) + jnp.arange(count // proj, dtype=jnp.int32)

    count = len(own)
    total_rows = sum(x.shape[0] for x in own)
    scores = pl.pallas_call(
        functools.partial(finish_kernel, count, width),
        out_shape=jax.ShapeDtypeStruct((total_rows // proj, tokens), jnp.float32),
        in_specs=[pl.BlockSpec(memory_space=pltpu.SMEM)] + [VMEM] * (2 * count + 2),
        out_specs=VMEM,
        scratch_shapes=[pltpu.VMEM((total_rows, tokens + LANES), jnp.float32)],
        compiler_params=PARAMS,
        name="finish",
    )(slots.astype(jnp.int32), *own, *far, norm, swapped(norm))
    return scores.T


def solution(mesh):
    return jax.shard_map(
        local,
        mesh=mesh,
        in_specs=(P(("groups", "ex"), "proj", None), P(("groups", "ex"), "proj", None)),
        out_specs=P(("groups", "ex"), "proj"),
        check_vma=False,
    )
```

time: 134 us -> 38.2 us (0.29)
  waiting for transfers between devices: 58.4 us -> 7.1 us
  matrix products: 27.5 us -> 0 us
  local copies, waits for them, and re-layouts: 21.2 us -> 2.29 us
  Pallas kernels: 0 us -> 14.3 us
  starting transfers between devices: 0.04 us -> 13.4 us
  between operations: 13.4 us -> 0.15 us
  other arithmetic: 9.53 us -> 0.7 us
  blocking collectives: 2.51 us -> 0 us
    all_gather x1 -> x0, waiting for transfers between devices: 50.3 us -> none  [local(): lax.all_gather(query_unit, 'ex', axis=0, tiled=True)]
    dot_general x8 -> x0, matrix products: 27.5 us -> none  [one_block(): jnp.einsum('tmj,qmij->tmqi', grad_rows, query_mats, preferred_element_typ...]
    pallas_call x0 -> x8, Pallas kernels: none -> 14.3 us  [the longest x5 12.3 us: score(): pl.pallas_call(functools.partial(score_kernel, count, modules, rank), out...]
    ppermute x0 -> x14, starting transfers between devices: none -> 13.4 us  [the longest x6 6.72 us: swapped(): return lax.ppermute(x, 'proj', swap)]
    reduce_scatter x1 -> x0, waiting for transfers between devices: 8.04 us -> none  [local(): lax.psum_scatter(block_scores, 'proj', scatter_dimension=1, tiled=True)]
    dynamic_slice x16 -> x1, local copies, waits for them, and re-layouts: 8.08 us -> 0.58 us  [local(): ahead = jnp.mod(place[wanted] - place[here], ex)]
    ppermute x0 -> x14, waiting for transfers between devices: none -> 7.1 us  [the longest x3 5.78 us: local(): low = lax.ppermute(low, 'ex', up)]
    while x1 -> x0, local copies, waits for them, and re-layouts: 6.47 us -> none  [contract_tokens(): return lax.map(one_block, blocks).reshape(token_count, query_count)]
  transfers between devices with their start and end apart: 2 -> 14, of which waited for: 2 -> 5; matrix products, arithmetic and copies ran while one was open for 0% -> 5% of each run, Pallas kernels for 0% -> 33%
where the time goes in v1:
time: 38.2 us; the launch traced here: 38 us
  Pallas kernels  14.3 us (37%)
  starting transfers between devices  13.4 us (35%)
  waiting for transfers between devices  7.1 us (19%)
  local copies, waits for them, and re-layouts  2.29 us (6%)
  other arithmetic  0.7 us (2%)
    pallas_call x5, Pallas kernels, score(): pl.pallas_call(functools.partial(score_kernel, count, modules, rank), out...  12.3 us
    ppermute x6, starting transfers between devices, swapped(): return lax.ppermute(x, 'proj', swap)  6.72 us
    ppermute x3, waiting for transfers between devices, local(): low = lax.ppermute(low, 'ex', up)  5.78 us
    ppermute x3, starting transfers between devices, local(): low = lax.ppermute(low, 'ex', up)  4.84 us
    pallas_call x1, Pallas kernels, local(): pl.pallas_call(functools.partial(finish_kernel, count, width), out_shape=...  1.42 us
    ppermute x1, starting transfers between devices, local(): second = lax.ppermute(high[half:], 'ex', down)  1.19 us
    unnamed x6, local copies, waits for them, and re-layouts  1.05 us
  transfers between devices with their start and end apart: 14, of which 5 were waited for; matrix products, arithmetic and copies ran while one was open for 5% of the time, Pallas kernels for 33%

profile of v1, /device:TPU:1, one launch (start us, length us, event | category | flops | bytes accessed | tf_op | source)
XLA Modules:
  0.0 38.0 jit_solution(2289965222496651179)
XLA Ops:
  0.0 0.0 copy-start
  0.0 1.0 %copy-done = f32[16,2,4096]{2,1,0:T(2,128)S(1)} copy-done((f32[16,2,4096]{2,1,0:T(2,128)S(1)}, f32[16,2,4096]{2,1,0:T(2,128)}, u32[]{:S(2)}) %copy-start) | copy-done | bytes 524312
  1.0 0.0 copy-start.1
  1.0 0.3 queries.1.refs_0_
  1.3 2.2 %collective-permute-start = (bf16[64,16,128]{2,1,0:T(8,128)(2,1)S(1)}, bf16[64,16,128]{2,1,0:T(8,128)(2,1)S(1)}, u32[]{:S(2)}, u32[]{:S(2)}) collective-permute-start(bf16[64,16,128]{2,1,0:T(8,128)(2,1)S(1)} %queries.1.refs_0_), channel_id=1, source_target_pairs={{0,4},{4,8},{8,12},{12,14},{14,10},{10,6},{6,2},{2,0},{1,5},{5,9},... | collective-permute-start | bytes 786440 | tf_op jit(solution)/shard_map/ppermute | solution.py:156
  3.5 0.0 collective-permute-start.1
  3.5 0.0 copy-done.1
  3.5 0.3 tokens.1
  3.8 5.7 %collective-permute-done.refs_0_ = bf16[64,16,128]{2,1,0:T(8,128)(2,1)S(1)} collective-permute-done((bf16[64,16,128]{2,1,0:T(8,128)(2,1)S(1)}, bf16[64,16,128]{2,1,0:T(8,128)(2,1)S(1)}, u32[]{:S(2)}, u32[]{:S(2)}) %collective-permute-start) | collective-permute-done | bytes 262176 | tf_op jit(solution)/shard_map/ppermute | solution.py:156
  9.5 1.2 %collective-permute-start.2 = (bf16[64,16,128]{2,1,0:T(8,128)(2,1)S(1)}, bf16[64,16,128]{2,1,0:T(8,128)(2,1)S(1)}, u32[]{:S(2)}, u32[]{:S(2)}) collective-permute-start(bf16[64,16,128]{2,1,0:T(8,128)(2,1)S(1)} %collective-permute-done.refs_0_), channel_id=1, source_target_pairs={{0,4},{4,8},{8,12},{12,14},{14,10},{10,6},{6,2},{2,0},{1,5},{5,9},... | collective-permute-start | bytes 786440 | tf_op jit(solution)/shard_map/ppermute | solution.py:156
  10.7 0.0 collective-permute-done.1.refs_1_
  10.7 0.2 collective-permute-start.3
  10.9 0.0 copy-start.2
  10.9 1.8 %scores.5.refs_0_ = f32[16,1152]{1,0:T(8,128)S(1)} custom-call(bf16[64,16,128]{2,1,0:T(8,128)(2,1)S(1)} %queries.1.refs_0_, bf16[2,192,1024]{2,1,0:T(8,128)(2,1)S(1)} %get-tuple-element.8.refs_1_.refs_2_, f32[2,64,1024]{2,1,0:T(8,128)S(1)} %get-tuple-element.9.refs_2_.refs_3_), custom_call_target="tpu_custom_call" | custom-call | flops 1073741824 | bytes 2097152 | tf_op jit(solution)/shard_map/scores/pallas_call | solution.py:121
  12.7 1.8 %collective-permute-start.8 = (f32[16,1152]{1,0:T(8,128)S(1)}, f32[16,1152]{1,0:T(8,128)S(1)}, u32[]{:S(2)}, u32[]{:S(2)}) collective-permute-start(f32[16,1152]{1,0:T(8,128)S(1)} %scores.5.refs_0_), channel_id=1, source_target_pairs={{0,1},{1,0},{2,3},{3,2},{4,5},{5,4},{6,7},{7,6},{8,9},{9,8},{10,11... | collective-permute-start | bytes 221192 | tf_op jit(solution)/shard_map/ppermute | solution.py:134
  14.6 0.1 collective-permute-start.13
  14.7 0.0 copy-done.2
  14.7 0.6 %gather_fusion = s32[4]{0:T(128)S(1)} fusion(s32[8]{0:T(128)S(1)} %copy-done.2, s32[1024]{0:T(1024)S(1)} %pad_clamp_fusion), kind=kCustom, calls=%fused_computation | custom fusion | bytes 48 | tf_op jit(solution)/shard_map/gather | solution.py:170
  15.3 0.6 %dynamic_slice.3 = s32[1]{0:T(128)} dynamic-slice(s32[8]{0:T(128)S(1)} %copy-done.2, s32[]{:T(128)S(6)} %select_n.33), dynamic_slice_sizes={1} | dynamic-slice | bytes 12 | tf_op jit(solution)/shard_map/dynamic_slice | solution.py:170
  15.9 0.1 collective-permute-done.2.refs_0_
  16.0 1.4 %collective-permute-start.4 = (bf16[64,16,128]{2,1,0:T(8,128)(2,1)S(1)}, bf16[64,16,128]{2,1,0:T(8,128)(2,1)S(1)}, u32[]{:S(2)}, u32[]{:S(2)}) collective-permute-start(bf16[64,16,128]{2,1,0:T(8,128)(2,1)S(1)} %collective-permute-done.2.refs_0_), channel_id=1, source_target_pairs={{0,4},{4,8},{8,12},{12,14},{14,10},{10,6},{6,2},{2,0},{1,5},{5,9},... | collective-permute-start | bytes 786440 | tf_op jit(solution)/shard_map/ppermute | solution.py:156
  17.5 0.0 collective-permute-done.3.refs_1_
  17.5 0.0 collective-permute-start.5
  17.5 2.9 %scores.6.refs_1_ = f32[32,1152]{1,0:T(8,128)S(1)} custom-call(bf16[64,16,128]{2,1,0:T(8,128)(2,1)S(1)} %collective-permute-done.refs_0_, bf16[64,16,128]{2,1,0:T(8,128)(2,1)S(1)} %collective-permute-done.1.refs_1_, bf16[2,192,1024]{2,1,0:T(8,128)(2,1)S(1)} %get-tuple-element.8.refs_1_.refs_2_, f32[2,64,1024]{2,1,0:T(8,128)S(1)} %get-tuple-element.9.refs_2_.refs_3_), custom_call_target="tpu_custom_call" | custom-call | flops 2147483648 | bytes 2097152 | tf_op jit(solution)/shard_map/scores/pallas_call | solution.py:121
  20.4 2.8 %collective-permute-start.9 = (f32[32,1152]{1,0:T(8,128)S(1)}, f32[32,1152]{1,0:T(8,128)S(1)}, u32[]{:S(2)}, u32[]{:S(2)}) collective-permute-start(f32[32,1152]{1,0:T(8,128)S(1)} %scores.6.refs_1_), channel_id=1, source_target_pairs={{0,1},{1,0},{2,3},{3,2},{4,5},{5,4},{6,7},{7,6},{8,9},{9,8},{10,11... | collective-permute-start | bytes 442376 | tf_op jit(solution)/shard_map/ppermute | solution.py:134
  23.2 2.9 %scores.7.refs_2_ = f32[32,1152]{1,0:T(8,128)S(1)} custom-call(bf16[64,16,128]{2,1,0:T(8,128)(2,1)S(1)} %collective-permute-done.2.refs_0_, bf16[64,16,128]{2,1,0:T(8,128)(2,1)S(1)} %collective-permute-done.3.refs_1_, bf16[2,192,1024]{2,1,0:T(8,128)(2,1)S(1)} %get-tuple-element.8.refs_1_.refs_2_, f32[2,64,1024]{2,1,0:T(8,128)S(1)} %get-tuple-element.9.refs_2_.refs_3_), custom_call_target="tpu_custom_call" | custom-call | flops 2147483648 | bytes 2097152 | tf_op jit(solution)/shard_map/scores/pallas_call | solution.py:121
  26.1 0.0 collective-permute-done.5.refs_1_
  26.2 1.2 %collective-permute-start.7 = (bf16[32,16,128]{2,1,0:T(8,128)(2,1)S(1)}, bf16[32,16,128]{2,1,0:T(8,128)(2,1)S(1)}, u32[]{:S(2)}, u32[]{:S(2)}) collective-permute-start(bf16[32,16,128]{2,1,0:T(8,128)(2,1)S(1)} %slice.11), channel_id=1, source_target_pairs={{4,0},{8,4},{12,8},{14,12},{10,14},{6,10},{2,6},{0,2},{5,1},{9,5},... | collective-permute-start | bytes 393224 | tf_op jit(solution)/shard_map/ppermute | solution.py:161
  27.4 0.0 collective-permute-done.4.refs_0_
  27.4 0.4 collective-permute-start.6
  27.8 2.9 %scores.8.refs_3_ = f32[32,1152]{1,0:T(8,128)S(1)} custom-call(bf16[64,16,128]{2,1,0:T(8,128)(2,1)S(1)} %collective-permute-done.4.refs_0_, bf16[64,16,128]{2,1,0:T(8,128)(2,1)S(1)} %collective-permute-done.5.refs_1_, bf16[2,192,1024]{2,1,0:T(8,128)(2,1)S(1)} %get-tuple-element.8.refs_1_.refs_2_, f32[2,64,1024]{2,1,0:T(8,128)S(1)} %get-tuple-element.9.refs_2_.refs_3_), custom_call_target="tpu_custom_call" | custom-call | flops 2147483648 | bytes 2097152 | tf_op jit(solution)/shard_map/scores/pallas_call | solution.py:121
  30.7 0.6 %collective-permute-done.7 = bf16[32,16,128]{2,1,0:T(8,128)(2,1)S(1)} collective-permute-done((bf16[32,16,128]{2,1,0:T(8,128)(2,1)S(1)}, bf16[32,16,128]{2,1,0:T(8,128)(2,1)S(1)}, u32[]{:S(2)}, u32[]{:S(2)}) %collective-permute-start.7) | collective-permute-done | bytes 131104 | tf_op jit(solution)/shard_map/ppermute | solution.py:161
  31.3 0.8 %collective-permute-start.10 = (f32[32,1152]{1,0:T(8,128)S(1)}, f32[32,1152]{1,0:T(8,128)S(1)}, u32[]{:S(2)}, u32[]{:S(2)}) collective-permute-start(f32[32,1152]{1,0:T(8,128)S(1)} %scores.7.refs_2_), channel_id=1, source_target_pairs={{0,1},{1,0},{2,3},{3,2},{4,5},{5,4},{6,7},{7,6},{8,9},{9,8},{10,11... | collective-permute-start | bytes 442376 | tf_op jit(solution)/shard_map/ppermute | solution.py:134
  32.1 0.1 collective-permute-done.6
  32.2 1.1 %collective-permute-start.11 = (f32[32,1152]{1,0:T(8,128)S(1)}, f32[32,1152]{1,0:T(8,128)S(1)}, u32[]{:S(2)}, u32[]{:S(2)}) collective-permute-start(f32[32,1152]{1,0:T(8,128)S(1)} %scores.8.refs_3_), channel_id=1, source_target_pairs={{0,1},{1,0},{2,3},{3,2},{4,5},{5,4},{6,7},{7,6},{8,9},{9,8},{10,11... | collective-permute-start | bytes 442376 | tf_op jit(solution)/shard_map/ppermute | solution.py:134
  33.4 1.8 %scores.9.refs_4_ = f32[16,1152]{1,0:T(8,128)S(1)} custom-call(bf16[64,16,128]{2,1,0:T(8,128)(2,1)S(1)} %pad_maximum_fusion.refs_0_, bf16[2,192,1024]{2,1,0:T(8,128)(2,1)S(1)} %get-tuple-element.8.refs_1_.refs_2_, f32[2,64,1024]{2,1,0:T(8,128)S(1)} %get-tuple-element.9.refs_2_.refs_3_), custom_call_target="tpu_custom_call" | custom-call | flops 1073741824 | bytes 2097152 | tf_op jit(solution)/shard_map/scores/pallas_call | solution.py:121
  35.2 0.0 collective-permute-done.13.refs_11_
  35.2 0.1 collective-permute-start.12
  35.3 0.7 %compare_select_fusion.5.slot_ref = s32[4]{0:T(128)S(1)} fusion(s32[4]{0:T(128)S(1)} %gather_fusion, s32[]{:T(128)} %bitcast.1), kind=kLoop, calls=%fused_computation.8 | loop fusion | flops 88 | bytes 36 | tf_op jit(solution)/shard_map/jit(_where)/select_n | solution.py:171
  35.9 0.0 collective-permute-done.8.refs_5_
  36.0 0.0 collective-permute-done.9.refs_6_
  36.0 0.0 collective-permute-done.10.refs_7_
  36.0 0.0 collective-permute-done.11.refs_8_
  36.0 0.5 %collective-permute-done.12.refs_9_ = f32[16,1152]{1,0:T(8,128)S(1)} collective-permute-done((f32[16,1152]{1,0:T(8,128)S(1)}, f32[16,1152]{1,0:T(8,128)S(1)}, u32[]{:S(2)}, u32[]{:S(2)}) %collective-permute-start.12) | collective-permute-done | bytes 73760 | tf_op jit(solution)/shard_map/ppermute | solution.py:134
  36.5 1.4 %finish.1 = f32[64,1024]{1,0:T(8,128)} custom-call(s32[4]{0:T(128)S(1)} %compare_select_fusion.5.slot_ref, f32[16,1152]{1,0:T(8,128)S(1)} %scores.5.refs_0_, f32[32,1152]{1,0:T(8,128)S(1)} %scores.6.refs_1_, f32[32,1152]{1,0:T(8,128)S(1)} %scores.7.refs_2_, f32[32,1152]{1,0:T(8,128)S(1)} %scores.8.refs_3_, f32[16,1152]{1,0:T(8,128)S(1)} %scores.9.refs_4_, ...), custom_call_target="tpu_custom_call" | custom-call | tf_op jit(solution)/shard_map/finish/pallas_call | solution.py:190
  (5 shorter events, 0.1 us)
Async XLA Ops:
  0.0 1.0 %copy-start = (f32[16,2,4096]{2,1,0:T(2,128)S(1)}, f32[16,2,4096]{2,1,0:T(2,128)}, u32[]{:S(2)}) copy-start(f32[16,2,4096]{2,1,0:T(2,128)} %param.4) | copy-start | bytes 1572868
  1.0 2.5 %copy-start.1 = (bf16[1024,2,128]{2,1,0:T(2,128)(2,1)S(1)}, bf16[1024,2,128]{2,1,0:T(2,128)(2,1)}, u32[]{:S(2)}) copy-start(bf16[1024,2,128]{2,1,0:T(2,128)(2,1)} %param.3) | copy-start | bytes 1572868
  1.3 8.1 %collective-permute-start = (bf16[64,16,128]{2,1,0:T(8,128)(2,1)S(1)}, bf16[64,16,128]{2,1,0:T(8,128)(2,1)S(1)}, u32[]{:S(2)}, u32[]{:S(2)}) collective-permute-start(bf16[64,16,128]{2,1,0:T(8,128)(2,1)S(1)} %queries.1.refs_0_), channel_id=1, source_target_pairs={{0,4},{4,8},{8,12},{12,14},{14,10},{10,6},{6,2},{2,0},{1,5},{5,9},... | collective-permute-start | bytes 786440 | tf_op jit(solution)/shard_map/ppermute | solution.py:156
  3.5 7.2 %collective-permute-start.1 = (bf16[64,16,128]{2,1,0:T(8,128)(2,1)S(1)}, bf16[64,16,128]{2,1,0:T(8,128)(2,1)S(1)}, u32[]{:S(2)}, u32[]{:S(2)}) collective-permute-start(bf16[64,16,128]{2,1,0:T(8,128)(2,1)S(1)} %queries.1.refs_0_), channel_id=1, source_target_pairs={{4,0},{8,4},{12,8},{14,12},{10,14},{6,10},{2,6},{0,2},{5,1},{9,5},... | collective-permute-start | bytes 786440 | tf_op jit(solution)/shard_map/ppermute | solution.py:157
  9.5 6.6 %collective-permute-start.2 = (bf16[64,16,128]{2,1,0:T(8,128)(2,1)S(1)}, bf16[64,16,128]{2,1,0:T(8,128)(2,1)S(1)}, u32[]{:S(2)}, u32[]{:S(2)}) collective-permute-start(bf16[64,16,128]{2,1,0:T(8,128)(2,1)S(1)} %collective-permute-done.refs_0_), channel_id=1, source_target_pairs={{0,4},{4,8},{8,12},{12,14},{14,10},{10,6},{6,2},{2,0},{1,5},{5,9},... | collective-permute-start | bytes 786440 | tf_op jit(solution)/shard_map/ppermute | solution.py:156
  10.7 6.8 %collective-permute-start.3 = (bf16[64,16,128]{2,1,0:T(8,128)(2,1)S(1)}, bf16[64,16,128]{2,1,0:T(8,128)(2,1)S(1)}, u32[]{:S(2)}, u32[]{:S(2)}) collective-permute-start(bf16[64,16,128]{2,1,0:T(8,128)(2,1)S(1)} %collective-permute-done.1.refs_1_), channel_id=1, source_target_pairs={{4,0},{8,4},{12,8},{14,12},{10,14},{6,10},{2,6},{0,2},{5,1},{9,5},... | collective-permute-start | bytes 786440 | tf_op jit(solution)/shard_map/ppermute | solution.py:157
  10.9 3.8 %copy-start.2 = (s32[8]{0:T(128)S(1)}, s32[8]{0:T(128)}, u32[]{:S(2)}) copy-start(s32[8]{0:T(128)} %constant.37.clone) | copy-start | bytes 100
  12.7 23.2 %collective-permute-start.8 = (f32[16,1152]{1,0:T(8,128)S(1)}, f32[16,1152]{1,0:T(8,128)S(1)}, u32[]{:S(2)}, u32[]{:S(2)}) collective-permute-start(f32[16,1152]{1,0:T(8,128)S(1)} %scores.5.refs_0_), channel_id=1, source_target_pairs={{0,1},{1,0},{2,3},{3,2},{4,5},{5,4},{6,7},{7,6},{8,9},{9,8},{10,11... | collective-permute-start | bytes 221192 | tf_op jit(solution)/shard_map/ppermute | solution.py:134
  14.6 20.6 %collective-permute-start.13 = (f32[8,1024]{1,0:T(8,128)S(1)}, f32[8,1024]{1,0:T(8,128)S(1)}, u32[]{:S(2)}, u32[]{:S(2)}) collective-permute-start(f32[8,1024]{1,0:T(8,128)S(1)} %get-tuple-element.10.refs_10_), channel_id=1, source_target_pairs={{0,1},{1,0},{2,3},{3,2},{4,5},{5,4},{6,7},{7,6},{8,9},{9,8},{10,11... | collective-permute-start | bytes 98312 | tf_op jit(solution)/shard_map/ppermute | solution.py:134
  16.0 11.3 %collective-permute-start.4 = (bf16[64,16,128]{2,1,0:T(8,128)(2,1)S(1)}, bf16[64,16,128]{2,1,0:T(8,128)(2,1)S(1)}, u32[]{:S(2)}, u32[]{:S(2)}) collective-permute-start(bf16[64,16,128]{2,1,0:T(8,128)(2,1)S(1)} %collective-permute-done.2.refs_0_), channel_id=1, source_target_pairs={{0,4},{4,8},{8,12},{12,14},{14,10},{10,6},{6,2},{2,0},{1,5},{5,9},... | collective-permute-start | bytes 786440 | tf_op jit(solution)/shard_map/ppermute | solution.py:156
  17.5 8.7 %collective-permute-start.5 = (bf16[64,16,128]{2,1,0:T(8,128)(2,1)S(1)}, bf16[64,16,128]{2,1,0:T(8,128)(2,1)S(1)}, u32[]{:S(2)}, u32[]{:S(2)}) collective-permute-start(bf16[64,16,128]{2,1,0:T(8,128)(2,1)S(1)} %collective-permute-done.3.refs_1_), channel_id=1, source_target_pairs={{4,0},{8,4},{12,8},{14,12},{10,14},{6,10},{2,6},{0,2},{5,1},{9,5},... | collective-permute-start | bytes 786440 | tf_op jit(solution)/shard_map/ppermute | solution.py:157
  20.4 15.5 %collective-permute-start.9 = (f32[32,1152]{1,0:T(8,128)S(1)}, f32[32,1152]{1,0:T(8,128)S(1)}, u32[]{:S(2)}, u32[]{:S(2)}) collective-permute-start(f32[32,1152]{1,0:T(8,128)S(1)} %scores.6.refs_1_), channel_id=1, source_target_pairs={{0,1},{1,0},{2,3},{3,2},{4,5},{5,4},{6,7},{7,6},{8,9},{9,8},{10,11... | collective-permute-start | bytes 442376 | tf_op jit(solution)/shard_map/ppermute | solution.py:134
  26.2 5.1 %collective-permute-start.7 = (bf16[32,16,128]{2,1,0:T(8,128)(2,1)S(1)}, bf16[32,16,128]{2,1,0:T(8,128)(2,1)S(1)}, u32[]{:S(2)}, u32[]{:S(2)}) collective-permute-start(bf16[32,16,128]{2,1,0:T(8,128)(2,1)S(1)} %slice.11), channel_id=1, source_target_pairs={{4,0},{8,4},{12,8},{14,12},{10,14},{6,10},{2,6},{0,2},{5,1},{9,5},... | collective-permute-start | bytes 393224 | tf_op jit(solution)/shard_map/ppermute | solution.py:161
  27.4 4.9 %collective-permute-start.6 = (bf16[32,16,128]{2,1,0:T(8,128)(2,1)S(1)}, bf16[32,16,128]{2,1,0:T(8,128)(2,1)S(1)}, u32[]{:S(2)}, u32[]{:S(2)}) collective-permute-start(bf16[32,16,128]{2,1,0:T(8,128)(2,1)S(1)} %slice.10), channel_id=1, source_target_pairs={{0,4},{4,8},{8,12},{12,14},{14,10},{10,6},{6,2},{2,0},{1,5},{5,9},... | collective-permute-start | bytes 393224 | tf_op jit(solution)/shard_map/ppermute | solution.py:160
  31.3 4.7 %collective-permute-start.10 = (f32[32,1152]{1,0:T(8,128)S(1)}, f32[32,1152]{1,0:T(8,128)S(1)}, u32[]{:S(2)}, u32[]{:S(2)}) collective-permute-start(f32[32,1152]{1,0:T(8,128)S(1)} %scores.7.refs_2_), channel_id=1, source_target_pairs={{0,1},{1,0},{2,3},{3,2},{4,5},{5,4},{6,7},{7,6},{8,9},{9,8},{10,11... | collective-permute-start | bytes 442376 | tf_op jit(solution)/shard_map/ppermute | solution.py:134
  32.2 3.7 %collective-permute-start.11 = (f32[32,1152]{1,0:T(8,128)S(1)}, f32[32,1152]{1,0:T(8,128)S(1)}, u32[]{:S(2)}, u32[]{:S(2)}) collective-permute-start(f32[32,1152]{1,0:T(8,128)S(1)} %scores.8.refs_3_), channel_id=1, source_target_pairs={{0,1},{1,0},{2,3},{3,2},{4,5},{5,4},{6,7},{7,6},{8,9},{9,8},{10,11... | collective-permute-start | bytes 442376 | tf_op jit(solution)/shard_map/ppermute | solution.py:134
  35.2 1.3 %collective-permute-start.12 = (f32[16,1152]{1,0:T(8,128)S(1)}, f32[16,1152]{1,0:T(8,128)S(1)}, u32[]{:S(2)}, u32[]{:S(2)}) collective-permute-start(f32[16,1152]{1,0:T(8,128)S(1)} %scores.9.refs_4_), channel_id=1, source_target_pairs={{0,1},{1,0},{2,3},{3,2},{4,5},{5,4},{6,7},{7,6},{8,9},{9,8},{10,11... | collective-permute-start | bytes 221192 | tf_op jit(solution)/shard_map/ppermute | solution.py:134

commit v2 on v0

v2 whole, which is shorter than its diff:
```python
import functools

import jax
import jax.numpy as jnp
from jax import lax
from jax.experimental import pallas as pl
from jax.experimental.pallas import tpu as pltpu
from jax.sharding import PartitionSpec as P

epsilon = 1e-06
LANES = 128
GROUP = 16
VMEM = pl.BlockSpec(memory_space=pltpu.VMEM)
ANY = pl.BlockSpec(memory_space=pl.ANY)
PARAMS = pltpu.CompilerParams(vmem_limit_bytes=16 * 1024 * 1024)


def place_of(index, count):
    return jnp.where(index % 2 == 0, index // 2, count - (index + 1) // 2)


def index_at(place, count):
    place = lax.rem(place + count, count)
    return jnp.where(place < count // 2, 2 * place, 2 * (count - place) - 1)


def query_kernel(modules, pairs, x_ref, *chunks):
    queries = chunks[0].shape[1]
    own = pairs // len(chunks)
    for c, o_ref in enumerate(chunks):
        for m in range(modules):
            for i in range(own):
                at = (c * own + i) * modules + m
                rows = x_ref[pl.ds(at, queries, stride=pairs * modules), :]
                o_ref[m * own + i] = rows.astype(jnp.bfloat16)


def token_kernel(modules, rank, x_ref, w_ref, a_ref, b_ref, n_ref, wide):
    tokens = x_ref.shape[0] // modules
    wide[...] = x_ref[...].astype(jnp.float32)
    norm = jnp.zeros((1, tokens), jnp.float32)
    for m in range(modules):
        turned = wide[pl.ds(m, tokens, stride=modules), :].T
        act, grad = turned[:rank], turned[rank:]
        norm += jnp.sum(act * act, axis=0, keepdims=True) * jnp.sum(
            grad * grad, axis=0, keepdims=True
        )
        grad = grad.astype(jnp.bfloat16)
        w_ref[m, :rank] = grad
        w_ref[m, rank : 2 * rank] = jnp.zeros_like(grad)
        w_ref[m, 2 * rank :] = grad
        a_ref[m] = act
        b_ref[m] = act.astype(jnp.bfloat16)
    n_ref[...] = jnp.broadcast_to(norm, n_ref.shape)


def lane_squares(chunks):
    total = jnp.zeros((GROUP, LANES), jnp.float32)
    for chunk in chunks:
        for k in range(chunk.shape[0]):
            v = chunk[k].astype(jnp.float32)
            total += v * v
    return total


def last_kernel(parts, modules, rank, *refs):
    chunks = refs[:parts]
    w_ref, a_ref, o_ref = refs[parts:]
    tokens = w_ref.shape[2]
    own = rank // 2 // parts
    step = min(8, own)
    tile = 512 if tokens % 512 == 0 else tokens
    o_ref[:, tokens:] = lane_squares(chunks)
    for t in range(0, tokens, tile):
        acc = jnp.zeros((GROUP, tile), jnp.float32)
        for m in range(modules):
            for odd in range(2):
                w = w_ref[m, odd * rank : (odd + 2) * rank, t : t + tile]
                for c, chunk in enumerate(chunks):
                    for i in range(0, own, step):
                        k = m * own + i
                        left = chunk[k : k + step].reshape(step * GROUP, LANES)
                        inner = jnp.dot(left, w, preferred_element_type=jnp.float32)
                        for s in range(step):
                            row = 2 * (c * own + i + s) + odd
                            acc += inner[s * GROUP : (s + 1) * GROUP] * a_ref[m, row : row + 1, t : t + tile]
        o_ref[:, t : t + tile] = acc


def bulk_kernel(count, parts, modules, rank, ring, core, *refs):
    blocks = [refs[b * parts : (b + 1) * parts] for b in range(count)]
    w_ref, b_ref, n_ref, keep_ref, send_ref, both = refs[count * parts :]
    tokens = w_ref.shape[2]
    own = rank // 2 // parts
    tile = 256 if tokens % 256 == 0 else tokens
    half = keep_ref.shape[0] // GROUP
    send_ref[half * GROUP :, :tokens] = n_ref[...]
    for b in range(count):
        both[b * GROUP : (b + 1) * GROUP, tokens:] = lane_squares(blocks[b])

    @pl.loop(0, tokens // tile)
    def _(t):
        lanes = pl.ds(pl.multiple_of(t * tile, tile), tile)
        acc = jnp.zeros((count * GROUP, tile), jnp.float32)
        for m in range(modules):
            grad = w_ref[m, :rank, lanes]
            for c in range(parts):
                for i in range(0, own, 2):
                    k = m * own + i
                    row = 2 * (c * own + i)
                    left = jnp.concatenate(
                        [
                            jnp.concatenate([blocks[b][c][k + s] for b in range(count)], axis=0)
                            for s in range(2)
                        ],
                        axis=1,
                    )
                    right = jnp.concatenate(
                        [grad * b_ref[m, row + s : row + s + 1, lanes] for s in range(4)], axis=0
                    )
                    acc += jnp.dot(left, right, preferred_element_type=jnp.float32)
        both[:, lanes] = acc

    me = lax.axis_index("proj") if core else 0
    for b, index in enumerate(ring()):
        rows = both[b * GROUP : (b + 1) * GROUP]
        at = pl.multiple_of(lax.rem(index, half) * GROUP, GROUP)

        @pl.when(index // half == me)
        def _():
            keep_ref[pl.ds(at, GROUP), :] = rows

        @pl.when(index // half != me)
        def _():
            send_ref[pl.ds(at, GROUP), :] = rows


def scaled(rows, tokens, width, token_scale):
    square = jnp.sum(rows[:, tokens:], axis=1, keepdims=True)
    return rows[:, :tokens] * lax.rsqrt(square / width + epsilon) * token_scale


def most_kernel(width, keep_ref, far_ref, n_ref, o_ref, s_ref):
    rows, tokens = o_ref.shape
    norm = n_ref[...] + far_ref[rows:, :tokens]
    scale = lax.rsqrt(norm / width + epsilon) / jnp.sqrt(jnp.float32(width))
    s_ref[...] = scale
    o_ref[...] = scaled(keep_ref[...] + far_ref[:rows], tokens, width, scale[:1])


def rest_kernel(width, ring, own_ref, far_ref, s_ref, most_ref, o_ref, rows, sem):
    del most_ref
    tokens = o_ref.shape[1]
    half = o_ref.shape[0] // GROUP
    index = ring()

    @pl.when(index // half == lax.axis_index("proj"))
    def _():
        rows[...] = scaled(own_ref[...] + far_ref[...], tokens, width, s_ref[:1])
        at = pl.multiple_of(lax.rem(index, half) * GROUP, GROUP)
        copy = pltpu.make_async_copy(rows, o_ref.at[pl.ds(at, GROUP), :], sem)
        copy.start()
        copy.wait()


def local(train_factors, query_grads):
    tokens, modules, doubled = train_factors.shape
    rank = doubled // 2
    pairs = rank // 2
    ex, proj = lax.axis_size("ex"), lax.axis_size("proj")
    queries = query_grads.shape[0]
    width = modules * proj * rank * rank
    wide = tokens + LANES
    columns = queries * ex // proj

    token_rows = train_factors.reshape(tokens * modules, doubled)
    weights, acts, narrow, norm = pl.pallas_call(
        functools.partial(token_kernel, modules, rank),
        out_shape=(
            jax.ShapeDtypeStruct((modules, 3 * rank, tokens), jnp.bfloat16),
            jax.ShapeDtypeStruct((modules, rank, tokens), jnp.float32),
            jax.ShapeDtypeStruct((modules, rank, tokens), jnp.bfloat16),
            jax.ShapeDtypeStruct((8, tokens), jnp.float32),
        ),
        in_specs=[VMEM],
        out_specs=(VMEM,) * 4,
        scratch_shapes=[pltpu.VMEM((tokens * modules, doubled), jnp.float32)],
        compiler_params=PARAMS,
        name="tokens",
    )(token_rows)

    def swapped(x):
        return lax.ppermute(x, "proj", [(i, (i + 1) % proj) for i in range(proj)])

    def bulk(blocks, ring):
        count, parts = len(blocks), len(blocks[0])
        return pl.pallas_call(
            functools.partial(bulk_kernel, count, parts, modules, rank, ring, proj > 1),
            out_shape=(
                jax.ShapeDtypeStruct((columns, wide), jnp.float32),
                jax.ShapeDtypeStruct((columns + 8, wide), jnp.float32),
            ),
            in_specs=[VMEM] * (count * parts + 3),
            out_specs=(VMEM, VMEM),
            scratch_shapes=[pltpu.VMEM((count * GROUP, wide), jnp.float32)],
            compiler_params=PARAMS,
            cost_estimate=pl.CostEstimate(
                flops=4 * 2 * 128 * modules * rank * rank * tokens,
                bytes_accessed=4 * 1024 * 1024,
                transcendentals=0,
            ),
            name="bulk",
        )(*[chunk for block in blocks for chunk in block], weights, narrow, norm)

    def most(keep, far):
        return pl.pallas_call(
            functools.partial(most_kernel, width),
            out_shape=(
                jax.ShapeDtypeStruct((columns, tokens), jnp.float32),
                jax.ShapeDtypeStruct((8, tokens), jnp.float32),
            ),
            in_specs=[VMEM] * 3,
            out_specs=(VMEM, VMEM),
            compiler_params=PARAMS,
            name="most",
        )(keep, far, norm)

    if queries == GROUP and ex % 2 == 0 and ex <= 16:
        order = list(range(0, ex, 2)) + list(range(ex - 1, 0, -2))
        up_pairs = [(order[i], order[(i + 1) % ex]) for i in range(ex)]
        down_pairs = [(b, a) for a, b in up_pairs]

        def up(x):
            return lax.ppermute(x, "ex", up_pairs)

        def down(x):
            return lax.ppermute(x, "ex", down_pairs)

        rows = query_grads.reshape(queries, modules, pairs, LANES)
        rows = rows.transpose(0, 2, 1, 3).reshape(queries * pairs * modules, LANES)
        chunk = jax.ShapeDtypeStruct((modules * pairs // 2, queries, LANES), jnp.bfloat16)
        block = pl.pallas_call(
            functools.partial(query_kernel, modules, pairs),
            out_shape=(chunk, chunk),
            in_specs=[VMEM],
            out_specs=(VMEM, VMEM),
            compiler_params=PARAMS,
            name="queries",
        )(rows)
        below, above = block, block
        blocks, steps = [block], [0]
        for step in range(1, ex // 2):
            first = (up(below[0]), down(above[0]))
            second = (up(below[1]), down(above[1]))
            below, above = (first[0], second[0]), (first[1], second[1])
            blocks += [below, above]
            steps += [-step, step]
        across = (up(below[0]), down(above[1]))

        def ring():
            here = place_of(lax.axis_index("ex"), ex)
            return [index_at(here + step, ex) for step in steps]

        def opposite():
            return index_at(place_of(lax.axis_index("ex"), ex) + ex // 2, ex)

        keep, send = bulk(blocks, ring)
        out, scale = most(keep, swapped(send))
        mine = pl.pallas_call(
            functools.partial(last_kernel, 2, modules, rank),
            out_shape=jax.ShapeDtypeStruct((GROUP, wide), jnp.float32),
            in_specs=[VMEM] * 4,
            out_specs=VMEM,
            compiler_params=PARAMS,
            name="last",
        )(*across, weights, acts)
        out = pl.pallas_call(
            functools.partial(rest_kernel, width, opposite),
            out_shape=jax.ShapeDtypeStruct((columns, tokens), jnp.float32),
            in_specs=[VMEM, VMEM, VMEM, ANY],
            out_specs=ANY,
            scratch_shapes=[pltpu.VMEM((GROUP, tokens), jnp.float32), pltpu.SemaphoreType.DMA],
            input_output_aliases={3: 0},
            compiler_params=PARAMS,
            name="rest",
        )(mine, swapped(mine), scale, out)
    else:
        gathered = lax.all_gather(query_grads.astype(jnp.bfloat16), "ex", axis=0, tiled=True)
        count = queries * ex // GROUP
        gathered = gathered.reshape(count, GROUP, modules * pairs, LANES).transpose(0, 2, 1, 3)
        blocks = [(gathered[i],) for i in range(count)]
        keep, send = bulk(blocks, lambda: [jnp.int32(i) for i in range(count)])
        out, _ = most(keep, swapped(send))
    return out.T


def solution(mesh):
    return jax.shard_map(
        local,
        mesh=mesh,
        in_specs=(P(("groups", "ex"), "proj", None), P(("groups", "ex"), "proj", None)),
        out_specs=P(("groups", "ex"), "proj"),
        check_vma=False,
    )
```

time: 134 us -> 38.7 us (0.29)
  waiting for transfers between devices: 58.4 us -> 13.8 us
  matrix products: 27.5 us -> 0 us
  local copies, waits for them, and re-layouts: 21.2 us -> 1.04 us
  starting transfers between devices: 0.04 us -> 16.9 us
  between operations: 13.4 us -> 0.05 us
  other arithmetic: 9.53 us -> 0 us
  Pallas kernels: 0 us -> 6.69 us
  blocking collectives: 2.51 us -> 0 us
    all_gather x1 -> x0, waiting for transfers between devices: 50.3 us -> none  [local(): lax.all_gather(query_unit, 'ex', axis=0, tiled=True)]
    dot_general x8 -> x0, matrix products: 27.5 us -> none  [one_block(): jnp.einsum('tmj,qmij->tmqi', grad_rows, query_mats, preferred_element_typ...]
    ppermute x0 -> x16, starting transfers between devices: none -> 16.9 us  [the longest x7 10.1 us: up(): return lax.ppermute(x, 'ex', up_pairs)]
    ppermute x0 -> x16, waiting for transfers between devices: none -> 13.8 us  [the longest x7 10.8 us: up(): return lax.ppermute(x, 'ex', up_pairs)]
    dynamic_slice x16 -> x0, local copies, waits for them, and re-layouts: 8.08 us -> none  [contract_tokens(): return lax.map(one_block, blocks).reshape(token_count, query_count)]
    reduce_scatter x1 -> x0, waiting for transfers between devices: 8.04 us -> none  [local(): lax.psum_scatter(block_scores, 'proj', scatter_dimension=1, tiled=True)]
    pallas_call x0 -> x6, Pallas kernels: none -> 6.69 us  [the longest x1 3.33 us: bulk(): pl.pallas_call(functools.partial(bulk_kernel, count, parts, modules, rank...]
    while x1 -> x0, local copies, waits for them, and re-layouts: 6.47 us -> none  [contract_tokens(): return lax.map(one_block, blocks).reshape(token_count, query_count)]
  transfers between devices with their start and end apart: 2 -> 16, of which waited for: 2 -> 11; matrix products, arithmetic and copies ran while one was open for 0% -> 0% of each run, Pallas kernels for 0% -> 6%
where the time goes in v2:
time: 38.7 us; the launch traced here: 38.5 us
  starting transfers between devices  16.9 us (44%)
  waiting for transfers between devices  13.8 us (36%)
  Pallas kernels  6.69 us (17%)
  local copies, waits for them, and re-layouts  1.04 us (3%)
    ppermute x7, waiting for transfers between devices, up(): return lax.ppermute(x, 'ex', up_pairs)  10.8 us
    ppermute x7, starting transfers between devices, up(): return lax.ppermute(x, 'ex', up_pairs)  10.1 us
    ppermute x2, starting transfers between devices, swapped(): return lax.ppermute(x, 'proj', [(i, (i + 1) % proj) for i in range(proj)])  5.73 us
    pallas_call x1, Pallas kernels, bulk(): pl.pallas_call(functools.partial(bulk_kernel, count, parts, modules, rank...  3.33 us
    ppermute x7, waiting for transfers between devices, down(): return lax.ppermute(x, 'ex', down_pairs)  2.94 us
    pallas_call x1, Pallas kernels, local(): pl.pallas_call(functools.partial(last_kernel, 2, modules, rank), out_shap...  1.25 us
    ppermute x7, starting transfers between devices, down(): return lax.ppermute(x, 'ex', down_pairs)  1.14 us
    unnamed x4, local copies, waits for them, and re-layouts  1.04 us
  transfers between devices with their start and end apart: 16, of which 11 were waited for; matrix products, arithmetic and copies ran while one was open for 0% of the time, Pallas kernels for 6%

profile of v2, /device:TPU:1, one launch (start us, length us, event | category | flops | bytes accessed | tf_op | source)
XLA Modules:
  0.0 38.5 jit_solution(16390119530465500113)
XLA Ops:
  0.0 0.0 copy-start
  0.0 1.0 %copy-done = f32[16,2,4096]{2,1,0:T(2,128)S(1)} copy-done((f32[16,2,4096]{2,1,0:T(2,128)S(1)}, f32[16,2,4096]{2,1,0:T(2,128)}, u32[]{:S(2)}) %copy-start) | copy-done | bytes 524312
  1.0 0.0 copy-start.1
  1.0 0.3 queries.1
  1.3 2.2 %collective-permute-start = (bf16[32,16,128]{2,1,0:T(8,128)(2,1)S(1)}, bf16[32,16,128]{2,1,0:T(8,128)(2,1)S(1)}, u32[]{:S(2)}, u32[]{:S(2)}) collective-permute-start(bf16[32,16,128]{2,1,0:T(8,128)(2,1)S(1)} %get-tuple-element.15.refs_0_), channel_id=1, source_target_pairs={{0,4},{4,8},{8,12},{12,14},{14,10},{10,6},{6,2},{2,0},{1,5},{5,9},... | collective-permute-start | bytes 393224 | tf_op jit(solution)/shard_map/ppermute | solution.py:234
  3.5 0.0 collective-permute-start.4
  3.5 1.5 %collective-permute-start.9 = (bf16[32,16,128]{2,1,0:T(8,128)(2,1)S(1)}, bf16[32,16,128]{2,1,0:T(8,128)(2,1)S(1)}, u32[]{:S(2)}, u32[]{:S(2)}) collective-permute-start(bf16[32,16,128]{2,1,0:T(8,128)(2,1)S(1)} %get-tuple-element.16.refs_1_), channel_id=1, source_target_pairs={{0,4},{4,8},{8,12},{12,14},{14,10},{10,6},{6,2},{2,0},{1,5},{5,9},... | collective-permute-start | bytes 393224 | tf_op jit(solution)/shard_map/ppermute | solution.py:234
  5.0 0.0 collective-permute-start.10
  5.0 1.7 %collective-permute-done.refs_2_ = bf16[32,16,128]{2,1,0:T(8,128)(2,1)S(1)} collective-permute-done((bf16[32,16,128]{2,1,0:T(8,128)(2,1)S(1)}, bf16[32,16,128]{2,1,0:T(8,128)(2,1)S(1)}, u32[]{:S(2)}, u32[]{:S(2)}) %collective-permute-start) | collective-permute-done | bytes 131104 | tf_op jit(solution)/shard_map/ppermute | solution.py:234
  6.7 1.2 %collective-permute-start.1 = (bf16[32,16,128]{2,1,0:T(8,128)(2,1)S(1)}, bf16[32,16,128]{2,1,0:T(8,128)(2,1)S(1)}, u32[]{:S(2)}, u32[]{:S(2)}) collective-permute-start(bf16[32,16,128]{2,1,0:T(8,128)(2,1)S(1)} %collective-permute-done.refs_2_), channel_id=1, source_target_pairs={{0,4},{4,8},{8,12},{12,14},{14,10},{10,6},{6,2},{2,0},{1,5},{5,9},... | collective-permute-start | bytes 393224 | tf_op jit(solution)/shard_map/ppermute | solution.py:234
  7.9 0.0 collective-permute-done.4.refs_5_
  7.9 0.2 collective-permute-start.5
  8.1 1.3 %collective-permute-done.9.refs_3_ = bf16[32,16,128]{2,1,0:T(8,128)(2,1)S(1)} collective-permute-done((bf16[32,16,128]{2,1,0:T(8,128)(2,1)S(1)}, bf16[32,16,128]{2,1,0:T(8,128)(2,1)S(1)}, u32[]{:S(2)}, u32[]{:S(2)}) %collective-permute-start.9) | collective-permute-done | bytes 131104 | tf_op jit(solution)/shard_map/ppermute | solution.py:234
  9.5 1.2 %collective-permute-start.11 = (bf16[32,16,128]{2,1,0:T(8,128)(2,1)S(1)}, bf16[32,16,128]{2,1,0:T(8,128)(2,1)S(1)}, u32[]{:S(2)}, u32[]{:S(2)}) collective-permute-start(bf16[32,16,128]{2,1,0:T(8,128)(2,1)S(1)} %collective-permute-done.9.refs_3_), channel_id=1, source_target_pairs={{0,4},{4,8},{8,12},{12,14},{14,10},{10,6},{6,2},{2,0},{1,5},{5,9},... | collective-permute-start | bytes 393224 | tf_op jit(solution)/shard_map/ppermute | solution.py:234
  10.7 0.0 collective-permute-done.10.refs_4_
  10.7 0.2 collective-permute-start.12
  10.9 0.8 %collective-permute-done.1.refs_6_ = bf16[32,16,128]{2,1,0:T(8,128)(2,1)S(1)} collective-permute-done((bf16[32,16,128]{2,1,0:T(8,128)(2,1)S(1)}, bf16[32,16,128]{2,1,0:T(8,128)(2,1)S(1)}, u32[]{:S(2)}, u32[]{:S(2)}) %collective-permute-start.1) | collective-permute-done | bytes 131104 | tf_op jit(solution)/shard_map/ppermute | solution.py:234
  11.7 1.5 %collective-permute-start.2 = (bf16[32,16,128]{2,1,0:T(8,128)(2,1)S(1)}, bf16[32,16,128]{2,1,0:T(8,128)(2,1)S(1)}, u32[]{:S(2)}, u32[]{:S(2)}) collective-permute-start(bf16[32,16,128]{2,1,0:T(8,128)(2,1)S(1)} %collective-permute-done.1.refs_6_), channel_id=1, source_target_pairs={{0,4},{4,8},{8,12},{12,14},{14,10},{10,6},{6,2},{2,0},{1,5},{5,9},... | collective-permute-start | bytes 393224 | tf_op jit(solution)/shard_map/ppermute | solution.py:234
  13.2 0.0 collective-permute-done.5.refs_9_
  13.3 0.0 collective-permute-start.6
  13.3 1.5 %collective-permute-done.11.refs_7_ = bf16[32,16,128]{2,1,0:T(8,128)(2,1)S(1)} collective-permute-done((bf16[32,16,128]{2,1,0:T(8,128)(2,1)S(1)}, bf16[32,16,128]{2,1,0:T(8,128)(2,1)S(1)}, u32[]{:S(2)}, u32[]{:S(2)}) %collective-permute-start.11) | collective-permute-done | bytes 131104 | tf_op jit(solution)/shard_map/ppermute | solution.py:234
  14.7 1.1 %collective-permute-start.13 = (bf16[32,16,128]{2,1,0:T(8,128)(2,1)S(1)}, bf16[32,16,128]{2,1,0:T(8,128)(2,1)S(1)}, u32[]{:S(2)}, u32[]{:S(2)}) collective-permute-start(bf16[32,16,128]{2,1,0:T(8,128)(2,1)S(1)} %collective-permute-done.11.refs_7_), channel_id=1, source_target_pairs={{0,4},{4,8},{8,12},{12,14},{14,10},{10,6},{6,2},{2,0},{1,5},{5,9},... | collective-permute-start | bytes 393224 | tf_op jit(solution)/shard_map/ppermute | solution.py:234
  15.9 0.0 collective-permute-done.12.refs_8_
  15.9 0.5 %collective-permute-start.14 = (bf16[32,16,128]{2,1,0:T(8,128)(2,1)S(1)}, bf16[32,16,128]{2,1,0:T(8,128)(2,1)S(1)}, u32[]{:S(2)}, u32[]{:S(2)}) collective-permute-start(bf16[32,16,128]{2,1,0:T(8,128)(2,1)S(1)} %collective-permute-done.12.refs_8_), channel_id=1, source_target_pairs={{4,0},{8,4},{12,8},{14,12},{10,14},{6,10},{2,6},{0,2},{5,1},{9,5},... | collective-permute-start | bytes 393224 | tf_op jit(solution)/shard_map/ppermute | solution.py:237
  16.3 0.0 copy-done.1
  16.3 0.3 tokens.1
  16.6 0.8 %collective-permute-done.2.refs_10_ = bf16[32,16,128]{2,1,0:T(8,128)(2,1)S(1)} collective-permute-done((bf16[32,16,128]{2,1,0:T(8,128)(2,1)S(1)}, bf16[32,16,128]{2,1,0:T(8,128)(2,1)S(1)}, u32[]{:S(2)}, u32[]{:S(2)}) %collective-permute-start.2) | collective-permute-done | bytes 131104 | tf_op jit(solution)/shard_map/ppermute | solution.py:234
  17.5 0.9 %collective-permute-done.6.refs_13_ = bf16[32,16,128]{2,1,0:T(8,128)(2,1)S(1)} collective-permute-done((bf16[32,16,128]{2,1,0:T(8,128)(2,1)S(1)}, bf16[32,16,128]{2,1,0:T(8,128)(2,1)S(1)}, u32[]{:S(2)}, u32[]{:S(2)}) %collective-permute-start.6) | collective-permute-done | bytes 131104 | tf_op jit(solution)/shard_map/ppermute | solution.py:237
  18.4 1.1 %collective-permute-done.13.refs_11_ = bf16[32,16,128]{2,1,0:T(8,128)(2,1)S(1)} collective-permute-done((bf16[32,16,128]{2,1,0:T(8,128)(2,1)S(1)}, bf16[32,16,128]{2,1,0:T(8,128)(2,1)S(1)}, u32[]{:S(2)}, u32[]{:S(2)}) %collective-permute-start.13) | collective-permute-done | bytes 131104 | tf_op jit(solution)/shard_map/ppermute | solution.py:234
  19.5 1.0 %collective-permute-done.14.refs_12_ = bf16[32,16,128]{2,1,0:T(8,128)(2,1)S(1)} collective-permute-done((bf16[32,16,128]{2,1,0:T(8,128)(2,1)S(1)}, bf16[32,16,128]{2,1,0:T(8,128)(2,1)S(1)}, u32[]{:S(2)}, u32[]{:S(2)}) %collective-permute-start.14) | collective-permute-done | bytes 131104 | tf_op jit(solution)/shard_map/ppermute | solution.py:237
  20.5 3.3 %bulk.1 = (f32[64,1152]{1,0:T(8,128)S(1)}, f32[72,1152]{1,0:T(8,128)S(1)}) custom-call(bf16[32,16,128]{2,1,0:T(8,128)(2,1)S(1)} %get-tuple-element.15.refs_0_, bf16[32,16,128]{2,1,0:T(8,128)(2,1)S(1)} %get-tuple-element.16.refs_1_, bf16[32,16,128]{2,1,0:T(8,128)(2,1)S(1)} %collective-permute-done.refs_2_, ...), custom_call_target="tpu_custom_call" | custom-call | flops 8589934592 | bytes 4194304 | tf_op jit(solution)/shard_map/bulk/pallas_call | solution.py:197
  23.9 4.5 %collective-permute-start.15 = (f32[72,1152]{1,0:T(8,128)S(1)}, f32[72,1152]{1,0:T(8,128)S(1)}, u32[]{:S(2)}, u32[]{:S(2)}) collective-permute-start(f32[72,1152]{1,0:T(8,128)S(1)} %get-tuple-element.22), channel_id=1, source_target_pairs={{0,1},{1,0},{2,3},{3,2},{4,5},{5,4},{6,7},{7,6},{8,9},{9,8},{10,11... | collective-permute-start | bytes 995336 | tf_op jit(solution)/shard_map/ppermute | solution.py:193
  28.4 1.3 %collective-permute-start.3 = (bf16[32,16,128]{2,1,0:T(8,128)(2,1)S(1)}, bf16[32,16,128]{2,1,0:T(8,128)(2,1)S(1)}, u32[]{:S(2)}, u32[]{:S(2)}) collective-permute-start(bf16[32,16,128]{2,1,0:T(8,128)(2,1)S(1)} %collective-permute-done.2.refs_10_), channel_id=1, source_target_pairs={{0,4},{4,8},{8,12},{12,14},{14,10},{10,6},{6,2},{2,0},{1,5},{5,9},... | collective-permute-start | bytes 393224 | tf_op jit(solution)/shard_map/ppermute | solution.py:234
  29.7 0.2 collective-permute-start.7
  29.8 3.6 %collective-permute-done.3.refs_0_ = bf16[32,16,128]{2,1,0:T(8,128)(2,1)S(1)} collective-permute-done((bf16[32,16,128]{2,1,0:T(8,128)(2,1)S(1)}, bf16[32,16,128]{2,1,0:T(8,128)(2,1)S(1)}, u32[]{:S(2)}, u32[]{:S(2)}) %collective-permute-start.3) | collective-permute-done | bytes 131104 | tf_op jit(solution)/shard_map/ppermute | solution.py:234
  33.4 1.0 %collective-permute-done.7.refs_1_ = bf16[32,16,128]{2,1,0:T(8,128)(2,1)S(1)} collective-permute-done((bf16[32,16,128]{2,1,0:T(8,128)(2,1)S(1)}, bf16[32,16,128]{2,1,0:T(8,128)(2,1)S(1)}, u32[]{:S(2)}, u32[]{:S(2)}) %collective-permute-start.7) | collective-permute-done | bytes 131104 | tf_op jit(solution)/shard_map/ppermute | solution.py:237
  34.4 1.3 %last.1.own_ref = f32[16,1152]{1,0:T(8,128)S(1)} custom-call(bf16[32,16,128]{2,1,0:T(8,128)(2,1)S(1)} %collective-permute-done.3.refs_0_, bf16[32,16,128]{2,1,0:T(8,128)(2,1)S(1)} %collective-permute-done.7.refs_1_, bf16[2,192,1024]{2,1,0:T(8,128)(2,1)S(1)} %get-tuple-element.17.refs_2_.refs_14_, f32[2,64,1024]{2,1,0:T(8,128)S(1)} %get-tuple-element.18.refs_3_), custom_call_target="tpu_custom_call" | custom-call | tf_op jit(solution)/shard_map/last/pallas_call | solution.py:269
  35.7 1.2 %collective-permute-start.8 = (f32[16,1152]{1,0:T(8,128)S(1)}, f32[16,1152]{1,0:T(8,128)S(1)}, u32[]{:S(2)}, u32[]{:S(2)}) collective-permute-start(f32[16,1152]{1,0:T(8,128)S(1)} %last.1.own_ref), channel_id=1, source_target_pairs={{0,1},{1,0},{2,3},{3,2},{4,5},{5,4},{6,7},{7,6},{8,9},{9,8},{10,11... | collective-permute-start | bytes 221192 | tf_op jit(solution)/shard_map/ppermute | solution.py:193
  36.9 0.0 collective-permute-done.15.far_ref
  36.9 0.8 %most.1 = (f32[64,1024]{1,0:T(8,128)}, f32[8,1024]{1,0:T(8,128)S(1)}) custom-call(f32[64,1152]{1,0:T(8,128)S(1)} %get-tuple-element.21.keep_ref, f32[72,1152]{1,0:T(8,128)S(1)} %collective-permute-done.15.far_ref, f32[8,1024]{1,0:T(8,128)S(1)} %get-tuple-element.20.refs_16_.n_ref), custom_call_target="tpu_custom_call" | custom-call | tf_op jit(solution)/shard_map/most/pallas_call | solution.py:216
  37.7 0.1 collective-permute-done.8.far_ref
  37.8 0.7 %rest.1 = f32[64,1024]{1,0:T(8,128)} custom-call(f32[16,1152]{1,0:T(8,128)S(1)} %last.1.own_ref, f32[16,1152]{1,0:T(8,128)S(1)} %collective-permute-done.8.far_ref, f32[8,1024]{1,0:T(8,128)S(1)} %get-tuple-element.23.s_ref, f32[64,1024]{1,0:T(8,128)} %get-tuple-element.24.most_ref), custom_call_target="tpu_custom_call", output_to_operand_aliasing={{}: (3, {})} | custom-call | tf_op jit(solution)/shard_map/rest/pallas_call | solution.py:277
Async XLA Ops:
  0.0 1.0 %copy-start = (f32[16,2,4096]{2,1,0:T(2,128)S(1)}, f32[16,2,4096]{2,1,0:T(2,128)}, u32[]{:S(2)}) copy-start(f32[16,2,4096]{2,1,0:T(2,128)} %param.3) | copy-start | bytes 1572868
  1.0 15.3 %copy-start.1 = (bf16[1024,2,128]{2,1,0:T(2,128)(2,1)S(1)}, bf16[1024,2,128]{2,1,0:T(2,128)(2,1)}, u32[]{:S(2)}) copy-start(bf16[1024,2,128]{2,1,0:T(2,128)(2,1)} %param.2) | copy-start | bytes 1572868
  1.3 5.3 %collective-permute-start = (bf16[32,16,128]{2,1,0:T(8,128)(2,1)S(1)}, bf16[32,16,128]{2,1,0:T(8,128)(2,1)S(1)}, u32[]{:S(2)}, u32[]{:S(2)}) collective-permute-start(bf16[32,16,128]{2,1,0:T(8,128)(2,1)S(1)} %get-tuple-element.15.refs_0_), channel_id=1, source_target_pairs={{0,4},{4,8},{8,12},{12,14},{14,10},{10,6},{6,2},{2,0},{1,5},{5,9},... | collective-permute-start | bytes 393224 | tf_op jit(solution)/shard_map/ppermute | solution.py:234
  3.5 4.4 %collective-permute-start.4 = (bf16[32,16,128]{2,1,0:T(8,128)(2,1)S(1)}, bf16[32,16,128]{2,1,0:T(8,128)(2,1)S(1)}, u32[]{:S(2)}, u32[]{:S(2)}) collective-permute-start(bf16[32,16,128]{2,1,0:T(8,128)(2,1)S(1)} %get-tuple-element.16.refs_1_), channel_id=1, source_target_pairs={{4,0},{8,4},{12,8},{14,12},{10,14},{6,10},{2,6},{0,2},{5,1},{9,5},... | collective-permute-start | bytes 393224 | tf_op jit(solution)/shard_map/ppermute | solution.py:237
  3.5 5.9 %collective-permute-start.9 = (bf16[32,16,128]{2,1,0:T(8,128)(2,1)S(1)}, bf16[32,16,128]{2,1,0:T(8,128)(2,1)S(1)}, u32[]{:S(2)}, u32[]{:S(2)}) collective-permute-start(bf16[32,16,128]{2,1,0:T(8,128)(2,1)S(1)} %get-tuple-element.16.refs_1_), channel_id=1, source_target_pairs={{0,4},{4,8},{8,12},{12,14},{14,10},{10,6},{6,2},{2,0},{1,5},{5,9},... | collective-permute-start | bytes 393224 | tf_op jit(solution)/shard_map/ppermute | solution.py:234
  5.0 5.7 %collective-permute-start.10 = (bf16[32,16,128]{2,1,0:T(8,128)(2,1)S(1)}, bf16[32,16,128]{2,1,0:T(8,128)(2,1)S(1)}, u32[]{:S(2)}, u32[]{:S(2)}) collective-permute-start(bf16[32,16,128]{2,1,0:T(8,128)(2,1)S(1)} %get-tuple-element.15.refs_0_), channel_id=1, source_target_pairs={{4,0},{8,4},{12,8},{14,12},{10,14},{6,10},{2,6},{0,2},{5,1},{9,5},... | collective-permute-start | bytes 393224 | tf_op jit(solution)/shard_map/ppermute | solution.py:237
  6.7 5.0 %collective-permute-start.1 = (bf16[32,16,128]{2,1,0:T(8,128)(2,1)S(1)}, bf16[32,16,128]{2,1,0:T(8,128)(2,1)S(1)}, u32[]{:S(2)}, u32[]{:S(2)}) collective-permute-start(bf16[32,16,128]{2,1,0:T(8,128)(2,1)S(1)} %collective-permute-done.refs_2_), channel_id=1, source_target_pairs={{0,4},{4,8},{8,12},{12,14},{14,10},{10,6},{6,2},{2,0},{1,5},{5,9},... | collective-permute-start | bytes 393224 | tf_op jit(solution)/shard_map/ppermute | solution.py:234
  7.9 5.4 %collective-permute-start.5 = (bf16[32,16,128]{2,1,0:T(8,128)(2,1)S(1)}, bf16[32,16,128]{2,1,0:T(8,128)(2,1)S(1)}, u32[]{:S(2)}, u32[]{:S(2)}) collective-permute-start(bf16[32,16,128]{2,1,0:T(8,128)(2,1)S(1)} %collective-permute-done.4.refs_5_), channel_id=1, source_target_pairs={{4,0},{8,4},{12,8},{14,12},{10,14},{6,10},{2,6},{0,2},{5,1},{9,5},... | collective-permute-start | bytes 393224 | tf_op jit(solution)/shard_map/ppermute | solution.py:237
  9.5 5.3 %collective-permute-start.11 = (bf16[32,16,128]{2,1,0:T(8,128)(2,1)S(1)}, bf16[32,16,128]{2,1,0:T(8,128)(2,1)S(1)}, u32[]{:S(2)}, u32[]{:S(2)}) collective-permute-start(bf16[32,16,128]{2,1,0:T(8,128)(2,1)S(1)} %collective-permute-done.9.refs_3_), channel_id=1, source_target_pairs={{0,4},{4,8},{8,12},{12,14},{14,10},{10,6},{6,2},{2,0},{1,5},{5,9},... | collective-permute-start | bytes 393224 | tf_op jit(solution)/shard_map/ppermute | solution.py:234
  10.7 5.2 %collective-permute-start.12 = (bf16[32,16,128]{2,1,0:T(8,128)(2,1)S(1)}, bf16[32,16,128]{2,1,0:T(8,128)(2,1)S(1)}, u32[]{:S(2)}, u32[]{:S(2)}) collective-permute-start(bf16[32,16,128]{2,1,0:T(8,128)(2,1)S(1)} %collective-permute-done.10.refs_4_), channel_id=1, source_target_pairs={{4,0},{8,4},{12,8},{14,12},{10,14},{6,10},{2,6},{0,2},{5,1},{9,5},... | collective-permute-start | bytes 393224 | tf_op jit(solution)/shard_map/ppermute | solution.py:237
  11.7 5.8 %collective-permute-start.2 = (bf16[32,16,128]{2,1,0:T(8,128)(2,1)S(1)}, bf16[32,16,128]{2,1,0:T(8,128)(2,1)S(1)}, u32[]{:S(2)}, u32[]{:S(2)}) collective-permute-start(bf16[32,16,128]{2,1,0:T(8,128)(2,1)S(1)} %collective-permute-done.1.refs_6_), channel_id=1, source_target_pairs={{0,4},{4,8},{8,12},{12,14},{14,10},{10,6},{6,2},{2,0},{1,5},{5,9},... | collective-permute-start | bytes 393224 | tf_op jit(solution)/shard_map/ppermute | solution.py:234
  13.3 5.1 %collective-permute-start.6 = (bf16[32,16,128]{2,1,0:T(8,128)(2,1)S(1)}, bf16[32,16,128]{2,1,0:T(8,128)(2,1)S(1)}, u32[]{:S(2)}, u32[]{:S(2)}) collective-permute-start(bf16[32,16,128]{2,1,0:T(8,128)(2,1)S(1)} %collective-permute-done.5.refs_9_), channel_id=1, source_target_pairs={{4,0},{8,4},{12,8},{14,12},{10,14},{6,10},{2,6},{0,2},{5,1},{9,5},... | collective-permute-start | bytes 393224 | tf_op jit(solution)/shard_map/ppermute | solution.py:237
  14.7 4.8 %collective-permute-start.13 = (bf16[32,16,128]{2,1,0:T(8,128)(2,1)S(1)}, bf16[32,16,128]{2,1,0:T(8,128)(2,1)S(1)}, u32[]{:S(2)}, u32[]{:S(2)}) collective-permute-start(bf16[32,16,128]{2,1,0:T(8,128)(2,1)S(1)} %collective-permute-done.11.refs_7_), channel_id=1, source_target_pairs={{0,4},{4,8},{8,12},{12,14},{14,10},{10,6},{6,2},{2,0},{1,5},{5,9},... | collective-permute-start | bytes 393224 | tf_op jit(solution)/shard_map/ppermute | solution.py:234
  15.9 4.7 %collective-permute-start.14 = (bf16[32,16,128]{2,1,0:T(8,128)(2,1)S(1)}, bf16[32,16,128]{2,1,0:T(8,128)(2,1)S(1)}, u32[]{:S(2)}, u32[]{:S(2)}) collective-permute-start(bf16[32,16,128]{2,1,0:T(8,128)(2,1)S(1)} %collective-permute-done.12.refs_8_), channel_id=1, source_target_pairs={{4,0},{8,4},{12,8},{14,12},{10,14},{6,10},{2,6},{0,2},{5,1},{9,5},... | collective-permute-start | bytes 393224 | tf_op jit(solution)/shard_map/ppermute | solution.py:237
  23.9 13.0 %collective-permute-start.15 = (f32[72,1152]{1,0:T(8,128)S(1)}, f32[72,1152]{1,0:T(8,128)S(1)}, u32[]{:S(2)}, u32[]{:S(2)}) collective-permute-start(f32[72,1152]{1,0:T(8,128)S(1)} %get-tuple-element.22), channel_id=1, source_target_pairs={{0,1},{1,0},{2,3},{3,2},{4,5},{5,4},{6,7},{7,6},{8,9},{9,8},{10,11... | collective-permute-start | bytes 995336 | tf_op jit(solution)/shard_map/ppermute | solution.py:193
  28.4 5.1 %collective-permute-start.3 = (bf16[32,16,128]{2,1,0:T(8,128)(2,1)S(1)}, bf16[32,16,128]{2,1,0:T(8,128)(2,1)S(1)}, u32[]{:S(2)}, u32[]{:S(2)}) collective-permute-start(bf16[32,16,128]{2,1,0:T(8,128)(2,1)S(1)} %collective-permute-done.2.refs_10_), channel_id=1, source_target_pairs={{0,4},{4,8},{8,12},{12,14},{14,10},{10,6},{6,2},{2,0},{1,5},{5,9},... | collective-permute-start | bytes 393224 | tf_op jit(solution)/shard_map/ppermute | solution.py:234
  29.7 4.7 %collective-permute-start.7 = (bf16[32,16,128]{2,1,0:T(8,128)(2,1)S(1)}, bf16[32,16,128]{2,1,0:T(8,128)(2,1)S(1)}, u32[]{:S(2)}, u32[]{:S(2)}) collective-permute-start(bf16[32,16,128]{2,1,0:T(8,128)(2,1)S(1)} %collective-permute-done.6.refs_13_), channel_id=1, source_target_pairs={{4,0},{8,4},{12,8},{14,12},{10,14},{6,10},{2,6},{0,2},{5,1},{9,5},... | collective-permute-start | bytes 393224 | tf_op jit(solution)/shard_map/ppermute | solution.py:237
  35.7 2.2 %collective-permute-start.8 = (f32[16,1152]{1,0:T(8,128)S(1)}, f32[16,1152]{1,0:T(8,128)S(1)}, u32[]{:S(2)}, u32[]{:S(2)}) collective-permute-start(f32[16,1152]{1,0:T(8,128)S(1)} %last.1.own_ref), channel_id=1, source_target_pairs={{0,1},{1,0},{2,3},{3,2},{4,5},{5,4},{6,7},{7,6},{8,9},{9,8},{10,11... | collective-permute-start | bytes 221192 | tf_op jit(solution)/shard_map/ppermute | solution.py:193

commit v3 on v2

--- a/solution.py
+++ b/solution.py
@@ -13,6 +13,7 @@
 VMEM = pl.BlockSpec(memory_space=pltpu.VMEM)
 ANY = pl.BlockSpec(memory_space=pl.ANY)
 PARAMS = pltpu.CompilerParams(vmem_limit_bytes=16 * 1024 * 1024)
+LONG = pl.CostEstimate(flops=10**10, bytes_accessed=4 * 1024 * 1024, transcendentals=0)
 
 
 def place_of(index, count):
@@ -87,41 +88,58 @@
         o_ref[:, t : t + tile] = acc
 
 
-def bulk_kernel(count, parts, modules, rank, ring, core, *refs):
-    blocks = [refs[b * parts : (b + 1) * parts] for b in range(count)]
-    w_ref, b_ref, n_ref, keep_ref, send_ref, both = refs[count * parts :]
+def products(blocks, part, parts, modules, rank, w_ref, b_ref, lanes):
+    own = rank // 2 // parts
+    acc = jnp.zeros((len(blocks) * GROUP, lanes.size), jnp.float32)
+    for m in range(modules):
+        grad = w_ref[m, :rank, lanes]
+        for i in range(0, own, 2):
+            k = m * own + i
+            row = 2 * (part * own + i)
+            left = jnp.concatenate(
+                [jnp.concatenate([block[k + s] for block in blocks], axis=0) for s in range(2)],
+                axis=1,
+            )
+            right = jnp.concatenate(
+                [grad * b_ref[m, row + s : row + s + 1, lanes] for s in range(4)], axis=0
+            )
+            acc += jnp.dot(left, right, preferred_element_type=jnp.float32)
+    return acc
+
+
+def early_kernel(count, parts, modules, rank, *refs):
+    blocks = refs[:count]
+    w_ref, b_ref, o_ref = refs[count:]
     tokens = w_ref.shape[2]
-    own = rank // 2 // parts
+    tile = 256 if tokens % 256 == 0 else tokens
+    for b in range(count):
+        o_ref[b * GROUP : (b + 1) * GROUP, tokens:] = lane_squares(blocks[b : b + 1])
+
+    @pl.loop(0, tokens // tile)
+    def _(t):
+        lanes = pl.ds(pl.multiple_of(t * tile, tile), tile)
+        o_ref[:, lanes] = products(blocks, parts - 1, parts, modules, rank, w_ref, b_ref, lanes)
+
+
+def late_kernel(count, parts, modules, rank, ring, *refs):
+    blocks = refs[:count]
+    w_ref, b_ref, n_ref, sum_ref, keep_ref, send_ref, both = refs[count:]
+    tokens = w_ref.shape[2]
     tile = 256 if tokens % 256 == 0 else tokens
     half = keep_ref.shape[0] // GROUP
     send_ref[half * GROUP :, :tokens] = n_ref[...]
     for b in range(count):
-        both[b * GROUP : (b + 1) * GROUP, tokens:] = lane_squares(blocks[b])
+        span = slice(b * GROUP, (b + 1) * GROUP)
+        both[span, tokens:] = sum_ref[span, tokens:] + lane_squares(blocks[b : b + 1])
 
     @pl.loop(0, tokens // tile)
     def _(t):
         lanes = pl.ds(pl.multiple_of(t * tile, tile), tile)
-        acc = jnp.zeros((count * GROUP, tile), jnp.float32)
-        for m in range(modules):
-            grad = w_ref[m, :rank, lanes]
-            for c in range(parts):
-                for i in range(0, own, 2):
-                    k = m * own + i
-                    row = 2 * (c * own + i)
-                    left = jnp.concatenate(
-                        [
-                            jnp.concatenate([blocks[b][c][k + s] for b in range(count)], axis=0)
-                            for s in range(2)
-                        ],
-                        axis=1,
-                    )
-                    right = jnp.concatenate(
-                        [grad * b_ref[m, row + s : row + s + 1, lanes] for s in range(4)], axis=0
-                    )
-                    acc += jnp.dot(left, right, preferred_element_type=jnp.float32)
-        both[:, lanes] = acc
-
-    me = lax.axis_index("proj") if core else 0
+        both[:, lanes] = sum_ref[:, lanes] + products(
+            blocks, 0, parts, modules, rank, w_ref, b_ref, lanes
+        )
+
+    me = lax.axis_index("proj")
     for b, index in enumerate(ring()):
         rows = both[b * GROUP : (b + 1) * GROUP]
         at = pl.multiple_of(lax.rem(index, half) * GROUP, GROUP)
@@ -194,23 +212,28 @@
 
     def bulk(blocks, ring):
         count, parts = len(blocks), len(blocks[0])
+        early = pl.pallas_call(
+            functools.partial(early_kernel, count, parts, modules, rank),
+            out_shape=jax.ShapeDtypeStruct((count * GROUP, wide), jnp.float32),
+            in_specs=[VMEM] * (count + 2),
+            out_specs=VMEM,
+            compiler_params=PARAMS,
+            cost_estimate=LONG,
+            name="early",
+        )(*[block[-1] for block in blocks], weights, narrow)
         return pl.pallas_call(
-            functools.partial(bulk_kernel, count, parts, modules, rank, ring, proj > 1),
+            functools.partial(late_kernel, count, parts, modules, rank, ring),
             out_shape=(
                 jax.ShapeDtypeStruct((columns, wide), jnp.float32),
                 jax.ShapeDtypeStruct((columns + 8, wide), jnp.float32),
             ),
-            in_specs=[VMEM] * (count * parts + 3),
+            in_specs=[VMEM] * (count + 4),
             out_specs=(VMEM, VMEM),
             scratch_shapes=[pltpu.VMEM((count * GROUP, wide), jnp.float32)],
             compiler_params=PARAMS,
-            cost_estimate=pl.CostEstimate(
-                flops=4 * 2 * 128 * modules * rank * rank * tokens,
-                bytes_accessed=4 * 1024 * 1024,
-                transcendentals=0,
-            ),
-            name="bulk",
-        )(*[chunk for block in blocks for chunk in block], weights, narrow, norm)
+            cost_estimate=LONG,
+            name="late",
+        )(*[block[0] for block in blocks], weights, narrow, norm, early)
 
     def most(keep, far):
         return pl.pallas_call(
@@ -222,6 +245,7 @@
             in_specs=[VMEM] * 3,
             out_specs=(VMEM, VMEM),
             compiler_params=PARAMS,
+            cost_estimate=LONG,
             name="most",
         )(keep, far, norm)
 
@@ -272,6 +296,7 @@
             in_specs=[VMEM] * 4,
             out_specs=VMEM,
             compiler_params=PARAMS,
+            cost_estimate=LONG,
             name="last",
         )(*across, weights, acts)
         out = pl.pallas_call(
@@ -287,8 +312,9 @@
     else:
         gathered = lax.all_gather(query_grads.astype(jnp.bfloat16), "ex", axis=0, tiled=True)
         count = queries * ex // GROUP
-        gathered = gathered.reshape(count, GROUP, modules * pairs, LANES).transpose(0, 2, 1, 3)
-        blocks = [(gathered[i],) for i in range(count)]
+        gathered = gathered.reshape(count, GROUP, modules, 2, pairs // 2, LANES)
+        gathered = gathered.transpose(0, 3, 2, 4, 1, 5).reshape(count, 2, -1, GROUP, LANES)
+        blocks = [(gathered[i, 0], gathered[i, 1]) for i in range(count)]
         keep, send = bulk(blocks, lambda: [jnp.int32(i) for i in range(count)])
         out, _ = most(keep, swapped(send))
     return out.T

time: 38.7 us -> 31.2 us (0.81)
  waiting for transfers between devices: 13.8 us -> 6.95 us
  starting transfers between devices: 16.9 us -> 15.6 us
  Pallas kernels: 6.69 us -> 7.38 us
    ppermute x7, waiting for transfers between devices: 10.8 us -> 6.62 us  [up(): return lax.ppermute(x, 'ex', up_pairs)]
    ppermute x7, waiting for transfers between devices: 2.94 us -> 0.03 us  [down(): return lax.ppermute(x, 'ex', down_pairs)]
    ppermute x2, starting transfers between devices: 5.73 us -> 4.31 us  [swapped(): return lax.ppermute(x, 'proj', [(i, (i + 1) % proj) for i in range(proj)])]
    pallas_call x1 -> x2, Pallas kernels: 3.33 us -> 4.01 us  [the longest x1 2.11 us: bulk(): pl.pallas_call(functools.partial(late_kernel, count, parts, modules, rank...]
  transfers between devices with their start and end apart: 16 -> 16, of which waited for: 11 -> 7; matrix products, arithmetic and copies ran while one was open for 0% -> 0% of each run, Pallas kernels for 6% -> 21%
where the time goes in v3:
time: 31.2 us; the launch traced here: 31 us
  starting transfers between devices  15.6 us (50%)
  Pallas kernels  7.38 us (24%)
  waiting for transfers between devices  6.95 us (22%)
  local copies, waits for them, and re-layouts  1.04 us (3%)
    ppermute x7, starting transfers between devices, up(): return lax.ppermute(x, 'ex', up_pairs)  10 us
    ppermute x7, waiting for transfers between devices, up(): return lax.ppermute(x, 'ex', up_pairs)  6.62 us
    ppermute x2, starting transfers between devices, swapped(): return lax.ppermute(x, 'proj', [(i, (i + 1) % proj) for i in range(proj)])  4.31 us
    pallas_call x1, Pallas kernels, bulk(): pl.pallas_call(functools.partial(late_kernel, count, parts, modules, rank...  2.11 us
    pallas_call x1, Pallas kernels, bulk(): pl.pallas_call(functools.partial(early_kernel, count, parts, modules, ran...  1.9 us
    pallas_call x1, Pallas kernels, local(): pl.pallas_call(functools.partial(last_kernel, 2, modules, rank), out_shap...  1.26 us
    ppermute x7, starting transfers between devices, down(): return lax.ppermute(x, 'ex', down_pairs)  1.22 us
    unnamed x4, local copies, waits for them, and re-layouts  1.04 us
  transfers between devices with their start and end apart: 16, of which 7 were waited for; matrix products, arithmetic and copies ran while one was open for 0% of the time, Pallas kernels for 21%

profile of v3, /device:TPU:1, one launch (start us, length us, event | category | flops | bytes accessed | tf_op | source)
XLA Modules:
  0.0 31.0 jit_solution(5517569352353950448)
XLA Ops:
  0.0 0.0 copy-start
  0.0 1.0 %copy-done = f32[16,2,4096]{2,1,0:T(2,128)S(1)} copy-done((f32[16,2,4096]{2,1,0:T(2,128)S(1)}, f32[16,2,4096]{2,1,0:T(2,128)}, u32[]{:S(2)}) %copy-start) | copy-done | bytes 524312
  1.0 0.0 copy-start.1
  1.0 0.3 queries.1
  1.3 2.2 %collective-permute-start = (bf16[32,16,128]{2,1,0:T(8,128)(2,1)S(1)}, bf16[32,16,128]{2,1,0:T(8,128)(2,1)S(1)}, u32[]{:S(2)}, u32[]{:S(2)}) collective-permute-start(bf16[32,16,128]{2,1,0:T(8,128)(2,1)S(1)} %get-tuple-element.15.refs_0_), channel_id=1, source_target_pairs={{0,4},{4,8},{8,12},{12,14},{14,10},{10,6},{6,2},{2,0},{1,5},{5,9},... | collective-permute-start | bytes 393224 | tf_op jit(solution)/shard_map/ppermute | solution.py:258
  3.5 0.0 collective-permute-start.4
  3.5 1.5 %collective-permute-start.12 = (bf16[32,16,128]{2,1,0:T(8,128)(2,1)S(1)}, bf16[32,16,128]{2,1,0:T(8,128)(2,1)S(1)}, u32[]{:S(2)}, u32[]{:S(2)}) collective-permute-start(bf16[32,16,128]{2,1,0:T(8,128)(2,1)S(1)} %get-tuple-element.16.refs_0_), channel_id=1, source_target_pairs={{0,4},{4,8},{8,12},{12,14},{14,10},{10,6},{6,2},{2,0},{1,5},{5,9},... | collective-permute-start | bytes 393224 | tf_op jit(solution)/shard_map/ppermute | solution.py:258
  5.0 0.0 collective-permute-start.9
  5.0 1.7 %collective-permute-done.refs_1_ = bf16[32,16,128]{2,1,0:T(8,128)(2,1)S(1)} collective-permute-done((bf16[32,16,128]{2,1,0:T(8,128)(2,1)S(1)}, bf16[32,16,128]{2,1,0:T(8,128)(2,1)S(1)}, u32[]{:S(2)}, u32[]{:S(2)}) %collective-permute-start) | collective-permute-done | bytes 131104 | tf_op jit(solution)/shard_map/ppermute | solution.py:258
  6.7 1.2 %collective-permute-start.1 = (bf16[32,16,128]{2,1,0:T(8,128)(2,1)S(1)}, bf16[32,16,128]{2,1,0:T(8,128)(2,1)S(1)}, u32[]{:S(2)}, u32[]{:S(2)}) collective-permute-start(bf16[32,16,128]{2,1,0:T(8,128)(2,1)S(1)} %collective-permute-done.refs_1_), channel_id=1, source_target_pairs={{0,4},{4,8},{8,12},{12,14},{14,10},{10,6},{6,2},{2,0},{1,5},{5,9},... | collective-permute-start | bytes 393224 | tf_op jit(solution)/shard_map/ppermute | solution.py:258
  7.9 0.0 collective-permute-done.4.refs_2_
  7.9 0.2 collective-permute-start.5
  8.1 1.3 %collective-permute-done.12.refs_1_ = bf16[32,16,128]{2,1,0:T(8,128)(2,1)S(1)} collective-permute-done((bf16[32,16,128]{2,1,0:T(8,128)(2,1)S(1)}, bf16[32,16,128]{2,1,0:T(8,128)(2,1)S(1)}, u32[]{:S(2)}, u32[]{:S(2)}) %collective-permute-start.12) | collective-permute-done | bytes 131104 | tf_op jit(solution)/shard_map/ppermute | solution.py:258
  9.5 1.2 %collective-permute-start.13 = (bf16[32,16,128]{2,1,0:T(8,128)(2,1)S(1)}, bf16[32,16,128]{2,1,0:T(8,128)(2,1)S(1)}, u32[]{:S(2)}, u32[]{:S(2)}) collective-permute-start(bf16[32,16,128]{2,1,0:T(8,128)(2,1)S(1)} %collective-permute-done.12.refs_1_), channel_id=1, source_target_pairs={{0,4},{4,8},{8,12},{12,14},{14,10},{10,6},{6,2},{2,0},{1,5},{5,9},... | collective-permute-start | bytes 393224 | tf_op jit(solution)/shard_map/ppermute | solution.py:258
  10.7 0.0 collective-permute-done.9.refs_2_
  10.7 0.2 collective-permute-start.10
  10.9 0.8 %collective-permute-done.1.refs_3_ = bf16[32,16,128]{2,1,0:T(8,128)(2,1)S(1)} collective-permute-done((bf16[32,16,128]{2,1,0:T(8,128)(2,1)S(1)}, bf16[32,16,128]{2,1,0:T(8,128)(2,1)S(1)}, u32[]{:S(2)}, u32[]{:S(2)}) %collective-permute-start.1) | collective-permute-done | bytes 131104 | tf_op jit(solution)/shard_map/ppermute | solution.py:258
  11.7 1.5 %collective-permute-start.2 = (bf16[32,16,128]{2,1,0:T(8,128)(2,1)S(1)}, bf16[32,16,128]{2,1,0:T(8,128)(2,1)S(1)}, u32[]{:S(2)}, u32[]{:S(2)}) collective-permute-start(bf16[32,16,128]{2,1,0:T(8,128)(2,1)S(1)} %collective-permute-done.1.refs_3_), channel_id=1, source_target_pairs={{0,4},{4,8},{8,12},{12,14},{14,10},{10,6},{6,2},{2,0},{1,5},{5,9},... | collective-permute-start | bytes 393224 | tf_op jit(solution)/shard_map/ppermute | solution.py:258
  13.2 0.0 collective-permute-done.5.refs_4_
  13.3 0.0 collective-permute-start.6
  13.3 1.5 %collective-permute-done.13.refs_3_ = bf16[32,16,128]{2,1,0:T(8,128)(2,1)S(1)} collective-permute-done((bf16[32,16,128]{2,1,0:T(8,128)(2,1)S(1)}, bf16[32,16,128]{2,1,0:T(8,128)(2,1)S(1)}, u32[]{:S(2)}, u32[]{:S(2)}) %collective-permute-start.13) | collective-permute-done | bytes 131104 | tf_op jit(solution)/shard_map/ppermute | solution.py:258
  14.7 1.1 %collective-permute-start.14 = (bf16[32,16,128]{2,1,0:T(8,128)(2,1)S(1)}, bf16[32,16,128]{2,1,0:T(8,128)(2,1)S(1)}, u32[]{:S(2)}, u32[]{:S(2)}) collective-permute-start(bf16[32,16,128]{2,1,0:T(8,128)(2,1)S(1)} %collective-permute-done.13.refs_3_), channel_id=1, source_target_pairs={{0,4},{4,8},{8,12},{12,14},{14,10},{10,6},{6,2},{2,0},{1,5},{5,9},... | collective-permute-start | bytes 393224 | tf_op jit(solution)/shard_map/ppermute | solution.py:258
  15.9 0.0 copy-done.1
  15.9 0.3 tokens.1
  16.1 0.0 collective-permute-done.10.refs_4_
  16.2 0.4 %collective-permute-start.11 = (bf16[32,16,128]{2,1,0:T(8,128)(2,1)S(1)}, bf16[32,16,128]{2,1,0:T(8,128)(2,1)S(1)}, u32[]{:S(2)}, u32[]{:S(2)}) collective-permute-start(bf16[32,16,128]{2,1,0:T(8,128)(2,1)S(1)} %collective-permute-done.10.refs_4_), channel_id=1, source_target_pairs={{4,0},{8,4},{12,8},{14,12},{10,14},{6,10},{2,6},{0,2},{5,1},{9,5},... | collective-permute-start | bytes 393224 | tf_op jit(solution)/shard_map/ppermute | solution.py:261
  16.5 0.9 %collective-permute-done.2.refs_5_ = bf16[32,16,128]{2,1,0:T(8,128)(2,1)S(1)} collective-permute-done((bf16[32,16,128]{2,1,0:T(8,128)(2,1)S(1)}, bf16[32,16,128]{2,1,0:T(8,128)(2,1)S(1)}, u32[]{:S(2)}, u32[]{:S(2)}) %collective-permute-start.2) | collective-permute-done | bytes 131104 | tf_op jit(solution)/shard_map/ppermute | solution.py:258
  17.5 1.2 %collective-permute-start.3 = (bf16[32,16,128]{2,1,0:T(8,128)(2,1)S(1)}, bf16[32,16,128]{2,1,0:T(8,128)(2,1)S(1)}, u32[]{:S(2)}, u32[]{:S(2)}) collective-permute-start(bf16[32,16,128]{2,1,0:T(8,128)(2,1)S(1)} %collective-permute-done.2.refs_5_), channel_id=1, source_target_pairs={{0,4},{4,8},{8,12},{12,14},{14,10},{10,6},{6,2},{2,0},{1,5},{5,9},... | collective-permute-start | bytes 393224 | tf_op jit(solution)/shard_map/ppermute | solution.py:258
  18.7 0.0 collective-permute-done.6.refs_6_
  18.7 0.4 %collective-permute-start.7 = (bf16[32,16,128]{2,1,0:T(8,128)(2,1)S(1)}, bf16[32,16,128]{2,1,0:T(8,128)(2,1)S(1)}, u32[]{:S(2)}, u32[]{:S(2)}) collective-permute-start(bf16[32,16,128]{2,1,0:T(8,128)(2,1)S(1)} %collective-permute-done.6.refs_6_), channel_id=1, source_target_pairs={{4,0},{8,4},{12,8},{14,12},{10,14},{6,10},{2,6},{0,2},{5,1},{9,5},... | collective-permute-start | bytes 393224 | tf_op jit(solution)/shard_map/ppermute | solution.py:261
  19.1 0.5 %collective-permute-done.14.refs_5_ = bf16[32,16,128]{2,1,0:T(8,128)(2,1)S(1)} collective-permute-done((bf16[32,16,128]{2,1,0:T(8,128)(2,1)S(1)}, bf16[32,16,128]{2,1,0:T(8,128)(2,1)S(1)}, u32[]{:S(2)}, u32[]{:S(2)}) %collective-permute-start.14) | collective-permute-done | bytes 131104 | tf_op jit(solution)/shard_map/ppermute | solution.py:258
  19.5 1.9 %early.1.refs_10_ = f32[112,1152]{1,0:T(8,128)S(1)} custom-call(bf16[32,16,128]{2,1,0:T(8,128)(2,1)S(1)} %get-tuple-element.16.refs_0_, bf16[32,16,128]{2,1,0:T(8,128)(2,1)S(1)} %collective-permute-done.12.refs_1_, bf16[32,16,128]{2,1,0:T(8,128)(2,1)S(1)} %collective-permute-done.4.refs_2_, bf16[32,16,128]{2,1,0:T(8,128)(2,1)S(1)} %collective-permute-done.13.refs_3_, ...), custom_call_target="tpu_custom_call" | custom-call | flops 10000000000 | bytes 4194304 | tf_op jit(solution)/shard_map/early/pallas_call | solution.py:215
  21.4 0.0 collective-permute-done.11.refs_6_
  21.4 2.1 %late.1 = (f32[64,1152]{1,0:T(8,128)S(1)}, f32[72,1152]{1,0:T(8,128)S(1)}) custom-call(bf16[32,16,128]{2,1,0:T(8,128)(2,1)S(1)} %get-tuple-element.15.refs_0_, bf16[32,16,128]{2,1,0:T(8,128)(2,1)S(1)} %collective-permute-done.refs_1_, bf16[32,16,128]{2,1,0:T(8,128)(2,1)S(1)} %collective-permute-done.9.refs_2_, ...), custom_call_target="tpu_custom_call" | custom-call | flops 10000000000 | bytes 4194304 | tf_op jit(solution)/shard_map/late/pallas_call | solution.py:224
  23.6 4.1 %collective-permute-start.15 = (f32[72,1152]{1,0:T(8,128)S(1)}, f32[72,1152]{1,0:T(8,128)S(1)}, u32[]{:S(2)}, u32[]{:S(2)}) collective-permute-start(f32[72,1152]{1,0:T(8,128)S(1)} %get-tuple-element.22), channel_id=1, source_target_pairs={{0,1},{1,0},{2,3},{3,2},{4,5},{5,4},{6,7},{7,6},{8,9},{9,8},{10,11... | collective-permute-start | bytes 995336 | tf_op jit(solution)/shard_map/ppermute | solution.py:211
  27.7 0.0 collective-permute-done.3.refs_0_
  27.7 0.0 collective-permute-done.7.refs_1_
  27.7 1.3 %last.1.own_ref = f32[16,1152]{1,0:T(8,128)S(1)} custom-call(bf16[32,16,128]{2,1,0:T(8,128)(2,1)S(1)} %collective-permute-done.3.refs_0_, bf16[32,16,128]{2,1,0:T(8,128)(2,1)S(1)} %collective-permute-done.7.refs_1_, bf16[2,192,1024]{2,1,0:T(8,128)(2,1)S(1)} %get-tuple-element.17.refs_2_.refs_7_, f32[2,64,1024]{2,1,0:T(8,128)S(1)} %get-tuple-element.18.refs_3_), custom_call_target="tpu_custom_call" | custom-call | flops 10000000000 | bytes 4194304 | tf_op jit(solution)/shard_map/last/pallas_call | solution.py:293
  28.9 0.2 collective-permute-start.8
  29.2 0.0 collective-permute-done.15.far_ref
  29.2 0.8 %most.1 = (f32[64,1024]{1,0:T(8,128)}, f32[8,1024]{1,0:T(8,128)S(1)}) custom-call(f32[64,1152]{1,0:T(8,128)S(1)} %get-tuple-element.21.keep_ref, f32[72,1152]{1,0:T(8,128)S(1)} %collective-permute-done.15.far_ref, f32[8,1024]{1,0:T(8,128)S(1)} %get-tuple-element.20.refs_9_.n_ref), custom_call_target="tpu_custom_call" | custom-call | flops 10000000000 | bytes 4194304 | tf_op jit(solution)/shard_map/most/pallas_call | solution.py:239
  30.0 0.3 collective-permute-done.8.far_ref
  30.3 0.7 %rest.1 = f32[64,1024]{1,0:T(8,128)} custom-call(f32[16,1152]{1,0:T(8,128)S(1)} %last.1.own_ref, f32[16,1152]{1,0:T(8,128)S(1)} %collective-permute-done.8.far_ref, f32[8,1024]{1,0:T(8,128)S(1)} %get-tuple-element.23.s_ref, f32[64,1024]{1,0:T(8,128)} %get-tuple-element.24.most_ref), custom_call_target="tpu_custom_call", output_to_operand_aliasing={{}: (3, {})} | custom-call | tf_op jit(solution)/shard_map/rest/pallas_call | solution.py:302
Async XLA Ops:
  0.0 1.0 %copy-start = (f32[16,2,4096]{2,1,0:T(2,128)S(1)}, f32[16,2,4096]{2,1,0:T(2,128)}, u32[]{:S(2)}) copy-start(f32[16,2,4096]{2,1,0:T(2,128)} %param.3) | copy-start | bytes 1572868
  1.0 14.8 %copy-start.1 = (bf16[1024,2,128]{2,1,0:T(2,128)(2,1)S(1)}, bf16[1024,2,128]{2,1,0:T(2,128)(2,1)}, u32[]{:S(2)}) copy-start(bf16[1024,2,128]{2,1,0:T(2,128)(2,1)} %param.2) | copy-start | bytes 1572868
  1.3 5.3 %collective-permute-start = (bf16[32,16,128]{2,1,0:T(8,128)(2,1)S(1)}, bf16[32,16,128]{2,1,0:T(8,128)(2,1)S(1)}, u32[]{:S(2)}, u32[]{:S(2)}) collective-permute-start(bf16[32,16,128]{2,1,0:T(8,128)(2,1)S(1)} %get-tuple-element.15.refs_0_), channel_id=1, source_target_pairs={{0,4},{4,8},{8,12},{12,14},{14,10},{10,6},{6,2},{2,0},{1,5},{5,9},... | collective-permute-start | bytes 393224 | tf_op jit(solution)/shard_map/ppermute | solution.py:258
  3.5 4.4 %collective-permute-start.4 = (bf16[32,16,128]{2,1,0:T(8,128)(2,1)S(1)}, bf16[32,16,128]{2,1,0:T(8,128)(2,1)S(1)}, u32[]{:S(2)}, u32[]{:S(2)}) collective-permute-start(bf16[32,16,128]{2,1,0:T(8,128)(2,1)S(1)} %get-tuple-element.16.refs_0_), channel_id=1, source_target_pairs={{4,0},{8,4},{12,8},{14,12},{10,14},{6,10},{2,6},{0,2},{5,1},{9,5},... | collective-permute-start | bytes 393224 | tf_op jit(solution)/shard_map/ppermute | solution.py:261
  3.5 5.9 %collective-permute-start.12 = (bf16[32,16,128]{2,1,0:T(8,128)(2,1)S(1)}, bf16[32,16,128]{2,1,0:T(8,128)(2,1)S(1)}, u32[]{:S(2)}, u32[]{:S(2)}) collective-permute-start(bf16[32,16,128]{2,1,0:T(8,128)(2,1)S(1)} %get-tuple-element.16.refs_0_), channel_id=1, source_target_pairs={{0,4},{4,8},{8,12},{12,14},{14,10},{10,6},{6,2},{2,0},{1,5},{5,9},... | collective-permute-start | bytes 393224 | tf_op jit(solution)/shard_map/ppermute | solution.py:258
  5.0 5.7 %collective-permute-start.9 = (bf16[32,16,128]{2,1,0:T(8,128)(2,1)S(1)}, bf16[32,16,128]{2,1,0:T(8,128)(2,1)S(1)}, u32[]{:S(2)}, u32[]{:S(2)}) collective-permute-start(bf16[32,16,128]{2,1,0:T(8,128)(2,1)S(1)} %get-tuple-element.15.refs_0_), channel_id=1, source_target_pairs={{4,0},{8,4},{12,8},{14,12},{10,14},{6,10},{2,6},{0,2},{5,1},{9,5},... | collective-permute-start | bytes 393224 | tf_op jit(solution)/shard_map/ppermute | solution.py:261
  6.7 5.0 %collective-permute-start.1 = (bf16[32,16,128]{2,1,0:T(8,128)(2,1)S(1)}, bf16[32,16,128]{2,1,0:T(8,128)(2,1)S(1)}, u32[]{:S(2)}, u32[]{:S(2)}) collective-permute-start(bf16[32,16,128]{2,1,0:T(8,128)(2,1)S(1)} %collective-permute-done.refs_1_), channel_id=1, source_target_pairs={{0,4},{4,8},{8,12},{12,14},{14,10},{10,6},{6,2},{2,0},{1,5},{5,9},... | collective-permute-start | bytes 393224 | tf_op jit(solution)/shard_map/ppermute | solution.py:258
  7.9 5.4 %collective-permute-start.5 = (bf16[32,16,128]{2,1,0:T(8,128)(2,1)S(1)}, bf16[32,16,128]{2,1,0:T(8,128)(2,1)S(1)}, u32[]{:S(2)}, u32[]{:S(2)}) collective-permute-start(bf16[32,16,128]{2,1,0:T(8,128)(2,1)S(1)} %collective-permute-done.4.refs_2_), channel_id=1, source_target_pairs={{4,0},{8,4},{12,8},{14,12},{10,14},{6,10},{2,6},{0,2},{5,1},{9,5},... | collective-permute-start | bytes 393224 | tf_op jit(solution)/shard_map/ppermute | solution.py:261
  9.5 5.3 %collective-permute-start.13 = (bf16[32,16,128]{2,1,0:T(8,128)(2,1)S(1)}, bf16[32,16,128]{2,1,0:T(8,128)(2,1)S(1)}, u32[]{:S(2)}, u32[]{:S(2)}) collective-permute-start(bf16[32,16,128]{2,1,0:T(8,128)(2,1)S(1)} %collective-permute-done.12.refs_1_), channel_id=1, source_target_pairs={{0,4},{4,8},{8,12},{12,14},{14,10},{10,6},{6,2},{2,0},{1,5},{5,9},... | collective-permute-start | bytes 393224 | tf_op jit(solution)/shard_map/ppermute | solution.py:258
  10.7 5.5 %collective-permute-start.10 = (bf16[32,16,128]{2,1,0:T(8,128)(2,1)S(1)}, bf16[32,16,128]{2,1,0:T(8,128)(2,1)S(1)}, u32[]{:S(2)}, u32[]{:S(2)}) collective-permute-start(bf16[32,16,128]{2,1,0:T(8,128)(2,1)S(1)} %collective-permute-done.9.refs_2_), channel_id=1, source_target_pairs={{4,0},{8,4},{12,8},{14,12},{10,14},{6,10},{2,6},{0,2},{5,1},{9,5},... | collective-permute-start | bytes 393224 | tf_op jit(solution)/shard_map/ppermute | solution.py:261
  11.7 5.8 %collective-permute-start.2 = (bf16[32,16,128]{2,1,0:T(8,128)(2,1)S(1)}, bf16[32,16,128]{2,1,0:T(8,128)(2,1)S(1)}, u32[]{:S(2)}, u32[]{:S(2)}) collective-permute-start(bf16[32,16,128]{2,1,0:T(8,128)(2,1)S(1)} %collective-permute-done.1.refs_3_), channel_id=1, source_target_pairs={{0,4},{4,8},{8,12},{12,14},{14,10},{10,6},{6,2},{2,0},{1,5},{5,9},... | collective-permute-start | bytes 393224 | tf_op jit(solution)/shard_map/ppermute | solution.py:258
  13.3 5.5 %collective-permute-start.6 = (bf16[32,16,128]{2,1,0:T(8,128)(2,1)S(1)}, bf16[32,16,128]{2,1,0:T(8,128)(2,1)S(1)}, u32[]{:S(2)}, u32[]{:S(2)}) collective-permute-start(bf16[32,16,128]{2,1,0:T(8,128)(2,1)S(1)} %collective-permute-done.5.refs_4_), channel_id=1, source_target_pairs={{4,0},{8,4},{12,8},{14,12},{10,14},{6,10},{2,6},{0,2},{5,1},{9,5},... | collective-permute-start | bytes 393224 | tf_op jit(solution)/shard_map/ppermute | solution.py:261
  14.7 4.8 %collective-permute-start.14 = (bf16[32,16,128]{2,1,0:T(8,128)(2,1)S(1)}, bf16[32,16,128]{2,1,0:T(8,128)(2,1)S(1)}, u32[]{:S(2)}, u32[]{:S(2)}) collective-permute-start(bf16[32,16,128]{2,1,0:T(8,128)(2,1)S(1)} %collective-permute-done.13.refs_3_), channel_id=1, source_target_pairs={{0,4},{4,8},{8,12},{12,14},{14,10},{10,6},{6,2},{2,0},{1,5},{5,9},... | collective-permute-start | bytes 393224 | tf_op jit(solution)/shard_map/ppermute | solution.py:258
  16.2 5.3 %collective-permute-start.11 = (bf16[32,16,128]{2,1,0:T(8,128)(2,1)S(1)}, bf16[32,16,128]{2,1,0:T(8,128)(2,1)S(1)}, u32[]{:S(2)}, u32[]{:S(2)}) collective-permute-start(bf16[32,16,128]{2,1,0:T(8,128)(2,1)S(1)} %collective-permute-done.10.refs_4_), channel_id=1, source_target_pairs={{4,0},{8,4},{12,8},{14,12},{10,14},{6,10},{2,6},{0,2},{5,1},{9,5},... | collective-permute-start | bytes 393224 | tf_op jit(solution)/shard_map/ppermute | solution.py:261
  17.5 10.2 %collective-permute-start.3 = (bf16[32,16,128]{2,1,0:T(8,128)(2,1)S(1)}, bf16[32,16,128]{2,1,0:T(8,128)(2,1)S(1)}, u32[]{:S(2)}, u32[]{:S(2)}) collective-permute-start(bf16[32,16,128]{2,1,0:T(8,128)(2,1)S(1)} %collective-permute-done.2.refs_5_), channel_id=1, source_target_pairs={{0,4},{4,8},{8,12},{12,14},{14,10},{10,6},{6,2},{2,0},{1,5},{5,9},... | collective-permute-start | bytes 393224 | tf_op jit(solution)/shard_map/ppermute | solution.py:258
  18.7 9.0 %collective-permute-start.7 = (bf16[32,16,128]{2,1,0:T(8,128)(2,1)S(1)}, bf16[32,16,128]{2,1,0:T(8,128)(2,1)S(1)}, u32[]{:S(2)}, u32[]{:S(2)}) collective-permute-start(bf16[32,16,128]{2,1,0:T(8,128)(2,1)S(1)} %collective-permute-done.6.refs_6_), channel_id=1, source_target_pairs={{4,0},{8,4},{12,8},{14,12},{10,14},{6,10},{2,6},{0,2},{5,1},{9,5},... | collective-permute-start | bytes 393224 | tf_op jit(solution)/shard_map/ppermute | solution.py:261
  23.6 5.6 %collective-permute-start.15 = (f32[72,1152]{1,0:T(8,128)S(1)}, f32[72,1152]{1,0:T(8,128)S(1)}, u32[]{:S(2)}, u32[]{:S(2)}) collective-permute-start(f32[72,1152]{1,0:T(8,128)S(1)} %get-tuple-element.22), channel_id=1, source_target_pairs={{0,1},{1,0},{2,3},{3,2},{4,5},{5,4},{6,7},{7,6},{8,9},{9,8},{10,11... | collective-permute-start | bytes 995336 | tf_op jit(solution)/shard_map/ppermute | solution.py:211
  28.9 1.3 %collective-permute-start.8 = (f32[16,1152]{1,0:T(8,128)S(1)}, f32[16,1152]{1,0:T(8,128)S(1)}, u32[]{:S(2)}, u32[]{:S(2)}) collective-permute-start(f32[16,1152]{1,0:T(8,128)S(1)} %last.1.own_ref), channel_id=1, source_target_pairs={{0,1},{1,0},{2,3},{3,2},{4,5},{5,4},{6,7},{7,6},{8,9},{9,8},{10,11... | collective-permute-start | bytes 221192 | tf_op jit(solution)/shard_map/ppermute | solution.py:211

commit v4 on v3

--- a/solution.py
+++ b/solution.py
@@ -11,34 +11,47 @@
 LANES = 128
 GROUP = 16
 VMEM = pl.BlockSpec(memory_space=pltpu.VMEM)
+HBM = pl.BlockSpec(memory_space=pltpu.HBM)
 ANY = pl.BlockSpec(memory_space=pl.ANY)
 PARAMS = pltpu.CompilerParams(vmem_limit_bytes=16 * 1024 * 1024)
 LONG = pl.CostEstimate(flops=10**10, bytes_accessed=4 * 1024 * 1024, transcendentals=0)
 
 
 def place_of(index, count):
-    return jnp.where(index % 2 == 0, index // 2, count - (index + 1) // 2)
+    return lax.rem(count - jnp.where(index % 2 == 0, index // 2, count - (index + 1) // 2), count)
 
 
 def index_at(place, count):
-    place = lax.rem(place + count, count)
+    place = lax.rem(2 * count - place, count)
     return jnp.where(place < count // 2, 2 * place, 2 * (count - place) - 1)
 
 
-def query_kernel(modules, pairs, x_ref, *chunks):
+def query_kernel(modules, pairs, x_ref, *refs):
+    chunks, rows, sems = refs[:-2], refs[-2], refs[-1]
     queries = chunks[0].shape[1]
     own = pairs // len(chunks)
+    span = own * modules
+    copies = [
+        pltpu.make_async_copy(x_ref.at[:, pl.ds(c * span, span), :], rows.at[c], sems.at[c])
+        for c in range(len(chunks))
+    ]
+    for copy in copies:
+        copy.start()
     for c, o_ref in enumerate(chunks):
+        copies[c].wait()
+        flat = rows.at[c].reshape(queries * span, LANES)
         for m in range(modules):
             for i in range(own):
-                at = (c * own + i) * modules + m
-                rows = x_ref[pl.ds(at, queries, stride=pairs * modules), :]
-                o_ref[m * own + i] = rows.astype(jnp.bfloat16)
-
-
-def token_kernel(modules, rank, x_ref, w_ref, a_ref, b_ref, n_ref, wide):
+                got = flat[pl.ds(i * modules + m, queries, stride=span), :]
+                o_ref[m * own + i] = got.astype(jnp.bfloat16)
+
+
+def token_kernel(modules, rank, x_ref, w_ref, a_ref, b_ref, n_ref, rows, wide, sem):
     tokens = x_ref.shape[0] // modules
-    wide[...] = x_ref[...].astype(jnp.float32)
+    copy = pltpu.make_async_copy(x_ref, rows, sem)
+    copy.start()
+    copy.wait()
+    wide[...] = rows[...].astype(jnp.float32)
     norm = jnp.zeros((1, tokens), jnp.float32)
     for m in range(modules):
         turned = wide[pl.ds(m, tokens, stride=modules), :].T
@@ -70,54 +83,56 @@
     tokens = w_ref.shape[2]
     own = rank // 2 // parts
     step = min(8, own)
-    tile = 512 if tokens % 512 == 0 else tokens
     o_ref[:, tokens:] = lane_squares(chunks)
-    for t in range(0, tokens, tile):
-        acc = jnp.zeros((GROUP, tile), jnp.float32)
+    for lanes in tiles(tokens):
+        acc = jnp.zeros((GROUP, lanes.stop - lanes.start), jnp.float32)
         for m in range(modules):
             for odd in range(2):
-                w = w_ref[m, odd * rank : (odd + 2) * rank, t : t + tile]
-                for c, chunk in enumerate(chunks):
+                w = w_ref[m, odd * rank : (odd + 2) * rank, lanes]
+                for part, chunk in enumerate(chunks):
                     for i in range(0, own, step):
                         k = m * own + i
                         left = chunk[k : k + step].reshape(step * GROUP, LANES)
                         inner = jnp.dot(left, w, preferred_element_type=jnp.float32)
                         for s in range(step):
-                            row = 2 * (c * own + i + s) + odd
-                            acc += inner[s * GROUP : (s + 1) * GROUP] * a_ref[m, row : row + 1, t : t + tile]
-        o_ref[:, t : t + tile] = acc
+                            row = 2 * (part * own + i + s) + odd
+                            acc += inner[s * GROUP : (s + 1) * GROUP] * a_ref[m, row : row + 1, lanes]
+        o_ref[:, lanes] = acc
 
 
 def products(blocks, part, parts, modules, rank, w_ref, b_ref, lanes):
     own = rank // 2 // parts
-    acc = jnp.zeros((len(blocks) * GROUP, lanes.size), jnp.float32)
+    step = min(4, own)
+    acc = jnp.zeros((len(blocks) * GROUP, lanes.stop - lanes.start), jnp.float32)
     for m in range(modules):
         grad = w_ref[m, :rank, lanes]
-        for i in range(0, own, 2):
+        for i in range(0, own, step):
             k = m * own + i
             row = 2 * (part * own + i)
             left = jnp.concatenate(
-                [jnp.concatenate([block[k + s] for block in blocks], axis=0) for s in range(2)],
+                [jnp.concatenate([block[k + s] for block in blocks], axis=0) for s in range(step)],
                 axis=1,
             )
             right = jnp.concatenate(
-                [grad * b_ref[m, row + s : row + s + 1, lanes] for s in range(4)], axis=0
+                [grad * b_ref[m, row + s : row + s + 1, lanes] for s in range(2 * step)], axis=0
             )
             acc += jnp.dot(left, right, preferred_element_type=jnp.float32)
     return acc
+
+
+def tiles(tokens):
+    size = 512 if tokens % 512 == 0 else tokens
+    return [slice(t, t + size) for t in range(0, tokens, size)]
 
 
 def early_kernel(count, parts, modules, rank, *refs):
     blocks = refs[:count]
     w_ref, b_ref, o_ref = refs[count:]
     tokens = w_ref.shape[2]
-    tile = 256 if tokens % 256 == 0 else tokens
     for b in range(count):
         o_ref[b * GROUP : (b + 1) * GROUP, tokens:] = lane_squares(blocks[b : b + 1])
 
-    @pl.loop(0, tokens // tile)
-    def _(t):
-        lanes = pl.ds(pl.multiple_of(t * tile, tile), tile)
+    for lanes in tiles(tokens):
         o_ref[:, lanes] = products(blocks, parts - 1, parts, modules, rank, w_ref, b_ref, lanes)
 
 
@@ -125,16 +140,13 @@
     blocks = refs[:count]
     w_ref, b_ref, n_ref, sum_ref, keep_ref, send_ref, both = refs[count:]
     tokens = w_ref.shape[2]
-    tile = 256 if tokens % 256 == 0 else tokens
     half = keep_ref.shape[0] // GROUP
     send_ref[half * GROUP :, :tokens] = n_ref[...]
     for b in range(count):
         span = slice(b * GROUP, (b + 1) * GROUP)
         both[span, tokens:] = sum_ref[span, tokens:] + lane_squares(blocks[b : b + 1])
 
-    @pl.loop(0, tokens // tile)
-    def _(t):
-        lanes = pl.ds(pl.multiple_of(t * tile, tile), tile)
+    for lanes in tiles(tokens):
         both[:, lanes] = sum_ref[:, lanes] + products(
             blocks, 0, parts, modules, rank, w_ref, b_ref, lanes
         )
@@ -200,12 +212,16 @@
             jax.ShapeDtypeStruct((modules, rank, tokens), jnp.bfloat16),
             jax.ShapeDtypeStruct((8, tokens), jnp.float32),
         ),
-        in_specs=[VMEM],
+        in_specs=[HBM],
         out_specs=(VMEM,) * 4,
-        scratch_shapes=[pltpu.VMEM((tokens * modules, doubled), jnp.float32)],
+        scratch_shapes=[
+            pltpu.VMEM((tokens * modules, doubled), jnp.bfloat16),
+            pltpu.VMEM((tokens * modules, doubled), jnp.float32),
+            pltpu.SemaphoreType.DMA,
+        ],
         compiler_params=PARAMS,
         name="tokens",
-    )(token_rows)
+    )(pltpu.with_memory_space_constraint(token_rows, pltpu.HBM))
 
     def swapped(x):
         return lax.ppermute(x, "proj", [(i, (i + 1) % proj) for i in range(proj)])
@@ -251,6 +267,7 @@
 
     if queries == GROUP and ex % 2 == 0 and ex <= 16:
         order = list(range(0, ex, 2)) + list(range(ex - 1, 0, -2))
+        order = order[:1] + order[:0:-1]
         up_pairs = [(order[i], order[(i + 1) % ex]) for i in range(ex)]
         down_pairs = [(b, a) for a, b in up_pairs]
 
@@ -261,21 +278,28 @@
             return lax.ppermute(x, "ex", down_pairs)
 
         rows = query_grads.reshape(queries, modules, pairs, LANES)
-        rows = rows.transpose(0, 2, 1, 3).reshape(queries * pairs * modules, LANES)
+        rows = rows.transpose(0, 2, 1, 3).reshape(queries, pairs * modules, LANES)
         chunk = jax.ShapeDtypeStruct((modules * pairs // 2, queries, LANES), jnp.bfloat16)
         block = pl.pallas_call(
             functools.partial(query_kernel, modules, pairs),
             out_shape=(chunk, chunk),
-            in_specs=[VMEM],
+            in_specs=[HBM],
             out_specs=(VMEM, VMEM),
+            scratch_shapes=[
+                pltpu.VMEM((2, queries, pairs * modules // 2, LANES), jnp.float32),
+                pltpu.SemaphoreType.DMA((2,)),
+            ],
             compiler_params=PARAMS,
             name="queries",
-        )(rows)
+        )(pltpu.with_memory_space_constraint(rows, pltpu.HBM))
         below, above = block, block
         blocks, steps = [block], [0]
         for step in range(1, ex // 2):
             first = (up(below[0]), down(above[0]))
             second = (up(below[1]), down(above[1]))
+            if step == 1:
+                arrived, weights = lax.optimization_barrier((first[0], weights))
+                first = (arrived, first[1])
             below, above = (first[0], second[0]), (first[1], second[1])
             blocks += [below, above]
             steps += [-step, step]
@@ -291,9 +315,9 @@
         keep, send = bulk(blocks, ring)
         out, scale = most(keep, swapped(send))
         mine = pl.pallas_call(
-            functools.partial(last_kernel, 2, modules, rank),
+            functools.partial(last_kernel, len(across), modules, rank),
             out_shape=jax.ShapeDtypeStruct((GROUP, wide), jnp.float32),
-            in_specs=[VMEM] * 4,
+            in_specs=[VMEM] * (len(across) + 2),
             out_specs=VMEM,
             compiler_params=PARAMS,
             cost_estimate=LONG,

time: 31.2 us -> 30.8 us (0.987)
  waiting for transfers between devices: 6.95 us -> 5.48 us
  starting transfers between devices: 15.6 us -> 16.7 us
  local copies, waits for them, and re-layouts: 1.04 us -> 0 us
  Pallas kernels: 7.38 us -> 8.37 us
    ppermute x7, waiting for transfers between devices: 6.62 us -> 5.35 us  [up(): return lax.ppermute(x, 'ex', up_pairs)]
    ppermute x7, starting transfers between devices: 1.22 us -> 2.45 us  [down(): return lax.ppermute(x, 'ex', down_pairs)]
    pallas_call x1, Pallas kernels: 0.27 us -> 1.43 us  [local(): pl.pallas_call(functools.partial(token_kernel, modules, rank), out_shape=...]
    unnamed x4 -> x0, local copies, waits for them, and re-layouts: 1.04 us -> none
    ppermute x7, starting transfers between devices: 10 us -> 9.01 us  [up(): return lax.ppermute(x, 'ex', up_pairs)]
    ppermute x2, starting transfers between devices: 4.31 us -> 5.29 us  [swapped(): return lax.ppermute(x, 'proj', [(i, (i + 1) % proj) for i in range(proj)])]
    pallas_call x1, Pallas kernels: 0.29 us -> 1.26 us  [local(): pl.pallas_call(functools.partial(query_kernel, modules, pairs), out_shape...]
    pallas_call x1, Pallas kernels: 2.11 us -> 1.5 us  [bulk(): pl.pallas_call(functools.partial(late_kernel, count, parts, modules, rank...]
where the time goes in v4:
time: 30.8 us; the launch traced here: 30.6 us
  starting transfers between devices  16.7 us (54%)
  Pallas kernels  8.37 us (27%)
  waiting for transfers between devices  5.48 us (18%)
    ppermute x7, starting transfers between devices, up(): return lax.ppermute(x, 'ex', up_pairs)  9.01 us
    ppermute x7, waiting for transfers between devices, up(): return lax.ppermute(x, 'ex', up_pairs)  5.35 us
    ppermute x2, starting transfers between devices, swapped(): return lax.ppermute(x, 'proj', [(i, (i + 1) % proj) for i in range(proj)])  5.29 us
    ppermute x7, starting transfers between devices, down(): return lax.ppermute(x, 'ex', down_pairs)  2.45 us
    pallas_call x1, Pallas kernels, bulk(): pl.pallas_call(functools.partial(late_kernel, count, parts, modules, rank...  1.5 us
    pallas_call x1, Pallas kernels, local(): pl.pallas_call(functools.partial(token_kernel, modules, rank), out_shape=...  1.43 us
    pallas_call x1, Pallas kernels, bulk(): pl.pallas_call(functools.partial(early_kernel, count, parts, modules, ran...  1.37 us
    pallas_call x1, Pallas kernels, local(): pl.pallas_call(functools.partial(query_kernel, modules, pairs), out_shape...  1.26 us
  transfers between devices with their start and end apart: 16, of which 7 were waited for; matrix products, arithmetic and copies ran while one was open for 0% of the time, Pallas kernels for 21%

profile of v4, /device:TPU:1, one launch (start us, length us, event | category | flops | bytes accessed | tf_op | source)
XLA Modules:
  0.0 30.6 jit_solution(12438941600037429166)
XLA Ops:
  0.0 1.3 %queries.1 = (bf16[32,16,128]{2,1,0:T(8,128)(2,1)S(1)}, bf16[32,16,128]{2,1,0:T(8,128)(2,1)S(1)}) custom-call(f32[16,64,128]{2,1,0:T(8,128)} %bitcast.7), custom_call_target="tpu_custom_call" | custom-call | tf_op jit(solution)/shard_map/queries/pallas_call | solution.py:283
  1.3 2.1 %collective-permute-start = (bf16[32,16,128]{2,1,0:T(8,128)(2,1)S(1)}, bf16[32,16,128]{2,1,0:T(8,128)(2,1)S(1)}, u32[]{:S(2)}, u32[]{:S(2)}) collective-permute-start(bf16[32,16,128]{2,1,0:T(8,128)(2,1)S(1)} %get-tuple-element.17.refs_0_), channel_id=1, source_target_pairs={{0,2},{2,6},{6,10},{10,14},{14,12},{12,8},{8,4},{4,0},{1,3},{3,7},... | collective-permute-start | bytes 393224 | tf_op jit(solution)/shard_map/ppermute | solution.py:275
  3.4 0.2 collective-permute-start.4
  3.5 1.3 %collective-permute-start.12 = (bf16[32,16,128]{2,1,0:T(8,128)(2,1)S(1)}, bf16[32,16,128]{2,1,0:T(8,128)(2,1)S(1)}, u32[]{:S(2)}, u32[]{:S(2)}) collective-permute-start(bf16[32,16,128]{2,1,0:T(8,128)(2,1)S(1)} %get-tuple-element.20.refs_0_), channel_id=1, source_target_pairs={{0,2},{2,6},{6,10},{10,14},{14,12},{12,8},{8,4},{4,0},{1,3},{3,7},... | collective-permute-start | bytes 393224 | tf_op jit(solution)/shard_map/ppermute | solution.py:275
  4.8 0.2 collective-permute-start.9
  5.0 1.4 %tokens.1 = (bf16[2,192,1024]{2,1,0:T(8,128)(2,1)S(1)}, f32[2,64,1024]{2,1,0:T(8,128)S(1)}, bf16[2,64,1024]{2,1,0:T(8,128)(2,1)S(1)}, f32[8,1024]{1,0:T(8,128)S(1)}) custom-call(bf16[2048,128]{1,0:T(8,128)(2,1)} %bitcast.8), custom_call_target="tpu_custom_call" | custom-call | tf_op jit(solution)/shard_map/tokens/pallas_call | solution.py:207
  6.4 0.3 collective-permute-done.refs_1_
  6.7 1.1 %collective-permute-start.1 = (bf16[32,16,128]{2,1,0:T(8,128)(2,1)S(1)}, bf16[32,16,128]{2,1,0:T(8,128)(2,1)S(1)}, u32[]{:S(2)}, u32[]{:S(2)}) collective-permute-start(bf16[32,16,128]{2,1,0:T(8,128)(2,1)S(1)} %collective-permute-done.refs_1_), channel_id=1, source_target_pairs={{0,2},{2,6},{6,10},{10,14},{14,12},{12,8},{8,4},{4,0},{1,3},{3,7},... | collective-permute-start | bytes 393224 | tf_op jit(solution)/shard_map/ppermute | solution.py:275
  7.8 0.0 collective-permute-done.4.refs_2_
  7.8 0.3 %collective-permute-start.5 = (bf16[32,16,128]{2,1,0:T(8,128)(2,1)S(1)}, bf16[32,16,128]{2,1,0:T(8,128)(2,1)S(1)}, u32[]{:S(2)}, u32[]{:S(2)}) collective-permute-start(bf16[32,16,128]{2,1,0:T(8,128)(2,1)S(1)} %collective-permute-done.4.refs_2_), channel_id=1, source_target_pairs={{2,0},{6,2},{10,6},{14,10},{12,14},{8,12},{4,8},{0,4},{3,1},{7,3},... | collective-permute-start | bytes 393224 | tf_op jit(solution)/shard_map/ppermute | solution.py:278
  8.1 1.3 %collective-permute-done.12.refs_1_ = bf16[32,16,128]{2,1,0:T(8,128)(2,1)S(1)} collective-permute-done((bf16[32,16,128]{2,1,0:T(8,128)(2,1)S(1)}, bf16[32,16,128]{2,1,0:T(8,128)(2,1)S(1)}, u32[]{:S(2)}, u32[]{:S(2)}) %collective-permute-start.12) | collective-permute-done | bytes 131104 | tf_op jit(solution)/shard_map/ppermute | solution.py:275
  9.5 1.1 %collective-permute-start.13 = (bf16[32,16,128]{2,1,0:T(8,128)(2,1)S(1)}, bf16[32,16,128]{2,1,0:T(8,128)(2,1)S(1)}, u32[]{:S(2)}, u32[]{:S(2)}) collective-permute-start(bf16[32,16,128]{2,1,0:T(8,128)(2,1)S(1)} %collective-permute-done.12.refs_1_), channel_id=1, source_target_pairs={{0,2},{2,6},{6,10},{10,14},{14,12},{12,8},{8,4},{4,0},{1,3},{3,7},... | collective-permute-start | bytes 393224 | tf_op jit(solution)/shard_map/ppermute | solution.py:275
  10.5 0.0 collective-permute-done.9.refs_2_
  10.5 0.4 %collective-permute-start.10 = (bf16[32,16,128]{2,1,0:T(8,128)(2,1)S(1)}, bf16[32,16,128]{2,1,0:T(8,128)(2,1)S(1)}, u32[]{:S(2)}, u32[]{:S(2)}) collective-permute-start(bf16[32,16,128]{2,1,0:T(8,128)(2,1)S(1)} %collective-permute-done.9.refs_2_), channel_id=1, source_target_pairs={{2,0},{6,2},{10,6},{14,10},{12,14},{8,12},{4,8},{0,4},{3,1},{7,3},... | collective-permute-start | bytes 393224 | tf_op jit(solution)/shard_map/ppermute | solution.py:278
  11.0 0.8 %collective-permute-done.1.refs_3_ = bf16[32,16,128]{2,1,0:T(8,128)(2,1)S(1)} collective-permute-done((bf16[32,16,128]{2,1,0:T(8,128)(2,1)S(1)}, bf16[32,16,128]{2,1,0:T(8,128)(2,1)S(1)}, u32[]{:S(2)}, u32[]{:S(2)}) %collective-permute-start.1) | collective-permute-done | bytes 131104 | tf_op jit(solution)/shard_map/ppermute | solution.py:275
  11.7 1.4 %collective-permute-start.2 = (bf16[32,16,128]{2,1,0:T(8,128)(2,1)S(1)}, bf16[32,16,128]{2,1,0:T(8,128)(2,1)S(1)}, u32[]{:S(2)}, u32[]{:S(2)}) collective-permute-start(bf16[32,16,128]{2,1,0:T(8,128)(2,1)S(1)} %collective-permute-done.1.refs_3_), channel_id=1, source_target_pairs={{0,2},{2,6},{6,10},{10,14},{14,12},{12,8},{8,4},{4,0},{1,3},{3,7},... | collective-permute-start | bytes 393224 | tf_op jit(solution)/shard_map/ppermute | solution.py:275
  13.1 0.0 collective-permute-done.5.refs_4_
  13.1 0.1 collective-permute-start.6
  13.2 1.6 %collective-permute-done.13.refs_3_ = bf16[32,16,128]{2,1,0:T(8,128)(2,1)S(1)} collective-permute-done((bf16[32,16,128]{2,1,0:T(8,128)(2,1)S(1)}, bf16[32,16,128]{2,1,0:T(8,128)(2,1)S(1)}, u32[]{:S(2)}, u32[]{:S(2)}) %collective-permute-start.13) | collective-permute-done | bytes 131104 | tf_op jit(solution)/shard_map/ppermute | solution.py:275
  14.7 1.0 %collective-permute-start.14 = (bf16[32,16,128]{2,1,0:T(8,128)(2,1)S(1)}, bf16[32,16,128]{2,1,0:T(8,128)(2,1)S(1)}, u32[]{:S(2)}, u32[]{:S(2)}) collective-permute-start(bf16[32,16,128]{2,1,0:T(8,128)(2,1)S(1)} %collective-permute-done.13.refs_3_), channel_id=1, source_target_pairs={{0,2},{2,6},{6,10},{10,14},{14,12},{12,8},{8,4},{4,0},{1,3},{3,7},... | collective-permute-start | bytes 393224 | tf_op jit(solution)/shard_map/ppermute | solution.py:275
  15.7 0.0 collective-permute-done.10.refs_4_
  15.7 0.7 %collective-permute-start.11 = (bf16[32,16,128]{2,1,0:T(8,128)(2,1)S(1)}, bf16[32,16,128]{2,1,0:T(8,128)(2,1)S(1)}, u32[]{:S(2)}, u32[]{:S(2)}) collective-permute-start(bf16[32,16,128]{2,1,0:T(8,128)(2,1)S(1)} %collective-permute-done.10.refs_4_), channel_id=1, source_target_pairs={{2,0},{6,2},{10,6},{14,10},{12,14},{8,12},{4,8},{0,4},{3,1},{7,3},... | collective-permute-start | bytes 393224 | tf_op jit(solution)/shard_map/ppermute | solution.py:278
  16.4 1.1 %collective-permute-done.2.refs_5_ = bf16[32,16,128]{2,1,0:T(8,128)(2,1)S(1)} collective-permute-done((bf16[32,16,128]{2,1,0:T(8,128)(2,1)S(1)}, bf16[32,16,128]{2,1,0:T(8,128)(2,1)S(1)}, u32[]{:S(2)}, u32[]{:S(2)}) %collective-permute-start.2) | collective-permute-done | bytes 131104 | tf_op jit(solution)/shard_map/ppermute | solution.py:275
  17.5 1.1 %collective-permute-start.3 = (bf16[32,16,128]{2,1,0:T(8,128)(2,1)S(1)}, bf16[32,16,128]{2,1,0:T(8,128)(2,1)S(1)}, u32[]{:S(2)}, u32[]{:S(2)}) collective-permute-start(bf16[32,16,128]{2,1,0:T(8,128)(2,1)S(1)} %collective-permute-done.2.refs_5_), channel_id=1, source_target_pairs={{0,2},{2,6},{6,10},{10,14},{14,12},{12,8},{8,4},{4,0},{1,3},{3,7},... | collective-permute-start | bytes 393224 | tf_op jit(solution)/shard_map/ppermute | solution.py:275
  18.6 0.0 collective-permute-done.6.refs_6_
  18.6 0.6 %collective-permute-start.7 = (bf16[32,16,128]{2,1,0:T(8,128)(2,1)S(1)}, bf16[32,16,128]{2,1,0:T(8,128)(2,1)S(1)}, u32[]{:S(2)}, u32[]{:S(2)}) collective-permute-start(bf16[32,16,128]{2,1,0:T(8,128)(2,1)S(1)} %collective-permute-done.6.refs_6_), channel_id=1, source_target_pairs={{2,0},{6,2},{10,6},{14,10},{12,14},{8,12},{4,8},{0,4},{3,1},{7,3},... | collective-permute-start | bytes 393224 | tf_op jit(solution)/shard_map/ppermute | solution.py:278
  19.2 0.3 %collective-permute-done.14.refs_5_ = bf16[32,16,128]{2,1,0:T(8,128)(2,1)S(1)} collective-permute-done((bf16[32,16,128]{2,1,0:T(8,128)(2,1)S(1)}, bf16[32,16,128]{2,1,0:T(8,128)(2,1)S(1)}, u32[]{:S(2)}, u32[]{:S(2)}) %collective-permute-start.14) | collective-permute-done | bytes 131104 | tf_op jit(solution)/shard_map/ppermute | solution.py:275
  19.5 1.4 %early.1.refs_10_ = f32[112,1152]{1,0:T(8,128)S(1)} custom-call(bf16[32,16,128]{2,1,0:T(8,128)(2,1)S(1)} %get-tuple-element.20.refs_0_, bf16[32,16,128]{2,1,0:T(8,128)(2,1)S(1)} %collective-permute-done.12.refs_1_, bf16[32,16,128]{2,1,0:T(8,128)(2,1)S(1)} %collective-permute-done.4.refs_2_, bf16[32,16,128]{2,1,0:T(8,128)(2,1)S(1)} %collective-permute-done.13.refs_3_, ...), custom_call_target="tpu_custom_call" | custom-call | flops 10000000000 | bytes 4194304 | tf_op jit(solution)/shard_map/early/pallas_call | solution.py:231
  20.9 0.0 collective-permute-done.11.refs_6_
  20.9 1.5 %late.1 = (f32[64,1152]{1,0:T(8,128)S(1)}, f32[72,1152]{1,0:T(8,128)S(1)}) custom-call(bf16[32,16,128]{2,1,0:T(8,128)(2,1)S(1)} %get-tuple-element.17.refs_0_, bf16[32,16,128]{2,1,0:T(8,128)(2,1)S(1)} %collective-permute-done.refs_1_, bf16[32,16,128]{2,1,0:T(8,128)(2,1)S(1)} %collective-permute-done.9.refs_2_, ...), custom_call_target="tpu_custom_call" | custom-call | flops 10000000000 | bytes 4194304 | tf_op jit(solution)/shard_map/late/pallas_call | solution.py:240
  22.4 4.1 %collective-permute-start.15 = (f32[72,1152]{1,0:T(8,128)S(1)}, f32[72,1152]{1,0:T(8,128)S(1)}, u32[]{:S(2)}, u32[]{:S(2)}) collective-permute-start(f32[72,1152]{1,0:T(8,128)S(1)} %get-tuple-element.26), channel_id=1, source_target_pairs={{0,1},{1,0},{2,3},{3,2},{4,5},{5,4},{6,7},{7,6},{8,9},{9,8},{10,11... | collective-permute-start | bytes 995336 | tf_op jit(solution)/shard_map/ppermute | solution.py:227
  26.5 0.0 collective-permute-done.3.refs_0_
  26.5 0.0 collective-permute-done.7.refs_1_
  26.5 1.3 %last.1.own_ref = f32[16,1152]{1,0:T(8,128)S(1)} custom-call(bf16[32,16,128]{2,1,0:T(8,128)(2,1)S(1)} %collective-permute-done.3.refs_0_, bf16[32,16,128]{2,1,0:T(8,128)(2,1)S(1)} %collective-permute-done.7.refs_1_, bf16[2,192,1024]{2,1,0:T(8,128)(2,1)S(1)} %get-tuple-element.21.refs_2_.refs_7_, f32[2,64,1024]{2,1,0:T(8,128)S(1)} %get-tuple-element.22.refs_3_), custom_call_target="tpu_custom_call" | custom-call | flops 10000000000 | bytes 4194304 | tf_op jit(solution)/shard_map/last/pallas_call | solution.py:317
  27.8 1.2 %collective-permute-start.8 = (f32[16,1152]{1,0:T(8,128)S(1)}, f32[16,1152]{1,0:T(8,128)S(1)}, u32[]{:S(2)}, u32[]{:S(2)}) collective-permute-start(f32[16,1152]{1,0:T(8,128)S(1)} %last.1.own_ref), channel_id=1, source_target_pairs={{0,1},{1,0},{2,3},{3,2},{4,5},{5,4},{6,7},{7,6},{8,9},{9,8},{10,11... | collective-permute-start | bytes 221192 | tf_op jit(solution)/shard_map/ppermute | solution.py:227
  29.0 0.0 collective-permute-done.15.far_ref
  29.0 0.8 %most.1 = (f32[64,1024]{1,0:T(8,128)}, f32[8,1024]{1,0:T(8,128)S(1)}) custom-call(f32[64,1152]{1,0:T(8,128)S(1)} %get-tuple-element.25.keep_ref, f32[72,1152]{1,0:T(8,128)S(1)} %collective-permute-done.15.far_ref, f32[8,1024]{1,0:T(8,128)S(1)} %get-tuple-element.24.refs_9_.n_ref), custom_call_target="tpu_custom_call" | custom-call | flops 10000000000 | bytes 4194304 | tf_op jit(solution)/shard_map/most/pallas_call | solution.py:255
  29.8 0.1 collective-permute-done.8.far_ref
  29.9 0.7 %rest.1 = f32[64,1024]{1,0:T(8,128)} custom-call(f32[16,1152]{1,0:T(8,128)S(1)} %last.1.own_ref, f32[16,1152]{1,0:T(8,128)S(1)} %collective-permute-done.8.far_ref, f32[8,1024]{1,0:T(8,128)S(1)} %get-tuple-element.27.s_ref, f32[64,1024]{1,0:T(8,128)} %get-tuple-element.28.most_ref), custom_call_target="tpu_custom_call", output_to_operand_aliasing={{}: (3, {})} | custom-call | tf_op jit(solution)/shard_map/rest/pallas_call | solution.py:326
Async XLA Ops:
  1.3 5.4 %collective-permute-start = (bf16[32,16,128]{2,1,0:T(8,128)(2,1)S(1)}, bf16[32,16,128]{2,1,0:T(8,128)(2,1)S(1)}, u32[]{:S(2)}, u32[]{:S(2)}) collective-permute-start(bf16[32,16,128]{2,1,0:T(8,128)(2,1)S(1)} %get-tuple-element.17.refs_0_), channel_id=1, source_target_pairs={{0,2},{2,6},{6,10},{10,14},{14,12},{12,8},{8,4},{4,0},{1,3},{3,7},... | collective-permute-start | bytes 393224 | tf_op jit(solution)/shard_map/ppermute | solution.py:275
  3.4 4.4 %collective-permute-start.4 = (bf16[32,16,128]{2,1,0:T(8,128)(2,1)S(1)}, bf16[32,16,128]{2,1,0:T(8,128)(2,1)S(1)}, u32[]{:S(2)}, u32[]{:S(2)}) collective-permute-start(bf16[32,16,128]{2,1,0:T(8,128)(2,1)S(1)} %get-tuple-element.20.refs_0_), channel_id=1, source_target_pairs={{2,0},{6,2},{10,6},{14,10},{12,14},{8,12},{4,8},{0,4},{3,1},{7,3},... | collective-permute-start | bytes 393224 | tf_op jit(solution)/shard_map/ppermute | solution.py:278
  3.5 6.0 %collective-permute-start.12 = (bf16[32,16,128]{2,1,0:T(8,128)(2,1)S(1)}, bf16[32,16,128]{2,1,0:T(8,128)(2,1)S(1)}, u32[]{:S(2)}, u32[]{:S(2)}) collective-permute-start(bf16[32,16,128]{2,1,0:T(8,128)(2,1)S(1)} %get-tuple-element.20.refs_0_), channel_id=1, source_target_pairs={{0,2},{2,6},{6,10},{10,14},{14,12},{12,8},{8,4},{4,0},{1,3},{3,7},... | collective-permute-start | bytes 393224 | tf_op jit(solution)/shard_map/ppermute | solution.py:275
  4.8 5.7 %collective-permute-start.9 = (bf16[32,16,128]{2,1,0:T(8,128)(2,1)S(1)}, bf16[32,16,128]{2,1,0:T(8,128)(2,1)S(1)}, u32[]{:S(2)}, u32[]{:S(2)}) collective-permute-start(bf16[32,16,128]{2,1,0:T(8,128)(2,1)S(1)} %get-tuple-element.17.refs_0_), channel_id=1, source_target_pairs={{2,0},{6,2},{10,6},{14,10},{12,14},{8,12},{4,8},{0,4},{3,1},{7,3},... | collective-permute-start | bytes 393224 | tf_op jit(solution)/shard_map/ppermute | solution.py:278
  6.7 5.0 %collective-permute-start.1 = (bf16[32,16,128]{2,1,0:T(8,128)(2,1)S(1)}, bf16[32,16,128]{2,1,0:T(8,128)(2,1)S(1)}, u32[]{:S(2)}, u32[]{:S(2)}) collective-permute-start(bf16[32,16,128]{2,1,0:T(8,128)(2,1)S(1)} %collective-permute-done.refs_1_), channel_id=1, source_target_pairs={{0,2},{2,6},{6,10},{10,14},{14,12},{12,8},{8,4},{4,0},{1,3},{3,7},... | collective-permute-start | bytes 393224 | tf_op jit(solution)/shard_map/ppermute | solution.py:275
  7.8 5.3 %collective-permute-start.5 = (bf16[32,16,128]{2,1,0:T(8,128)(2,1)S(1)}, bf16[32,16,128]{2,1,0:T(8,128)(2,1)S(1)}, u32[]{:S(2)}, u32[]{:S(2)}) collective-permute-start(bf16[32,16,128]{2,1,0:T(8,128)(2,1)S(1)} %collective-permute-done.4.refs_2_), channel_id=1, source_target_pairs={{2,0},{6,2},{10,6},{14,10},{12,14},{8,12},{4,8},{0,4},{3,1},{7,3},... | collective-permute-start | bytes 393224 | tf_op jit(solution)/shard_map/ppermute | solution.py:278
  9.5 5.3 %collective-permute-start.13 = (bf16[32,16,128]{2,1,0:T(8,128)(2,1)S(1)}, bf16[32,16,128]{2,1,0:T(8,128)(2,1)S(1)}, u32[]{:S(2)}, u32[]{:S(2)}) collective-permute-start(bf16[32,16,128]{2,1,0:T(8,128)(2,1)S(1)} %collective-permute-done.12.refs_1_), channel_id=1, source_target_pairs={{0,2},{2,6},{6,10},{10,14},{14,12},{12,8},{8,4},{4,0},{1,3},{3,7},... | collective-permute-start | bytes 393224 | tf_op jit(solution)/shard_map/ppermute | solution.py:275
  10.5 5.2 %collective-permute-start.10 = (bf16[32,16,128]{2,1,0:T(8,128)(2,1)S(1)}, bf16[32,16,128]{2,1,0:T(8,128)(2,1)S(1)}, u32[]{:S(2)}, u32[]{:S(2)}) collective-permute-start(bf16[32,16,128]{2,1,0:T(8,128)(2,1)S(1)} %collective-permute-done.9.refs_2_), channel_id=1, source_target_pairs={{2,0},{6,2},{10,6},{14,10},{12,14},{8,12},{4,8},{0,4},{3,1},{7,3},... | collective-permute-start | bytes 393224 | tf_op jit(solution)/shard_map/ppermute | solution.py:278
  11.7 5.8 %collective-permute-start.2 = (bf16[32,16,128]{2,1,0:T(8,128)(2,1)S(1)}, bf16[32,16,128]{2,1,0:T(8,128)(2,1)S(1)}, u32[]{:S(2)}, u32[]{:S(2)}) collective-permute-start(bf16[32,16,128]{2,1,0:T(8,128)(2,1)S(1)} %collective-permute-done.1.refs_3_), channel_id=1, source_target_pairs={{0,2},{2,6},{6,10},{10,14},{14,12},{12,8},{8,4},{4,0},{1,3},{3,7},... | collective-permute-start | bytes 393224 | tf_op jit(solution)/shard_map/ppermute | solution.py:275
  13.1 5.5 %collective-permute-start.6 = (bf16[32,16,128]{2,1,0:T(8,128)(2,1)S(1)}, bf16[32,16,128]{2,1,0:T(8,128)(2,1)S(1)}, u32[]{:S(2)}, u32[]{:S(2)}) collective-permute-start(bf16[32,16,128]{2,1,0:T(8,128)(2,1)S(1)} %collective-permute-done.5.refs_4_), channel_id=1, source_target_pairs={{2,0},{6,2},{10,6},{14,10},{12,14},{8,12},{4,8},{0,4},{3,1},{7,3},... | collective-permute-start | bytes 393224 | tf_op jit(solution)/shard_map/ppermute | solution.py:278
  14.7 4.8 %collective-permute-start.14 = (bf16[32,16,128]{2,1,0:T(8,128)(2,1)S(1)}, bf16[32,16,128]{2,1,0:T(8,128)(2,1)S(1)}, u32[]{:S(2)}, u32[]{:S(2)}) collective-permute-start(bf16[32,16,128]{2,1,0:T(8,128)(2,1)S(1)} %collective-permute-done.13.refs_3_), channel_id=1, source_target_pairs={{0,2},{2,6},{6,10},{10,14},{14,12},{12,8},{8,4},{4,0},{1,3},{3,7},... | collective-permute-start | bytes 393224 | tf_op jit(solution)/shard_map/ppermute | solution.py:275
  15.7 5.2 %collective-permute-start.11 = (bf16[32,16,128]{2,1,0:T(8,128)(2,1)S(1)}, bf16[32,16,128]{2,1,0:T(8,128)(2,1)S(1)}, u32[]{:S(2)}, u32[]{:S(2)}) collective-permute-start(bf16[32,16,128]{2,1,0:T(8,128)(2,1)S(1)} %collective-permute-done.10.refs_4_), channel_id=1, source_target_pairs={{2,0},{6,2},{10,6},{14,10},{12,14},{8,12},{4,8},{0,4},{3,1},{7,3},... | collective-permute-start | bytes 393224 | tf_op jit(solution)/shard_map/ppermute | solution.py:278
  17.5 9.1 %collective-permute-start.3 = (bf16[32,16,128]{2,1,0:T(8,128)(2,1)S(1)}, bf16[32,16,128]{2,1,0:T(8,128)(2,1)S(1)}, u32[]{:S(2)}, u32[]{:S(2)}) collective-permute-start(bf16[32,16,128]{2,1,0:T(8,128)(2,1)S(1)} %collective-permute-done.2.refs_5_), channel_id=1, source_target_pairs={{0,2},{2,6},{6,10},{10,14},{14,12},{12,8},{8,4},{4,0},{1,3},{3,7},... | collective-permute-start | bytes 393224 | tf_op jit(solution)/shard_map/ppermute | solution.py:275
  18.6 8.0 %collective-permute-start.7 = (bf16[32,16,128]{2,1,0:T(8,128)(2,1)S(1)}, bf16[32,16,128]{2,1,0:T(8,128)(2,1)S(1)}, u32[]{:S(2)}, u32[]{:S(2)}) collective-permute-start(bf16[32,16,128]{2,1,0:T(8,128)(2,1)S(1)} %collective-permute-done.6.refs_6_), channel_id=1, source_target_pairs={{2,0},{6,2},{10,6},{14,10},{12,14},{8,12},{4,8},{0,4},{3,1},{7,3},... | collective-permute-start | bytes 393224 | tf_op jit(solution)/shard_map/ppermute | solution.py:278
  22.4 6.6 %collective-permute-start.15 = (f32[72,1152]{1,0:T(8,128)S(1)}, f32[72,1152]{1,0:T(8,128)S(1)}, u32[]{:S(2)}, u32[]{:S(2)}) collective-permute-start(f32[72,1152]{1,0:T(8,128)S(1)} %get-tuple-element.26), channel_id=1, source_target_pairs={{0,1},{1,0},{2,3},{3,2},{4,5},{5,4},{6,7},{7,6},{8,9},{9,8},{10,11... | collective-permute-start | bytes 995336 | tf_op jit(solution)/shard_map/ppermute | solution.py:227
  27.8 2.1 %collective-permute-start.8 = (f32[16,1152]{1,0:T(8,128)S(1)}, f32[16,1152]{1,0:T(8,128)S(1)}, u32[]{:S(2)}, u32[]{:S(2)}) collective-permute-start(f32[16,1152]{1,0:T(8,128)S(1)} %last.1.own_ref), channel_id=1, source_target_pairs={{0,1},{1,0},{2,3},{3,2},{4,5},{5,4},{6,7},{7,6},{8,9},{9,8},{10,11... | collective-permute-start | bytes 221192 | tf_op jit(solution)/shard_map/ppermute | solution.py:227

commit v5 on v4

--- a/solution.py
+++ b/solution.py
@@ -12,6 +12,7 @@
 GROUP = 16
 VMEM = pl.BlockSpec(memory_space=pltpu.VMEM)
 HBM = pl.BlockSpec(memory_space=pltpu.HBM)
+COVER = pl.CostEstimate(flops=692100000, bytes_accessed=1024, transcendentals=0)
 ANY = pl.BlockSpec(memory_space=pl.ANY)
 PARAMS = pltpu.CompilerParams(vmem_limit_bytes=16 * 1024 * 1024)
 LONG = pl.CostEstimate(flops=10**10, bytes_accessed=4 * 1024 * 1024, transcendentals=0)
@@ -77,26 +78,25 @@
     return total
 
 
-def last_kernel(parts, modules, rank, *refs):
-    chunks = refs[:parts]
-    w_ref, a_ref, o_ref = refs[parts:]
+def last_kernel(part, parts, modules, rank, chunk, w_ref, a_ref, *refs):
+    before, o_ref = refs[:-1], refs[-1]
     tokens = w_ref.shape[2]
     own = rank // 2 // parts
     step = min(8, own)
-    o_ref[:, tokens:] = lane_squares(chunks)
+    squares = lane_squares([chunk])
+    o_ref[:, tokens:] = before[0][:, tokens:] + squares if before else squares
     for lanes in tiles(tokens):
-        acc = jnp.zeros((GROUP, lanes.stop - lanes.start), jnp.float32)
+        acc = before[0][:, lanes] if before else jnp.zeros((GROUP, lanes.stop - lanes.start), jnp.float32)
         for m in range(modules):
             for odd in range(2):
                 w = w_ref[m, odd * rank : (odd + 2) * rank, lanes]
-                for part, chunk in enumerate(chunks):
-                    for i in range(0, own, step):
-                        k = m * own + i
-                        left = chunk[k : k + step].reshape(step * GROUP, LANES)
-                        inner = jnp.dot(left, w, preferred_element_type=jnp.float32)
-                        for s in range(step):
-                            row = 2 * (part * own + i + s) + odd
-                            acc += inner[s * GROUP : (s + 1) * GROUP] * a_ref[m, row : row + 1, lanes]
+                for i in range(0, own, step):
+                    k = m * own + i
+                    left = chunk[k : k + step].reshape(step * GROUP, LANES)
+                    inner = jnp.dot(left, w, preferred_element_type=jnp.float32)
+                    for s in range(step):
+                        row = 2 * (part * own + i + s) + odd
+                        acc += inner[s * GROUP : (s + 1) * GROUP] * a_ref[m, row : row + 1, lanes]
         o_ref[:, lanes] = acc
 
 
@@ -234,7 +234,7 @@
             in_specs=[VMEM] * (count + 2),
             out_specs=VMEM,
             compiler_params=PARAMS,
-            cost_estimate=LONG,
+            cost_estimate=COVER,
             name="early",
         )(*[block[-1] for block in blocks], weights, narrow)
         return pl.pallas_call(
@@ -247,7 +247,7 @@
             out_specs=(VMEM, VMEM),
             scratch_shapes=[pltpu.VMEM((count * GROUP, wide), jnp.float32)],
             compiler_params=PARAMS,
-            cost_estimate=LONG,
+            cost_estimate=COVER,
             name="late",
         )(*[block[0] for block in blocks], weights, narrow, norm, early)
 
@@ -314,15 +314,20 @@
 
         keep, send = bulk(blocks, ring)
         out, scale = most(keep, swapped(send))
-        mine = pl.pallas_call(
-            functools.partial(last_kernel, len(across), modules, rank),
-            out_shape=jax.ShapeDtypeStruct((GROUP, wide), jnp.float32),
-            in_specs=[VMEM] * (len(across) + 2),
-            out_specs=VMEM,
-            compiler_params=PARAMS,
-            cost_estimate=LONG,
-            name="last",
-        )(*across, weights, acts)
+        mine = ()
+        for part, chunk in enumerate(across):
+            mine = (
+                pl.pallas_call(
+                    functools.partial(last_kernel, part, len(across), modules, rank),
+                    out_shape=jax.ShapeDtypeStruct((GROUP, wide), jnp.float32),
+                    in_specs=[VMEM] * (3 + len(mine)),
+                    out_specs=VMEM,
+                    compiler_params=PARAMS,
+                    cost_estimate=LONG if part else COVER,
+                    name="last",
+                )(chunk, weights, acts, *mine),
+            )
+        (mine,) = mine
         out = pl.pallas_call(
             functools.partial(rest_kernel, width, opposite),
             out_shape=jax.ShapeDtypeStruct((columns, tokens), jnp.float32),

time: 30.8 us -> 30.3 us (0.984)
  starting transfers between devices: 16.7 us -> 16 us
    ppermute x2, starting transfers between devices: 5.29 us -> 4.57 us  [swapped(): return lax.ppermute(x, 'proj', [(i, (i + 1) % proj) for i in range(proj)])]
    pallas_call x1 -> x2, Pallas kernels: 1.26 us -> 1.41 us  [local(): pl.pallas_call(functools.partial(last_kernel, part, len(across), modules,...]
  transfers between devices with their start and end apart: 16 -> 16, of which waited for: 7 -> 7; matrix products, arithmetic and copies ran while one was open for 0% -> 0% of each run, Pallas kernels for 21% -> 22%
where the time goes in v5:
time: 30.3 us; the launch traced here: 30.1 us
  starting transfers between devices  16 us (53%)
  Pallas kernels  8.52 us (28%)
  waiting for transfers between devices  5.48 us (18%)
    ppermute x7, starting transfers between devices, up(): return lax.ppermute(x, 'ex', up_pairs)  9.01 us
    ppermute x7, waiting for transfers between devices, up(): return lax.ppermute(x, 'ex', up_pairs)  5.35 us
    ppermute x2, starting transfers between devices, swapped(): return lax.ppermute(x, 'proj', [(i, (i + 1) % proj) for i in range(proj)])  4.57 us
    ppermute x7, starting transfers between devices, down(): return lax.ppermute(x, 'ex', down_pairs)  2.45 us
    pallas_call x1, Pallas kernels, bulk(): pl.pallas_call(functools.partial(late_kernel, count, parts, modules, rank...  1.5 us
    pallas_call x1, Pallas kernels, local(): pl.pallas_call(functools.partial(token_kernel, modules, rank), out_shape=...  1.43 us
    pallas_call x2, Pallas kernels, local(): pl.pallas_call(functools.partial(last_kernel, part, len(across), modules,...  1.41 us
    pallas_call x1, Pallas kernels, bulk(): pl.pallas_call(functools.partial(early_kernel, count, parts, modules, ran...  1.37 us
  transfers between devices with their start and end apart: 16, of which 7 were waited for; matrix products, arithmetic and copies ran while one was open for 0% of the time, Pallas kernels for 22%

profile of v5, /device:TPU:1, one launch (start us, length us, event | category | flops | bytes accessed | tf_op | source)
XLA Modules:
  0.0 30.1 jit_solution(12281734574153699236)
XLA Ops:
  0.0 1.3 %queries.1 = (bf16[32,16,128]{2,1,0:T(8,128)(2,1)S(1)}, bf16[32,16,128]{2,1,0:T(8,128)(2,1)S(1)}) custom-call(f32[16,64,128]{2,1,0:T(8,128)} %bitcast.7), custom_call_target="tpu_custom_call" | custom-call | tf_op jit(solution)/shard_map/queries/pallas_call | solution.py:283
  1.3 2.1 %collective-permute-start.4 = (bf16[32,16,128]{2,1,0:T(8,128)(2,1)S(1)}, bf16[32,16,128]{2,1,0:T(8,128)(2,1)S(1)}, u32[]{:S(2)}, u32[]{:S(2)}) collective-permute-start(bf16[32,16,128]{2,1,0:T(8,128)(2,1)S(1)} %get-tuple-element.18.refs_0_), channel_id=1, source_target_pairs={{0,2},{2,6},{6,10},{10,14},{14,12},{12,8},{8,4},{4,0},{1,3},{3,7},... | collective-permute-start | bytes 393224 | tf_op jit(solution)/shard_map/ppermute | solution.py:275
  3.4 0.2 collective-permute-start
  3.5 1.3 %collective-permute-start.12 = (bf16[32,16,128]{2,1,0:T(8,128)(2,1)S(1)}, bf16[32,16,128]{2,1,0:T(8,128)(2,1)S(1)}, u32[]{:S(2)}, u32[]{:S(2)}) collective-permute-start(bf16[32,16,128]{2,1,0:T(8,128)(2,1)S(1)} %get-tuple-element.17.refs_0_), channel_id=1, source_target_pairs={{0,2},{2,6},{6,10},{10,14},{14,12},{12,8},{8,4},{4,0},{1,3},{3,7},... | collective-permute-start | bytes 393224 | tf_op jit(solution)/shard_map/ppermute | solution.py:275
  4.8 0.2 collective-permute-start.9
  5.0 1.4 %tokens.1 = (bf16[2,192,1024]{2,1,0:T(8,128)(2,1)S(1)}, f32[2,64,1024]{2,1,0:T(8,128)S(1)}, bf16[2,64,1024]{2,1,0:T(8,128)(2,1)S(1)}, f32[8,1024]{1,0:T(8,128)S(1)}) custom-call(bf16[2048,128]{1,0:T(8,128)(2,1)} %bitcast.8), custom_call_target="tpu_custom_call" | custom-call | tf_op jit(solution)/shard_map/tokens/pallas_call | solution.py:207
  6.4 0.3 collective-permute-done.4.refs_1_
  6.7 1.1 %collective-permute-start.5 = (bf16[32,16,128]{2,1,0:T(8,128)(2,1)S(1)}, bf16[32,16,128]{2,1,0:T(8,128)(2,1)S(1)}, u32[]{:S(2)}, u32[]{:S(2)}) collective-permute-start(bf16[32,16,128]{2,1,0:T(8,128)(2,1)S(1)} %collective-permute-done.4.refs_1_), channel_id=1, source_target_pairs={{0,2},{2,6},{6,10},{10,14},{14,12},{12,8},{8,4},{4,0},{1,3},{3,7},... | collective-permute-start | bytes 393224 | tf_op jit(solution)/shard_map/ppermute | solution.py:275
  7.8 0.0 collective-permute-done.refs_2_
  7.8 0.3 %collective-permute-start.1 = (bf16[32,16,128]{2,1,0:T(8,128)(2,1)S(1)}, bf16[32,16,128]{2,1,0:T(8,128)(2,1)S(1)}, u32[]{:S(2)}, u32[]{:S(2)}) collective-permute-start(bf16[32,16,128]{2,1,0:T(8,128)(2,1)S(1)} %collective-permute-done.refs_2_), channel_id=1, source_target_pairs={{2,0},{6,2},{10,6},{14,10},{12,14},{8,12},{4,8},{0,4},{3,1},{7,3},... | collective-permute-start | bytes 393224 | tf_op jit(solution)/shard_map/ppermute | solution.py:278
  8.1 1.3 %collective-permute-done.12.refs_1_ = bf16[32,16,128]{2,1,0:T(8,128)(2,1)S(1)} collective-permute-done((bf16[32,16,128]{2,1,0:T(8,128)(2,1)S(1)}, bf16[32,16,128]{2,1,0:T(8,128)(2,1)S(1)}, u32[]{:S(2)}, u32[]{:S(2)}) %collective-permute-start.12) | collective-permute-done | bytes 131104 | tf_op jit(solution)/shard_map/ppermute | solution.py:275
  9.5 1.1 %collective-permute-start.13 = (bf16[32,16,128]{2,1,0:T(8,128)(2,1)S(1)}, bf16[32,16,128]{2,1,0:T(8,128)(2,1)S(1)}, u32[]{:S(2)}, u32[]{:S(2)}) collective-permute-start(bf16[32,16,128]{2,1,0:T(8,128)(2,1)S(1)} %collective-permute-done.12.refs_1_), channel_id=1, source_target_pairs={{0,2},{2,6},{6,10},{10,14},{14,12},{12,8},{8,4},{4,0},{1,3},{3,7},... | collective-permute-start | bytes 393224 | tf_op jit(solution)/shard_map/ppermute | solution.py:275
  10.5 0.0 collective-permute-done.9.refs_2_
  10.5 0.4 %collective-permute-start.10 = (bf16[32,16,128]{2,1,0:T(8,128)(2,1)S(1)}, bf16[32,16,128]{2,1,0:T(8,128)(2,1)S(1)}, u32[]{:S(2)}, u32[]{:S(2)}) collective-permute-start(bf16[32,16,128]{2,1,0:T(8,128)(2,1)S(1)} %collective-permute-done.9.refs_2_), channel_id=1, source_target_pairs={{2,0},{6,2},{10,6},{14,10},{12,14},{8,12},{4,8},{0,4},{3,1},{7,3},... | collective-permute-start | bytes 393224 | tf_op jit(solution)/shard_map/ppermute | solution.py:278
  11.0 0.8 %collective-permute-done.5.refs_3_ = bf16[32,16,128]{2,1,0:T(8,128)(2,1)S(1)} collective-permute-done((bf16[32,16,128]{2,1,0:T(8,128)(2,1)S(1)}, bf16[32,16,128]{2,1,0:T(8,128)(2,1)S(1)}, u32[]{:S(2)}, u32[]{:S(2)}) %collective-permute-start.5) | collective-permute-done | bytes 131104 | tf_op jit(solution)/shard_map/ppermute | solution.py:275
  11.7 1.4 %collective-permute-start.6 = (bf16[32,16,128]{2,1,0:T(8,128)(2,1)S(1)}, bf16[32,16,128]{2,1,0:T(8,128)(2,1)S(1)}, u32[]{:S(2)}, u32[]{:S(2)}) collective-permute-start(bf16[32,16,128]{2,1,0:T(8,128)(2,1)S(1)} %collective-permute-done.5.refs_3_), channel_id=1, source_target_pairs={{0,2},{2,6},{6,10},{10,14},{14,12},{12,8},{8,4},{4,0},{1,3},{3,7},... | collective-permute-start | bytes 393224 | tf_op jit(solution)/shard_map/ppermute | solution.py:275
  13.1 0.0 collective-permute-done.1.refs_4_
  13.1 0.1 collective-permute-start.2
  13.2 1.6 %collective-permute-done.13.refs_3_ = bf16[32,16,128]{2,1,0:T(8,128)(2,1)S(1)} collective-permute-done((bf16[32,16,128]{2,1,0:T(8,128)(2,1)S(1)}, bf16[32,16,128]{2,1,0:T(8,128)(2,1)S(1)}, u32[]{:S(2)}, u32[]{:S(2)}) %collective-permute-start.13) | collective-permute-done | bytes 131104 | tf_op jit(solution)/shard_map/ppermute | solution.py:275
  14.7 1.0 %collective-permute-start.14 = (bf16[32,16,128]{2,1,0:T(8,128)(2,1)S(1)}, bf16[32,16,128]{2,1,0:T(8,128)(2,1)S(1)}, u32[]{:S(2)}, u32[]{:S(2)}) collective-permute-start(bf16[32,16,128]{2,1,0:T(8,128)(2,1)S(1)} %collective-permute-done.13.refs_3_), channel_id=1, source_target_pairs={{0,2},{2,6},{6,10},{10,14},{14,12},{12,8},{8,4},{4,0},{1,3},{3,7},... | collective-permute-start | bytes 393224 | tf_op jit(solution)/shard_map/ppermute | solution.py:275
  15.7 0.0 collective-permute-done.10.refs_4_
  15.7 0.7 %collective-permute-start.11 = (bf16[32,16,128]{2,1,0:T(8,128)(2,1)S(1)}, bf16[32,16,128]{2,1,0:T(8,128)(2,1)S(1)}, u32[]{:S(2)}, u32[]{:S(2)}) collective-permute-start(bf16[32,16,128]{2,1,0:T(8,128)(2,1)S(1)} %collective-permute-done.10.refs_4_), channel_id=1, source_target_pairs={{2,0},{6,2},{10,6},{14,10},{12,14},{8,12},{4,8},{0,4},{3,1},{7,3},... | collective-permute-start | bytes 393224 | tf_op jit(solution)/shard_map/ppermute | solution.py:278
  16.4 1.1 %collective-permute-done.6.refs_5_ = bf16[32,16,128]{2,1,0:T(8,128)(2,1)S(1)} collective-permute-done((bf16[32,16,128]{2,1,0:T(8,128)(2,1)S(1)}, bf16[32,16,128]{2,1,0:T(8,128)(2,1)S(1)}, u32[]{:S(2)}, u32[]{:S(2)}) %collective-permute-start.6) | collective-permute-done | bytes 131104 | tf_op jit(solution)/shard_map/ppermute | solution.py:275
  17.5 1.1 %collective-permute-start.7 = (bf16[32,16,128]{2,1,0:T(8,128)(2,1)S(1)}, bf16[32,16,128]{2,1,0:T(8,128)(2,1)S(1)}, u32[]{:S(2)}, u32[]{:S(2)}) collective-permute-start(bf16[32,16,128]{2,1,0:T(8,128)(2,1)S(1)} %collective-permute-done.6.refs_5_), channel_id=1, source_target_pairs={{0,2},{2,6},{6,10},{10,14},{14,12},{12,8},{8,4},{4,0},{1,3},{3,7},... | collective-permute-start | bytes 393224 | tf_op jit(solution)/shard_map/ppermute | solution.py:275
  18.6 0.0 collective-permute-done.2.refs_6_
  18.6 0.6 %collective-permute-start.3 = (bf16[32,16,128]{2,1,0:T(8,128)(2,1)S(1)}, bf16[32,16,128]{2,1,0:T(8,128)(2,1)S(1)}, u32[]{:S(2)}, u32[]{:S(2)}) collective-permute-start(bf16[32,16,128]{2,1,0:T(8,128)(2,1)S(1)} %collective-permute-done.2.refs_6_), channel_id=1, source_target_pairs={{2,0},{6,2},{10,6},{14,10},{12,14},{8,12},{4,8},{0,4},{3,1},{7,3},... | collective-permute-start | bytes 393224 | tf_op jit(solution)/shard_map/ppermute | solution.py:278
  19.2 0.3 %collective-permute-done.14.refs_5_ = bf16[32,16,128]{2,1,0:T(8,128)(2,1)S(1)} collective-permute-done((bf16[32,16,128]{2,1,0:T(8,128)(2,1)S(1)}, bf16[32,16,128]{2,1,0:T(8,128)(2,1)S(1)}, u32[]{:S(2)}, u32[]{:S(2)}) %collective-permute-start.14) | collective-permute-done | bytes 131104 | tf_op jit(solution)/shard_map/ppermute | solution.py:275
  19.5 1.4 %early.1.refs_10_ = f32[112,1152]{1,0:T(8,128)S(1)} custom-call(bf16[32,16,128]{2,1,0:T(8,128)(2,1)S(1)} %get-tuple-element.17.refs_0_, bf16[32,16,128]{2,1,0:T(8,128)(2,1)S(1)} %collective-permute-done.12.refs_1_, bf16[32,16,128]{2,1,0:T(8,128)(2,1)S(1)} %collective-permute-done.refs_2_, bf16[32,16,128]{2,1,0:T(8,128)(2,1)S(1)} %collective-permute-done.13.refs_3_, ...), custom_call_target="tpu_custom_call" | custom-call | flops 692099968 | bytes 1024 | tf_op jit(solution)/shard_map/early/pallas_call | solution.py:231
  20.9 0.0 collective-permute-done.11.refs_6_
  20.9 1.5 %late.1 = (f32[64,1152]{1,0:T(8,128)S(1)}, f32[72,1152]{1,0:T(8,128)S(1)}) custom-call(bf16[32,16,128]{2,1,0:T(8,128)(2,1)S(1)} %get-tuple-element.18.refs_0_, bf16[32,16,128]{2,1,0:T(8,128)(2,1)S(1)} %collective-permute-done.4.refs_1_, bf16[32,16,128]{2,1,0:T(8,128)(2,1)S(1)} %collective-permute-done.9.refs_2_, ...), custom_call_target="tpu_custom_call" | custom-call | flops 692099968 | bytes 1024 | tf_op jit(solution)/shard_map/late/pallas_call | solution.py:240
  22.4 4.1 %collective-permute-start.15 = (f32[72,1152]{1,0:T(8,128)S(1)}, f32[72,1152]{1,0:T(8,128)S(1)}, u32[]{:S(2)}, u32[]{:S(2)}) collective-permute-start(f32[72,1152]{1,0:T(8,128)S(1)} %get-tuple-element.26), channel_id=1, source_target_pairs={{0,1},{1,0},{2,3},{3,2},{4,5},{5,4},{6,7},{7,6},{8,9},{9,8},{10,11... | collective-permute-start | bytes 995336 | tf_op jit(solution)/shard_map/ppermute | solution.py:227
  26.5 0.0 collective-permute-done.7.chunk
  26.5 0.7 %last.2.refs_0_ = f32[16,1152]{1,0:T(8,128)S(1)} custom-call(bf16[32,16,128]{2,1,0:T(8,128)(2,1)S(1)} %collective-permute-done.7.chunk, bf16[2,192,1024]{2,1,0:T(8,128)(2,1)S(1)} %get-tuple-element.20.w_ref.refs_7_, f32[2,64,1024]{2,1,0:T(8,128)S(1)} %get-tuple-element.21.a_ref), custom_call_target="tpu_custom_call" | custom-call | flops 692099968 | bytes 1024 | tf_op jit(solution)/shard_map/last/pallas_call | solution.py:320
  27.2 0.0 collective-permute-done.3.chunk
  27.3 0.7 %last.3.own_ref = f32[16,1152]{1,0:T(8,128)S(1)} custom-call(bf16[32,16,128]{2,1,0:T(8,128)(2,1)S(1)} %collective-permute-done.3.chunk, bf16[2,192,1024]{2,1,0:T(8,128)(2,1)S(1)} %get-tuple-element.20.w_ref.refs_7_, f32[2,64,1024]{2,1,0:T(8,128)S(1)} %get-tuple-element.21.a_ref, f32[16,1152]{1,0:T(8,128)S(1)} %last.2.refs_0_), custom_call_target="tpu_custom_call" | custom-call | flops 10000000000 | bytes 4194304 | tf_op jit(solution)/shard_map/last/pallas_call | solution.py:320
  28.0 0.5 %collective-permute-start.8 = (f32[16,1152]{1,0:T(8,128)S(1)}, f32[16,1152]{1,0:T(8,128)S(1)}, u32[]{:S(2)}, u32[]{:S(2)}) collective-permute-start(f32[16,1152]{1,0:T(8,128)S(1)} %last.3.own_ref), channel_id=1, source_target_pairs={{0,1},{1,0},{2,3},{3,2},{4,5},{5,4},{6,7},{7,6},{8,9},{9,8},{10,11... | collective-permute-start | bytes 221192 | tf_op jit(solution)/shard_map/ppermute | solution.py:227
  28.4 0.0 collective-permute-done.15.far_ref
  28.4 0.8 %most.1 = (f32[64,1024]{1,0:T(8,128)}, f32[8,1024]{1,0:T(8,128)S(1)}) custom-call(f32[64,1152]{1,0:T(8,128)S(1)} %get-tuple-element.25.keep_ref, f32[72,1152]{1,0:T(8,128)S(1)} %collective-permute-done.15.far_ref, f32[8,1024]{1,0:T(8,128)S(1)} %get-tuple-element.24.refs_9_.n_ref), custom_call_target="tpu_custom_call" | custom-call | flops 10000000000 | bytes 4194304 | tf_op jit(solution)/shard_map/most/pallas_call | solution.py:255
  29.3 0.1 collective-permute-done.8.far_ref
  29.4 0.7 %rest.1 = f32[64,1024]{1,0:T(8,128)} custom-call(f32[16,1152]{1,0:T(8,128)S(1)} %last.3.own_ref, f32[16,1152]{1,0:T(8,128)S(1)} %collective-permute-done.8.far_ref, f32[8,1024]{1,0:T(8,128)S(1)} %get-tuple-element.27.s_ref, f32[64,1024]{1,0:T(8,128)} %get-tuple-element.28.most_ref), custom_call_target="tpu_custom_call", output_to_operand_aliasing={{}: (3, {})} | custom-call | tf_op jit(solution)/shard_map/rest/pallas_call | solution.py:331
Async XLA Ops:
  1.3 5.4 %collective-permute-start.4 = (bf16[32,16,128]{2,1,0:T(8,128)(2,1)S(1)}, bf16[32,16,128]{2,1,0:T(8,128)(2,1)S(1)}, u32[]{:S(2)}, u32[]{:S(2)}) collective-permute-start(bf16[32,16,128]{2,1,0:T(8,128)(2,1)S(1)} %get-tuple-element.18.refs_0_), channel_id=1, source_target_pairs={{0,2},{2,6},{6,10},{10,14},{14,12},{12,8},{8,4},{4,0},{1,3},{3,7},... | collective-permute-start | bytes 393224 | tf_op jit(solution)/shard_map/ppermute | solution.py:275
  3.4 4.4 %collective-permute-start = (bf16[32,16,128]{2,1,0:T(8,128)(2,1)S(1)}, bf16[32,16,128]{2,1,0:T(8,128)(2,1)S(1)}, u32[]{:S(2)}, u32[]{:S(2)}) collective-permute-start(bf16[32,16,128]{2,1,0:T(8,128)(2,1)S(1)} %get-tuple-element.17.refs_0_), channel_id=1, source_target_pairs={{2,0},{6,2},{10,6},{14,10},{12,14},{8,12},{4,8},{0,4},{3,1},{7,3},... | collective-permute-start | bytes 393224 | tf_op jit(solution)/shard_map/ppermute | solution.py:278
  3.5 6.0 %collective-permute-start.12 = (bf16[32,16,128]{2,1,0:T(8,128)(2,1)S(1)}, bf16[32,16,128]{2,1,0:T(8,128)(2,1)S(1)}, u32[]{:S(2)}, u32[]{:S(2)}) collective-permute-start(bf16[32,16,128]{2,1,0:T(8,128)(2,1)S(1)} %get-tuple-element.17.refs_0_), channel_id=1, source_target_pairs={{0,2},{2,6},{6,10},{10,14},{14,12},{12,8},{8,4},{4,0},{1,3},{3,7},... | collective-permute-start | bytes 393224 | tf_op jit(solution)/shard_map/ppermute | solution.py:275
  4.8 5.7 %collective-permute-start.9 = (bf16[32,16,128]{2,1,0:T(8,128)(2,1)S(1)}, bf16[32,16,128]{2,1,0:T(8,128)(2,1)S(1)}, u32[]{:S(2)}, u32[]{:S(2)}) collective-permute-start(bf16[32,16,128]{2,1,0:T(8,128)(2,1)S(1)} %get-tuple-element.18.refs_0_), channel_id=1, source_target_pairs={{2,0},{6,2},{10,6},{14,10},{12,14},{8,12},{4,8},{0,4},{3,1},{7,3},... | collective-permute-start | bytes 393224 | tf_op jit(solution)/shard_map/ppermute | solution.py:278
  6.7 5.0 %collective-permute-start.5 = (bf16[32,16,128]{2,1,0:T(8,128)(2,1)S(1)}, bf16[32,16,128]{2,1,0:T(8,128)(2,1)S(1)}, u32[]{:S(2)}, u32[]{:S(2)}) collective-permute-start(bf16[32,16,128]{2,1,0:T(8,128)(2,1)S(1)} %collective-permute-done.4.refs_1_), channel_id=1, source_target_pairs={{0,2},{2,6},{6,10},{10,14},{14,12},{12,8},{8,4},{4,0},{1,3},{3,7},... | collective-permute-start | bytes 393224 | tf_op jit(solution)/shard_map/ppermute | solution.py:275
  7.8 5.3 %collective-permute-start.1 = (bf16[32,16,128]{2,1,0:T(8,128)(2,1)S(1)}, bf16[32,16,128]{2,1,0:T(8,128)(2,1)S(1)}, u32[]{:S(2)}, u32[]{:S(2)}) collective-permute-start(bf16[32,16,128]{2,1,0:T(8,128)(2,1)S(1)} %collective-permute-done.refs_2_), channel_id=1, source_target_pairs={{2,0},{6,2},{10,6},{14,10},{12,14},{8,12},{4,8},{0,4},{3,1},{7,3},... | collective-permute-start | bytes 393224 | tf_op jit(solution)/shard_map/ppermute | solution.py:278
  9.5 5.3 %collective-permute-start.13 = (bf16[32,16,128]{2,1,0:T(8,128)(2,1)S(1)}, bf16[32,16,128]{2,1,0:T(8,128)(2,1)S(1)}, u32[]{:S(2)}, u32[]{:S(2)}) collective-permute-start(bf16[32,16,128]{2,1,0:T(8,128)(2,1)S(1)} %collective-permute-done.12.refs_1_), channel_id=1, source_target_pairs={{0,2},{2,6},{6,10},{10,14},{14,12},{12,8},{8,4},{4,0},{1,3},{3,7},... | collective-permute-start | bytes 393224 | tf_op jit(solution)/shard_map/ppermute | solution.py:275
  10.5 5.2 %collective-permute-start.10 = (bf16[32,16,128]{2,1,0:T(8,128)(2,1)S(1)}, bf16[32,16,128]{2,1,0:T(8,128)(2,1)S(1)}, u32[]{:S(2)}, u32[]{:S(2)}) collective-permute-start(bf16[32,16,128]{2,1,0:T(8,128)(2,1)S(1)} %collective-permute-done.9.refs_2_), channel_id=1, source_target_pairs={{2,0},{6,2},{10,6},{14,10},{12,14},{8,12},{4,8},{0,4},{3,1},{7,3},... | collective-permute-start | bytes 393224 | tf_op jit(solution)/shard_map/ppermute | solution.py:278
  11.7 5.8 %collective-permute-start.6 = (bf16[32,16,128]{2,1,0:T(8,128)(2,1)S(1)}, bf16[32,16,128]{2,1,0:T(8,128)(2,1)S(1)}, u32[]{:S(2)}, u32[]{:S(2)}) collective-permute-start(bf16[32,16,128]{2,1,0:T(8,128)(2,1)S(1)} %collective-permute-done.5.refs_3_), channel_id=1, source_target_pairs={{0,2},{2,6},{6,10},{10,14},{14,12},{12,8},{8,4},{4,0},{1,3},{3,7},... | collective-permute-start | bytes 393224 | tf_op jit(solution)/shard_map/ppermute | solution.py:275
  13.1 5.5 %collective-permute-start.2 = (bf16[32,16,128]{2,1,0:T(8,128)(2,1)S(1)}, bf16[32,16,128]{2,1,0:T(8,128)(2,1)S(1)}, u32[]{:S(2)}, u32[]{:S(2)}) collective-permute-start(bf16[32,16,128]{2,1,0:T(8,128)(2,1)S(1)} %collective-permute-done.1.refs_4_), channel_id=1, source_target_pairs={{2,0},{6,2},{10,6},{14,10},{12,14},{8,12},{4,8},{0,4},{3,1},{7,3},... | collective-permute-start | bytes 393224 | tf_op jit(solution)/shard_map/ppermute | solution.py:278
  14.7 4.8 %collective-permute-start.14 = (bf16[32,16,128]{2,1,0:T(8,128)(2,1)S(1)}, bf16[32,16,128]{2,1,0:T(8,128)(2,1)S(1)}, u32[]{:S(2)}, u32[]{:S(2)}) collective-permute-start(bf16[32,16,128]{2,1,0:T(8,128)(2,1)S(1)} %collective-permute-done.13.refs_3_), channel_id=1, source_target_pairs={{0,2},{2,6},{6,10},{10,14},{14,12},{12,8},{8,4},{4,0},{1,3},{3,7},... | collective-permute-start | bytes 393224 | tf_op jit(solution)/shard_map/ppermute | solution.py:275
  15.7 5.2 %collective-permute-start.11 = (bf16[32,16,128]{2,1,0:T(8,128)(2,1)S(1)}, bf16[32,16,128]{2,1,0:T(8,128)(2,1)S(1)}, u32[]{:S(2)}, u32[]{:S(2)}) collective-permute-start(bf16[32,16,128]{2,1,0:T(8,128)(2,1)S(1)} %collective-permute-done.10.refs_4_), channel_id=1, source_target_pairs={{2,0},{6,2},{10,6},{14,10},{12,14},{8,12},{4,8},{0,4},{3,1},{7,3},... | collective-permute-start | bytes 393224 | tf_op jit(solution)/shard_map/ppermute | solution.py:278
  17.5 9.1 %collective-permute-start.7 = (bf16[32,16,128]{2,1,0:T(8,128)(2,1)S(1)}, bf16[32,16,128]{2,1,0:T(8,128)(2,1)S(1)}, u32[]{:S(2)}, u32[]{:S(2)}) collective-permute-start(bf16[32,16,128]{2,1,0:T(8,128)(2,1)S(1)} %collective-permute-done.6.refs_5_), channel_id=1, source_target_pairs={{0,2},{2,6},{6,10},{10,14},{14,12},{12,8},{8,4},{4,0},{1,3},{3,7},... | collective-permute-start | bytes 393224 | tf_op jit(solution)/shard_map/ppermute | solution.py:275
  18.6 8.7 %collective-permute-start.3 = (bf16[32,16,128]{2,1,0:T(8,128)(2,1)S(1)}, bf16[32,16,128]{2,1,0:T(8,128)(2,1)S(1)}, u32[]{:S(2)}, u32[]{:S(2)}) collective-permute-start(bf16[32,16,128]{2,1,0:T(8,128)(2,1)S(1)} %collective-permute-done.2.refs_6_), channel_id=1, source_target_pairs={{2,0},{6,2},{10,6},{14,10},{12,14},{8,12},{4,8},{0,4},{3,1},{7,3},... | collective-permute-start | bytes 393224 | tf_op jit(solution)/shard_map/ppermute | solution.py:278
  22.4 6.0 %collective-permute-start.15 = (f32[72,1152]{1,0:T(8,128)S(1)}, f32[72,1152]{1,0:T(8,128)S(1)}, u32[]{:S(2)}, u32[]{:S(2)}) collective-permute-start(f32[72,1152]{1,0:T(8,128)S(1)} %get-tuple-element.26), channel_id=1, source_target_pairs={{0,1},{1,0},{2,3},{3,2},{4,5},{5,4},{6,7},{7,6},{8,9},{9,8},{10,11... | collective-permute-start | bytes 995336 | tf_op jit(solution)/shard_map/ppermute | solution.py:227
  28.0 1.4 %collective-permute-start.8 = (f32[16,1152]{1,0:T(8,128)S(1)}, f32[16,1152]{1,0:T(8,128)S(1)}, u32[]{:S(2)}, u32[]{:S(2)}) collective-permute-start(f32[16,1152]{1,0:T(8,128)S(1)} %last.3.own_ref), channel_id=1, source_target_pairs={{0,1},{1,0},{2,3},{3,2},{4,5},{5,4},{6,7},{7,6},{8,9},{9,8},{10,11... | collective-permute-start | bytes 221192 | tf_op jit(solution)/shard_map/ppermute | solution.py:227

commit v6 on v5

--- a/solution.py
+++ b/solution.py
@@ -47,7 +47,7 @@
                 o_ref[m * own + i] = got.astype(jnp.bfloat16)
 
 
-def token_kernel(modules, rank, x_ref, w_ref, a_ref, b_ref, n_ref, rows, wide, sem):
+def token_kernel(modules, rank, x_ref, p_ref, n_ref, rows, wide, sem):
     tokens = x_ref.shape[0] // modules
     copy = pltpu.make_async_copy(x_ref, rows, sem)
     copy.start()
@@ -60,12 +60,8 @@
         norm += jnp.sum(act * act, axis=0, keepdims=True) * jnp.sum(
             grad * grad, axis=0, keepdims=True
         )
-        grad = grad.astype(jnp.bfloat16)
-        w_ref[m, :rank] = grad
-        w_ref[m, rank : 2 * rank] = jnp.zeros_like(grad)
-        w_ref[m, 2 * rank :] = grad
-        a_ref[m] = act
-        b_ref[m] = act.astype(jnp.bfloat16)
+        p_ref[0, m] = act.astype(jnp.bfloat16)
+        p_ref[1, m] = grad.astype(jnp.bfloat16)
     n_ref[...] = jnp.broadcast_to(norm, n_ref.shape)
 
 
@@ -78,9 +74,9 @@
     return total
 
 
-def last_kernel(part, parts, modules, rank, chunk, w_ref, a_ref, *refs):
+def last_kernel(part, parts, modules, rank, chunk, p_ref, *refs):
     before, o_ref = refs[:-1], refs[-1]
-    tokens = w_ref.shape[2]
+    tokens = p_ref.shape[3]
     own = rank // 2 // parts
     step = min(8, own)
     squares = lane_squares([chunk])
@@ -88,24 +84,26 @@
     for lanes in tiles(tokens):
         acc = before[0][:, lanes] if before else jnp.zeros((GROUP, lanes.stop - lanes.start), jnp.float32)
         for m in range(modules):
+            act = p_ref[0, m, 2 * part * own : 2 * (part + 1) * own, lanes].astype(jnp.float32)
+            grad = p_ref[1, m, :, lanes]
             for odd in range(2):
-                w = w_ref[m, odd * rank : (odd + 2) * rank, lanes]
                 for i in range(0, own, step):
                     k = m * own + i
                     left = chunk[k : k + step].reshape(step * GROUP, LANES)
-                    inner = jnp.dot(left, w, preferred_element_type=jnp.float32)
+                    left = left[:, odd * rank : (odd + 1) * rank]
+                    inner = jnp.dot(left, grad, preferred_element_type=jnp.float32)
                     for s in range(step):
-                        row = 2 * (part * own + i + s) + odd
-                        acc += inner[s * GROUP : (s + 1) * GROUP] * a_ref[m, row : row + 1, lanes]
+                        row = 2 * (i + s) + odd
+                        acc += inner[s * GROUP : (s + 1) * GROUP] * act[row : row + 1]
         o_ref[:, lanes] = acc
 
 
-def products(blocks, part, parts, modules, rank, w_ref, b_ref, lanes):
+def products(blocks, part, parts, modules, rank, p_ref, lanes):
     own = rank // 2 // parts
     step = min(4, own)
     acc = jnp.zeros((len(blocks) * GROUP, lanes.stop - lanes.start), jnp.float32)
     for m in range(modules):
-        grad = w_ref[m, :rank, lanes]
+        grad = p_ref[1, m, :, lanes]
         for i in range(0, own, step):
             k = m * own + i
             row = 2 * (part * own + i)
@@ -114,7 +112,7 @@
                 axis=1,
             )
             right = jnp.concatenate(
-                [grad * b_ref[m, row + s : row + s + 1, lanes] for s in range(2 * step)], axis=0
+                [grad * p_ref[0, m, row + s : row + s + 1, lanes] for s in range(2 * step)], axis=0
             )
             acc += jnp.dot(left, right, preferred_element_type=jnp.float32)
     return acc
@@ -127,19 +125,19 @@
 
 def early_kernel(count, parts, modules, rank, *refs):
     blocks = refs[:count]
-    w_ref, b_ref, o_ref = refs[count:]
-    tokens = w_ref.shape[2]
+    p_ref, o_ref = refs[count:]
+    tokens = p_ref.shape[3]
     for b in range(count):
         o_ref[b * GROUP : (b + 1) * GROUP, tokens:] = lane_squares(blocks[b : b + 1])
 
     for lanes in tiles(tokens):
-        o_ref[:, lanes] = products(blocks, parts - 1, parts, modules, rank, w_ref, b_ref, lanes)
+        o_ref[:, lanes] = products(blocks, parts - 1, parts, modules, rank, p_ref, lanes)
 
 
 def late_kernel(count, parts, modules, rank, ring, *refs):
     blocks = refs[:count]
-    w_ref, b_ref, n_ref, sum_ref, keep_ref, send_ref, both = refs[count:]
-    tokens = w_ref.shape[2]
+    p_ref, n_ref, sum_ref, keep_ref, send_ref, both = refs[count:]
+    tokens = p_ref.shape[3]
     half = keep_ref.shape[0] // GROUP
     send_ref[half * GROUP :, :tokens] = n_ref[...]
     for b in range(count):
@@ -148,7 +146,7 @@
 
     for lanes in tiles(tokens):
         both[:, lanes] = sum_ref[:, lanes] + products(
-            blocks, 0, parts, modules, rank, w_ref, b_ref, lanes
+            blocks, 0, parts, modules, rank, p_ref, lanes
         )
 
     me = lax.axis_index("proj")
@@ -204,16 +202,14 @@
     columns = queries * ex // proj
 
     token_rows = train_factors.reshape(tokens * modules, doubled)
-    weights, acts, narrow, norm = pl.pallas_call(
+    factors, norm = pl.pallas_call(
         functools.partial(token_kernel, modules, rank),
         out_shape=(
-            jax.ShapeDtypeStruct((modules, 3 * rank, tokens), jnp.bfloat16),
-            jax.ShapeDtypeStruct((modules, rank, tokens), jnp.float32),
-            jax.ShapeDtypeStruct((modules, rank, tokens), jnp.bfloat16),
+            jax.ShapeDtypeStruct((2, modules, rank, tokens), jnp.bfloat16),
             jax.ShapeDtypeStruct((8, tokens), jnp.float32),
         ),
         in_specs=[HBM],
-        out_specs=(VMEM,) * 4,
+        out_specs=(VMEM, VMEM),
         scratch_shapes=[
             pltpu.VMEM((tokens * modules, doubled), jnp.bfloat16),
             pltpu.VMEM((tokens * modules, doubled), jnp.float32),
@@ -231,25 +227,25 @@
         early = pl.pallas_call(
             functools.partial(early_kernel, count, parts, modules, rank),
             out_shape=jax.ShapeDtypeStruct((count * GROUP, wide), jnp.float32),
-            in_specs=[VMEM] * (count + 2),
+            in_specs=[VMEM] * (count + 1),
             out_specs=VMEM,
             compiler_params=PARAMS,
             cost_estimate=COVER,
             name="early",
-        )(*[block[-1] for block in blocks], weights, narrow)
+        )(*[block[-1] for block in blocks], factors)
         return pl.pallas_call(
             functools.partial(late_kernel, count, parts, modules, rank, ring),
             out_shape=(
                 jax.ShapeDtypeStruct((columns, wide), jnp.float32),
                 jax.ShapeDtypeStruct((columns + 8, wide), jnp.float32),
             ),
-            in_specs=[VMEM] * (count + 4),
+            in_specs=[VMEM] * (count + 3),
             out_specs=(VMEM, VMEM),
             scratch_shapes=[pltpu.VMEM((count * GROUP, wide), jnp.float32)],
             compiler_params=PARAMS,
             cost_estimate=COVER,
             name="late",
-        )(*[block[0] for block in blocks], weights, narrow, norm, early)
+        )(*[block[0] for block in blocks], factors, norm, early)
 
     def most(keep, far):
         return pl.pallas_call(
@@ -298,7 +294,7 @@
             first = (up(below[0]), down(above[0]))
             second = (up(below[1]), down(above[1]))
             if step == 1:
-                arrived, weights = lax.optimization_barrier((first[0], weights))
+                arrived, factors = lax.optimization_barrier((first[0], factors))
                 first = (arrived, first[1])
             below, above = (first[0], second[0]), (first[1], second[1])
             blocks += [below, above]
@@ -320,12 +316,12 @@
                 pl.pallas_call(
                     functools.partial(last_kernel, part, len(across), modules, rank),
                     out_shape=jax.ShapeDtypeStruct((GROUP, wide), jnp.float32),
-                    in_specs=[VMEM] * (3 + len(mine)),
+                    in_specs=[VMEM] * (2 + len(mine)),
                     out_specs=VMEM,
                     compiler_params=PARAMS,
                     cost_estimate=LONG if part else COVER,
                     name="last",
-                )(chunk, weights, acts, *mine),
+                )(chunk, factors, *mine),
             )
         (mine,) = mine
         out = pl.pallas_call(

time: 30.3 us -> 30.2 us (level)
  no operation moved by 1% of the time
where the time goes in v6:
time: 30.2 us; the launch traced here: 30.1 us
  starting transfers between devices  16 us (53%)
  Pallas kernels  8.48 us (28%)
  waiting for transfers between devices  5.5 us (18%)
    ppermute x7, starting transfers between devices, up(): return lax.ppermute(x, 'ex', up_pairs)  8.99 us
    ppermute x7, waiting for transfers between devices, up(): return lax.ppermute(x, 'ex', up_pairs)  5.37 us
    ppermute x2, starting transfers between devices, swapped(): return lax.ppermute(x, 'proj', [(i, (i + 1) % proj) for i in range(proj)])  4.58 us
    ppermute x7, starting transfers between devices, down(): return lax.ppermute(x, 'ex', down_pairs)  2.46 us
    pallas_call x1, Pallas kernels, bulk(): pl.pallas_call(functools.partial(late_kernel, count, parts, modules, rank...  1.52 us
    pallas_call x1, Pallas kernels, local(): pl.pallas_call(functools.partial(token_kernel, modules, rank), out_shape=...  1.41 us
    pallas_call x2, Pallas kernels, local(): pl.pallas_call(functools.partial(last_kernel, part, len(across), modules,...  1.38 us
    pallas_call x1, Pallas kernels, bulk(): pl.pallas_call(functools.partial(early_kernel, count, parts, modules, ran...  1.36 us
  transfers between devices with their start and end apart: 16, of which 7 were waited for; matrix products, arithmetic and copies ran while one was open for 0% of the time, Pallas kernels for 22%

profile of v6, /device:TPU:1, one launch (start us, length us, event | category | flops | bytes accessed | tf_op | source)
XLA Modules:
  0.0 30.1 jit_solution(6221433843443421949)
XLA Ops:
  0.0 1.3 %queries.1 = (bf16[32,16,128]{2,1,0:T(8,128)(2,1)S(1)}, bf16[32,16,128]{2,1,0:T(8,128)(2,1)S(1)}) custom-call(f32[16,64,128]{2,1,0:T(8,128)} %bitcast.7), custom_call_target="tpu_custom_call" | custom-call | tf_op jit(solution)/shard_map/queries/pallas_call | solution.py:279
  1.3 2.1 %collective-permute-start.4 = (bf16[32,16,128]{2,1,0:T(8,128)(2,1)S(1)}, bf16[32,16,128]{2,1,0:T(8,128)(2,1)S(1)}, u32[]{:S(2)}, u32[]{:S(2)}) collective-permute-start(bf16[32,16,128]{2,1,0:T(8,128)(2,1)S(1)} %get-tuple-element.16.refs_0_), channel_id=1, source_target_pairs={{0,2},{2,6},{6,10},{10,14},{14,12},{12,8},{8,4},{4,0},{1,3},{3,7},... | collective-permute-start | bytes 393224 | tf_op jit(solution)/shard_map/ppermute | solution.py:271
  3.4 0.2 collective-permute-start
  3.5 1.3 %collective-permute-start.12 = (bf16[32,16,128]{2,1,0:T(8,128)(2,1)S(1)}, bf16[32,16,128]{2,1,0:T(8,128)(2,1)S(1)}, u32[]{:S(2)}, u32[]{:S(2)}) collective-permute-start(bf16[32,16,128]{2,1,0:T(8,128)(2,1)S(1)} %get-tuple-element.15.refs_0_), channel_id=1, source_target_pairs={{0,2},{2,6},{6,10},{10,14},{14,12},{12,8},{8,4},{4,0},{1,3},{3,7},... | collective-permute-start | bytes 393224 | tf_op jit(solution)/shard_map/ppermute | solution.py:271
  4.8 0.2 collective-permute-start.9
  5.0 1.4 %tokens.1 = (bf16[2,2,64,1024]{3,2,1,0:T(8,128)(2,1)S(1)}, f32[8,1024]{1,0:T(8,128)S(1)}) custom-call(bf16[2048,128]{1,0:T(8,128)(2,1)} %bitcast.8), custom_call_target="tpu_custom_call" | custom-call | tf_op jit(solution)/shard_map/tokens/pallas_call | solution.py:205
  6.4 0.3 collective-permute-done.4.refs_1_
  6.7 1.1 %collective-permute-start.5 = (bf16[32,16,128]{2,1,0:T(8,128)(2,1)S(1)}, bf16[32,16,128]{2,1,0:T(8,128)(2,1)S(1)}, u32[]{:S(2)}, u32[]{:S(2)}) collective-permute-start(bf16[32,16,128]{2,1,0:T(8,128)(2,1)S(1)} %collective-permute-done.4.refs_1_), channel_id=1, source_target_pairs={{0,2},{2,6},{6,10},{10,14},{14,12},{12,8},{8,4},{4,0},{1,3},{3,7},... | collective-permute-start | bytes 393224 | tf_op jit(solution)/shard_map/ppermute | solution.py:271
  7.8 0.0 collective-permute-done.refs_2_
  7.8 0.4 %collective-permute-start.1 = (bf16[32,16,128]{2,1,0:T(8,128)(2,1)S(1)}, bf16[32,16,128]{2,1,0:T(8,128)(2,1)S(1)}, u32[]{:S(2)}, u32[]{:S(2)}) collective-permute-start(bf16[32,16,128]{2,1,0:T(8,128)(2,1)S(1)} %collective-permute-done.refs_2_), channel_id=1, source_target_pairs={{2,0},{6,2},{10,6},{14,10},{12,14},{8,12},{4,8},{0,4},{3,1},{7,3},... | collective-permute-start | bytes 393224 | tf_op jit(solution)/shard_map/ppermute | solution.py:274
  8.1 1.3 %collective-permute-done.12.refs_1_ = bf16[32,16,128]{2,1,0:T(8,128)(2,1)S(1)} collective-permute-done((bf16[32,16,128]{2,1,0:T(8,128)(2,1)S(1)}, bf16[32,16,128]{2,1,0:T(8,128)(2,1)S(1)}, u32[]{:S(2)}, u32[]{:S(2)}) %collective-permute-start.12) | collective-permute-done | bytes 131104 | tf_op jit(solution)/shard_map/ppermute | solution.py:271
  9.5 1.1 %collective-permute-start.13 = (bf16[32,16,128]{2,1,0:T(8,128)(2,1)S(1)}, bf16[32,16,128]{2,1,0:T(8,128)(2,1)S(1)}, u32[]{:S(2)}, u32[]{:S(2)}) collective-permute-start(bf16[32,16,128]{2,1,0:T(8,128)(2,1)S(1)} %collective-permute-done.12.refs_1_), channel_id=1, source_target_pairs={{0,2},{2,6},{6,10},{10,14},{14,12},{12,8},{8,4},{4,0},{1,3},{3,7},... | collective-permute-start | bytes 393224 | tf_op jit(solution)/shard_map/ppermute | solution.py:271
  10.5 0.0 collective-permute-done.9.refs_2_
  10.5 0.4 %collective-permute-start.10 = (bf16[32,16,128]{2,1,0:T(8,128)(2,1)S(1)}, bf16[32,16,128]{2,1,0:T(8,128)(2,1)S(1)}, u32[]{:S(2)}, u32[]{:S(2)}) collective-permute-start(bf16[32,16,128]{2,1,0:T(8,128)(2,1)S(1)} %collective-permute-done.9.refs_2_), channel_id=1, source_target_pairs={{2,0},{6,2},{10,6},{14,10},{12,14},{8,12},{4,8},{0,4},{3,1},{7,3},... | collective-permute-start | bytes 393224 | tf_op jit(solution)/shard_map/ppermute | solution.py:274
  11.0 0.8 %collective-permute-done.5.refs_3_ = bf16[32,16,128]{2,1,0:T(8,128)(2,1)S(1)} collective-permute-done((bf16[32,16,128]{2,1,0:T(8,128)(2,1)S(1)}, bf16[32,16,128]{2,1,0:T(8,128)(2,1)S(1)}, u32[]{:S(2)}, u32[]{:S(2)}) %collective-permute-start.5) | collective-permute-done | bytes 131104 | tf_op jit(solution)/shard_map/ppermute | solution.py:271
  11.7 1.4 %collective-permute-start.6 = (bf16[32,16,128]{2,1,0:T(8,128)(2,1)S(1)}, bf16[32,16,128]{2,1,0:T(8,128)(2,1)S(1)}, u32[]{:S(2)}, u32[]{:S(2)}) collective-permute-start(bf16[32,16,128]{2,1,0:T(8,128)(2,1)S(1)} %collective-permute-done.5.refs_3_), channel_id=1, source_target_pairs={{0,2},{2,6},{6,10},{10,14},{14,12},{12,8},{8,4},{4,0},{1,3},{3,7},... | collective-permute-start | bytes 393224 | tf_op jit(solution)/shard_map/ppermute | solution.py:271
  13.1 0.0 collective-permute-done.1.refs_4_
  13.1 0.1 collective-permute-start.2
  13.2 1.6 %collective-permute-done.13.refs_3_ = bf16[32,16,128]{2,1,0:T(8,128)(2,1)S(1)} collective-permute-done((bf16[32,16,128]{2,1,0:T(8,128)(2,1)S(1)}, bf16[32,16,128]{2,1,0:T(8,128)(2,1)S(1)}, u32[]{:S(2)}, u32[]{:S(2)}) %collective-permute-start.13) | collective-permute-done | bytes 131104 | tf_op jit(solution)/shard_map/ppermute | solution.py:271
  14.7 1.0 %collective-permute-start.14 = (bf16[32,16,128]{2,1,0:T(8,128)(2,1)S(1)}, bf16[32,16,128]{2,1,0:T(8,128)(2,1)S(1)}, u32[]{:S(2)}, u32[]{:S(2)}) collective-permute-start(bf16[32,16,128]{2,1,0:T(8,128)(2,1)S(1)} %collective-permute-done.13.refs_3_), channel_id=1, source_target_pairs={{0,2},{2,6},{6,10},{10,14},{14,12},{12,8},{8,4},{4,0},{1,3},{3,7},... | collective-permute-start | bytes 393224 | tf_op jit(solution)/shard_map/ppermute | solution.py:271
  15.7 0.0 collective-permute-done.10.refs_4_
  15.7 0.7 %collective-permute-start.11 = (bf16[32,16,128]{2,1,0:T(8,128)(2,1)S(1)}, bf16[32,16,128]{2,1,0:T(8,128)(2,1)S(1)}, u32[]{:S(2)}, u32[]{:S(2)}) collective-permute-start(bf16[32,16,128]{2,1,0:T(8,128)(2,1)S(1)} %collective-permute-done.10.refs_4_), channel_id=1, source_target_pairs={{2,0},{6,2},{10,6},{14,10},{12,14},{8,12},{4,8},{0,4},{3,1},{7,3},... | collective-permute-start | bytes 393224 | tf_op jit(solution)/shard_map/ppermute | solution.py:274
  16.4 1.1 %collective-permute-done.6.refs_5_ = bf16[32,16,128]{2,1,0:T(8,128)(2,1)S(1)} collective-permute-done((bf16[32,16,128]{2,1,0:T(8,128)(2,1)S(1)}, bf16[32,16,128]{2,1,0:T(8,128)(2,1)S(1)}, u32[]{:S(2)}, u32[]{:S(2)}) %collective-permute-start.6) | collective-permute-done | bytes 131104 | tf_op jit(solution)/shard_map/ppermute | solution.py:271
  17.5 1.1 %collective-permute-start.7 = (bf16[32,16,128]{2,1,0:T(8,128)(2,1)S(1)}, bf16[32,16,128]{2,1,0:T(8,128)(2,1)S(1)}, u32[]{:S(2)}, u32[]{:S(2)}) collective-permute-start(bf16[32,16,128]{2,1,0:T(8,128)(2,1)S(1)} %collective-permute-done.6.refs_5_), channel_id=1, source_target_pairs={{0,2},{2,6},{6,10},{10,14},{14,12},{12,8},{8,4},{4,0},{1,3},{3,7},... | collective-permute-start | bytes 393224 | tf_op jit(solution)/shard_map/ppermute | solution.py:271
  18.6 0.0 collective-permute-done.2.refs_6_
  18.6 0.6 %collective-permute-start.3 = (bf16[32,16,128]{2,1,0:T(8,128)(2,1)S(1)}, bf16[32,16,128]{2,1,0:T(8,128)(2,1)S(1)}, u32[]{:S(2)}, u32[]{:S(2)}) collective-permute-start(bf16[32,16,128]{2,1,0:T(8,128)(2,1)S(1)} %collective-permute-done.2.refs_6_), channel_id=1, source_target_pairs={{2,0},{6,2},{10,6},{14,10},{12,14},{8,12},{4,8},{0,4},{3,1},{7,3},... | collective-permute-start | bytes 393224 | tf_op jit(solution)/shard_map/ppermute | solution.py:274
  19.2 0.3 %collective-permute-done.14.refs_5_ = bf16[32,16,128]{2,1,0:T(8,128)(2,1)S(1)} collective-permute-done((bf16[32,16,128]{2,1,0:T(8,128)(2,1)S(1)}, bf16[32,16,128]{2,1,0:T(8,128)(2,1)S(1)}, u32[]{:S(2)}, u32[]{:S(2)}) %collective-permute-start.14) | collective-permute-done | bytes 131104 | tf_op jit(solution)/shard_map/ppermute | solution.py:271
  19.5 1.4 %early.1.refs_9_ = f32[112,1152]{1,0:T(8,128)S(1)} custom-call(bf16[32,16,128]{2,1,0:T(8,128)(2,1)S(1)} %get-tuple-element.15.refs_0_, bf16[32,16,128]{2,1,0:T(8,128)(2,1)S(1)} %collective-permute-done.12.refs_1_, bf16[32,16,128]{2,1,0:T(8,128)(2,1)S(1)} %collective-permute-done.refs_2_, bf16[32,16,128]{2,1,0:T(8,128)(2,1)S(1)} %collective-permute-done.13.refs_3_, ...), custom_call_target="tpu_custom_call" | custom-call | flops 692099968 | bytes 1024 | tf_op jit(solution)/shard_map/early/pallas_call | solution.py:227
  20.9 0.0 collective-permute-done.11.refs_6_
  20.9 1.5 %late.1 = (f32[64,1152]{1,0:T(8,128)S(1)}, f32[72,1152]{1,0:T(8,128)S(1)}) custom-call(bf16[32,16,128]{2,1,0:T(8,128)(2,1)S(1)} %get-tuple-element.16.refs_0_, bf16[32,16,128]{2,1,0:T(8,128)(2,1)S(1)} %collective-permute-done.4.refs_1_, bf16[32,16,128]{2,1,0:T(8,128)(2,1)S(1)} %collective-permute-done.9.refs_2_, ...), custom_call_target="tpu_custom_call" | custom-call | flops 692099968 | bytes 1024 | tf_op jit(solution)/shard_map/late/pallas_call | solution.py:236
  22.4 4.0 %collective-permute-start.15 = (f32[72,1152]{1,0:T(8,128)S(1)}, f32[72,1152]{1,0:T(8,128)S(1)}, u32[]{:S(2)}, u32[]{:S(2)}) collective-permute-start(f32[72,1152]{1,0:T(8,128)S(1)} %get-tuple-element.22), channel_id=1, source_target_pairs={{0,1},{1,0},{2,3},{3,2},{4,5},{5,4},{6,7},{7,6},{8,9},{9,8},{10,11... | collective-permute-start | bytes 995336 | tf_op jit(solution)/shard_map/ppermute | solution.py:223
  26.5 0.0 collective-permute-done.7.chunk
  26.5 0.7 %last.2.refs_0_ = f32[16,1152]{1,0:T(8,128)S(1)} custom-call(bf16[32,16,128]{2,1,0:T(8,128)(2,1)S(1)} %collective-permute-done.7.chunk, bf16[2,2,64,1024]{3,2,1,0:T(8,128)(2,1)S(1)} %get-tuple-element.18.p_ref.refs_7_), custom_call_target="tpu_custom_call" | custom-call | flops 692099968 | bytes 1024 | tf_op jit(solution)/shard_map/last/pallas_call | solution.py:316
  27.2 0.0 collective-permute-done.3.chunk
  27.2 0.7 %last.3.own_ref = f32[16,1152]{1,0:T(8,128)S(1)} custom-call(bf16[32,16,128]{2,1,0:T(8,128)(2,1)S(1)} %collective-permute-done.3.chunk, bf16[2,2,64,1024]{3,2,1,0:T(8,128)(2,1)S(1)} %get-tuple-element.18.p_ref.refs_7_, f32[16,1152]{1,0:T(8,128)S(1)} %last.2.refs_0_), custom_call_target="tpu_custom_call" | custom-call | flops 10000000000 | bytes 4194304 | tf_op jit(solution)/shard_map/last/pallas_call | solution.py:316
  27.9 0.5 %collective-permute-start.8 = (f32[16,1152]{1,0:T(8,128)S(1)}, f32[16,1152]{1,0:T(8,128)S(1)}, u32[]{:S(2)}, u32[]{:S(2)}) collective-permute-start(f32[16,1152]{1,0:T(8,128)S(1)} %last.3.own_ref), channel_id=1, source_target_pairs={{0,1},{1,0},{2,3},{3,2},{4,5},{5,4},{6,7},{7,6},{8,9},{9,8},{10,11... | collective-permute-start | bytes 221192 | tf_op jit(solution)/shard_map/ppermute | solution.py:223
  28.4 0.0 collective-permute-done.15.far_ref
  28.4 0.8 %most.1 = (f32[64,1024]{1,0:T(8,128)}, f32[8,1024]{1,0:T(8,128)S(1)}) custom-call(f32[64,1152]{1,0:T(8,128)S(1)} %get-tuple-element.21.keep_ref, f32[72,1152]{1,0:T(8,128)S(1)} %collective-permute-done.15.far_ref, f32[8,1024]{1,0:T(8,128)S(1)} %get-tuple-element.20.refs_8_.n_ref), custom_call_target="tpu_custom_call" | custom-call | flops 10000000000 | bytes 4194304 | tf_op jit(solution)/shard_map/most/pallas_call | solution.py:251
  29.2 0.1 collective-permute-done.8.far_ref
  29.3 0.7 %rest.1 = f32[64,1024]{1,0:T(8,128)} custom-call(f32[16,1152]{1,0:T(8,128)S(1)} %last.3.own_ref, f32[16,1152]{1,0:T(8,128)S(1)} %collective-permute-done.8.far_ref, f32[8,1024]{1,0:T(8,128)S(1)} %get-tuple-element.23.s_ref, f32[64,1024]{1,0:T(8,128)} %get-tuple-element.24.most_ref), custom_call_target="tpu_custom_call", output_to_operand_aliasing={{}: (3, {})} | custom-call | tf_op jit(solution)/shard_map/rest/pallas_call | solution.py:327
Async XLA Ops:
  1.3 5.4 %collective-permute-start.4 = (bf16[32,16,128]{2,1,0:T(8,128)(2,1)S(1)}, bf16[32,16,128]{2,1,0:T(8,128)(2,1)S(1)}, u32[]{:S(2)}, u32[]{:S(2)}) collective-permute-start(bf16[32,16,128]{2,1,0:T(8,128)(2,1)S(1)} %get-tuple-element.16.refs_0_), channel_id=1, source_target_pairs={{0,2},{2,6},{6,10},{10,14},{14,12},{12,8},{8,4},{4,0},{1,3},{3,7},... | collective-permute-start | bytes 393224 | tf_op jit(solution)/shard_map/ppermute | solution.py:271
  3.4 4.4 %collective-permute-start = (bf16[32,16,128]{2,1,0:T(8,128)(2,1)S(1)}, bf16[32,16,128]{2,1,0:T(8,128)(2,1)S(1)}, u32[]{:S(2)}, u32[]{:S(2)}) collective-permute-start(bf16[32,16,128]{2,1,0:T(8,128)(2,1)S(1)} %get-tuple-element.15.refs_0_), channel_id=1, source_target_pairs={{2,0},{6,2},{10,6},{14,10},{12,14},{8,12},{4,8},{0,4},{3,1},{7,3},... | collective-permute-start | bytes 393224 | tf_op jit(solution)/shard_map/ppermute | solution.py:274
  3.5 6.0 %collective-permute-start.12 = (bf16[32,16,128]{2,1,0:T(8,128)(2,1)S(1)}, bf16[32,16,128]{2,1,0:T(8,128)(2,1)S(1)}, u32[]{:S(2)}, u32[]{:S(2)}) collective-permute-start(bf16[32,16,128]{2,1,0:T(8,128)(2,1)S(1)} %get-tuple-element.15.refs_0_), channel_id=1, source_target_pairs={{0,2},{2,6},{6,10},{10,14},{14,12},{12,8},{8,4},{4,0},{1,3},{3,7},... | collective-permute-start | bytes 393224 | tf_op jit(solution)/shard_map/ppermute | solution.py:271
  4.8 5.7 %collective-permute-start.9 = (bf16[32,16,128]{2,1,0:T(8,128)(2,1)S(1)}, bf16[32,16,128]{2,1,0:T(8,128)(2,1)S(1)}, u32[]{:S(2)}, u32[]{:S(2)}) collective-permute-start(bf16[32,16,128]{2,1,0:T(8,128)(2,1)S(1)} %get-tuple-element.16.refs_0_), channel_id=1, source_target_pairs={{2,0},{6,2},{10,6},{14,10},{12,14},{8,12},{4,8},{0,4},{3,1},{7,3},... | collective-permute-start | bytes 393224 | tf_op jit(solution)/shard_map/ppermute | solution.py:274
  6.7 5.0 %collective-permute-start.5 = (bf16[32,16,128]{2,1,0:T(8,128)(2,1)S(1)}, bf16[32,16,128]{2,1,0:T(8,128)(2,1)S(1)}, u32[]{:S(2)}, u32[]{:S(2)}) collective-permute-start(bf16[32,16,128]{2,1,0:T(8,128)(2,1)S(1)} %collective-permute-done.4.refs_1_), channel_id=1, source_target_pairs={{0,2},{2,6},{6,10},{10,14},{14,12},{12,8},{8,4},{4,0},{1,3},{3,7},... | collective-permute-start | bytes 393224 | tf_op jit(solution)/shard_map/ppermute | solution.py:271
  7.8 5.3 %collective-permute-start.1 = (bf16[32,16,128]{2,1,0:T(8,128)(2,1)S(1)}, bf16[32,16,128]{2,1,0:T(8,128)(2,1)S(1)}, u32[]{:S(2)}, u32[]{:S(2)}) collective-permute-start(bf16[32,16,128]{2,1,0:T(8,128)(2,1)S(1)} %collective-permute-done.refs_2_), channel_id=1, source_target_pairs={{2,0},{6,2},{10,6},{14,10},{12,14},{8,12},{4,8},{0,4},{3,1},{7,3},... | collective-permute-start | bytes 393224 | tf_op jit(solution)/shard_map/ppermute | solution.py:274
  9.5 5.3 %collective-permute-start.13 = (bf16[32,16,128]{2,1,0:T(8,128)(2,1)S(1)}, bf16[32,16,128]{2,1,0:T(8,128)(2,1)S(1)}, u32[]{:S(2)}, u32[]{:S(2)}) collective-permute-start(bf16[32,16,128]{2,1,0:T(8,128)(2,1)S(1)} %collective-permute-done.12.refs_1_), channel_id=1, source_target_pairs={{0,2},{2,6},{6,10},{10,14},{14,12},{12,8},{8,4},{4,0},{1,3},{3,7},... | collective-permute-start | bytes 393224 | tf_op jit(solution)/shard_map/ppermute | solution.py:271
  10.5 5.2 %collective-permute-start.10 = (bf16[32,16,128]{2,1,0:T(8,128)(2,1)S(1)}, bf16[32,16,128]{2,1,0:T(8,128)(2,1)S(1)}, u32[]{:S(2)}, u32[]{:S(2)}) collective-permute-start(bf16[32,16,128]{2,1,0:T(8,128)(2,1)S(1)} %collective-permute-done.9.refs_2_), channel_id=1, source_target_pairs={{2,0},{6,2},{10,6},{14,10},{12,14},{8,12},{4,8},{0,4},{3,1},{7,3},... | collective-permute-start | bytes 393224 | tf_op jit(solution)/shard_map/ppermute | solution.py:274
  11.7 5.8 %collective-permute-start.6 = (bf16[32,16,128]{2,1,0:T(8,128)(2,1)S(1)}, bf16[32,16,128]{2,1,0:T(8,128)(2,1)S(1)}, u32[]{:S(2)}, u32[]{:S(2)}) collective-permute-start(bf16[32,16,128]{2,1,0:T(8,128)(2,1)S(1)} %collective-permute-done.5.refs_3_), channel_id=1, source_target_pairs={{0,2},{2,6},{6,10},{10,14},{14,12},{12,8},{8,4},{4,0},{1,3},{3,7},... | collective-permute-start | bytes 393224 | tf_op jit(solution)/shard_map/ppermute | solution.py:271
  13.1 5.5 %collective-permute-start.2 = (bf16[32,16,128]{2,1,0:T(8,128)(2,1)S(1)}, bf16[32,16,128]{2,1,0:T(8,128)(2,1)S(1)}, u32[]{:S(2)}, u32[]{:S(2)}) collective-permute-start(bf16[32,16,128]{2,1,0:T(8,128)(2,1)S(1)} %collective-permute-done.1.refs_4_), channel_id=1, source_target_pairs={{2,0},{6,2},{10,6},{14,10},{12,14},{8,12},{4,8},{0,4},{3,1},{7,3},... | collective-permute-start | bytes 393224 | tf_op jit(solution)/shard_map/ppermute | solution.py:274
  14.7 4.8 %collective-permute-start.14 = (bf16[32,16,128]{2,1,0:T(8,128)(2,1)S(1)}, bf16[32,16,128]{2,1,0:T(8,128)(2,1)S(1)}, u32[]{:S(2)}, u32[]{:S(2)}) collective-permute-start(bf16[32,16,128]{2,1,0:T(8,128)(2,1)S(1)} %collective-permute-done.13.refs_3_), channel_id=1, source_target_pairs={{0,2},{2,6},{6,10},{10,14},{14,12},{12,8},{8,4},{4,0},{1,3},{3,7},... | collective-permute-start | bytes 393224 | tf_op jit(solution)/shard_map/ppermute | solution.py:271
  15.7 5.2 %collective-permute-start.11 = (bf16[32,16,128]{2,1,0:T(8,128)(2,1)S(1)}, bf16[32,16,128]{2,1,0:T(8,128)(2,1)S(1)}, u32[]{:S(2)}, u32[]{:S(2)}) collective-permute-start(bf16[32,16,128]{2,1,0:T(8,128)(2,1)S(1)} %collective-permute-done.10.refs_4_), channel_id=1, source_target_pairs={{2,0},{6,2},{10,6},{14,10},{12,14},{8,12},{4,8},{0,4},{3,1},{7,3},... | collective-permute-start | bytes 393224 | tf_op jit(solution)/shard_map/ppermute | solution.py:274
  17.5 9.0 %collective-permute-start.7 = (bf16[32,16,128]{2,1,0:T(8,128)(2,1)S(1)}, bf16[32,16,128]{2,1,0:T(8,128)(2,1)S(1)}, u32[]{:S(2)}, u32[]{:S(2)}) collective-permute-start(bf16[32,16,128]{2,1,0:T(8,128)(2,1)S(1)} %collective-permute-done.6.refs_5_), channel_id=1, source_target_pairs={{0,2},{2,6},{6,10},{10,14},{14,12},{12,8},{8,4},{4,0},{1,3},{3,7},... | collective-permute-start | bytes 393224 | tf_op jit(solution)/shard_map/ppermute | solution.py:271
  18.6 8.6 %collective-permute-start.3 = (bf16[32,16,128]{2,1,0:T(8,128)(2,1)S(1)}, bf16[32,16,128]{2,1,0:T(8,128)(2,1)S(1)}, u32[]{:S(2)}, u32[]{:S(2)}) collective-permute-start(bf16[32,16,128]{2,1,0:T(8,128)(2,1)S(1)} %collective-permute-done.2.refs_6_), channel_id=1, source_target_pairs={{2,0},{6,2},{10,6},{14,10},{12,14},{8,12},{4,8},{0,4},{3,1},{7,3},... | collective-permute-start | bytes 393224 | tf_op jit(solution)/shard_map/ppermute | solution.py:274
  22.4 6.0 %collective-permute-start.15 = (f32[72,1152]{1,0:T(8,128)S(1)}, f32[72,1152]{1,0:T(8,128)S(1)}, u32[]{:S(2)}, u32[]{:S(2)}) collective-permute-start(f32[72,1152]{1,0:T(8,128)S(1)} %get-tuple-element.22), channel_id=1, source_target_pairs={{0,1},{1,0},{2,3},{3,2},{4,5},{5,4},{6,7},{7,6},{8,9},{9,8},{10,11... | collective-permute-start | bytes 995336 | tf_op jit(solution)/shard_map/ppermute | solution.py:223
  27.9 1.5 %collective-permute-start.8 = (f32[16,1152]{1,0:T(8,128)S(1)}, f32[16,1152]{1,0:T(8,128)S(1)}, u32[]{:S(2)}, u32[]{:S(2)}) collective-permute-start(f32[16,1152]{1,0:T(8,128)S(1)} %last.3.own_ref), channel_id=1, source_target_pairs={{0,1},{1,0},{2,3},{3,2},{4,5},{5,4},{6,7},{7,6},{8,9},{9,8},{10,11... | collective-permute-start | bytes 221192 | tf_op jit(solution)/shard_map/ppermute | solution.py:223

commit v7 on v6

--- a/solution.py
+++ b/solution.py
@@ -12,7 +12,12 @@
 GROUP = 16
 VMEM = pl.BlockSpec(memory_space=pltpu.VMEM)
 HBM = pl.BlockSpec(memory_space=pltpu.HBM)
-COVER = pl.CostEstimate(flops=692100000, bytes_accessed=1024, transcendentals=0)
+
+
+def cover(share):
+    return pl.CostEstimate(flops=int(share * 10**9), bytes_accessed=1024, transcendentals=0)
+
+
 ANY = pl.BlockSpec(memory_space=pl.ANY)
 PARAMS = pltpu.CompilerParams(vmem_limit_bytes=16 * 1024 * 1024)
 LONG = pl.CostEstimate(flops=10**10, bytes_accessed=4 * 1024 * 1024, transcendentals=0)
@@ -47,22 +52,30 @@
                 o_ref[m * own + i] = got.astype(jnp.bfloat16)
 
 
-def token_kernel(modules, rank, x_ref, p_ref, n_ref, rows, wide, sem):
+def token_kernel(modules, rank, core, x_ref, *refs):
+    p_ref, n_ref, rows, wide, sem = refs[-5:]
     tokens = x_ref.shape[0] // modules
-    copy = pltpu.make_async_copy(x_ref, rows, sem)
-    copy.start()
-    copy.wait()
-    wide[...] = rows[...].astype(jnp.float32)
-    norm = jnp.zeros((1, tokens), jnp.float32)
-    for m in range(modules):
-        turned = wide[pl.ds(m, tokens, stride=modules), :].T
-        act, grad = turned[:rank], turned[rank:]
-        norm += jnp.sum(act * act, axis=0, keepdims=True) * jnp.sum(
-            grad * grad, axis=0, keepdims=True
-        )
-        p_ref[0, m] = act.astype(jnp.bfloat16)
-        p_ref[1, m] = grad.astype(jnp.bfloat16)
-    n_ref[...] = jnp.broadcast_to(norm, n_ref.shape)
+
+    def run():
+        copy = pltpu.make_async_copy(x_ref, rows, sem)
+        copy.start()
+        copy.wait()
+        wide[...] = rows[...].astype(jnp.float32)
+        norm = jnp.zeros((1, tokens), jnp.float32)
+        for m in range(modules):
+            turned = wide[pl.ds(m, tokens, stride=modules), :].T
+            act, grad = turned[:rank], turned[rank:]
+            norm += jnp.sum(act * act, axis=0, keepdims=True) * jnp.sum(
+                grad * grad, axis=0, keepdims=True
+            )
+            p_ref[0, m] = act.astype(jnp.bfloat16)
+            p_ref[1, m] = grad.astype(jnp.bfloat16)
+        n_ref[...] = jnp.broadcast_to(norm, n_ref.shape)
+
+    if core is None:
+        run()
+    else:
+        pl.when((lax.axis_index("proj") == 0) == (core == 0))(run)
 
 
 def lane_squares(chunks):
@@ -129,29 +142,31 @@
     tokens = p_ref.shape[3]
     for b in range(count):
         o_ref[b * GROUP : (b + 1) * GROUP, tokens:] = lane_squares(blocks[b : b + 1])
-
+    for lanes in tiles(tokens):
+        o_ref[:, lanes] = products(blocks, 0, parts, modules, rank, p_ref, lanes)
+
+
+def late_kernel(count, parts, modules, rank, *refs):
+    blocks = refs[:count]
+    p_ref, sum_ref, o_ref = refs[count:]
+    tokens = p_ref.shape[3]
+    known = sum_ref.shape[0]
+    for b in range(count):
+        o_ref[b * GROUP : (b + 1) * GROUP, tokens:] = lane_squares(blocks[b : b + 1])
     for lanes in tiles(tokens):
         o_ref[:, lanes] = products(blocks, parts - 1, parts, modules, rank, p_ref, lanes)
-
-
-def late_kernel(count, parts, modules, rank, ring, *refs):
-    blocks = refs[:count]
-    p_ref, n_ref, sum_ref, keep_ref, send_ref, both = refs[count:]
+    o_ref[:known] += sum_ref[...]
+
+
+def third_kernel(count, parts, modules, rank, ring, chunk, p_ref, n_ref, sum_ref, keep_ref, send_ref, last):
     tokens = p_ref.shape[3]
     half = keep_ref.shape[0] // GROUP
+    first = (count - 1) * GROUP
+    last_kernel(0, parts, modules, rank, chunk, p_ref, sum_ref.at[first:], last)
     send_ref[half * GROUP :, :tokens] = n_ref[...]
-    for b in range(count):
-        span = slice(b * GROUP, (b + 1) * GROUP)
-        both[span, tokens:] = sum_ref[span, tokens:] + lane_squares(blocks[b : b + 1])
-
-    for lanes in tiles(tokens):
-        both[:, lanes] = sum_ref[:, lanes] + products(
-            blocks, 0, parts, modules, rank, p_ref, lanes
-        )
-
     me = lax.axis_index("proj")
     for b, index in enumerate(ring()):
-        rows = both[b * GROUP : (b + 1) * GROUP]
+        rows = last[...] if b == count - 1 else sum_ref[b * GROUP : (b + 1) * GROUP]
         at = pl.multiple_of(lax.rem(index, half) * GROUP, GROUP)
 
         @pl.when(index // half == me)
@@ -202,52 +217,63 @@
     columns = queries * ex // proj
 
     token_rows = train_factors.reshape(tokens * modules, doubled)
-    factors, norm = pl.pallas_call(
-        functools.partial(token_kernel, modules, rank),
-        out_shape=(
-            jax.ShapeDtypeStruct((2, modules, rank, tokens), jnp.bfloat16),
-            jax.ShapeDtypeStruct((8, tokens), jnp.float32),
-        ),
-        in_specs=[HBM],
-        out_specs=(VMEM, VMEM),
-        scratch_shapes=[
-            pltpu.VMEM((tokens * modules, doubled), jnp.bfloat16),
-            pltpu.VMEM((tokens * modules, doubled), jnp.float32),
-            pltpu.SemaphoreType.DMA,
-        ],
-        compiler_params=PARAMS,
-        name="tokens",
-    )(pltpu.with_memory_space_constraint(token_rows, pltpu.HBM))
+    def token_work(core, *before):
+        return pl.pallas_call(
+            functools.partial(token_kernel, modules, rank, core),
+            out_shape=(
+                jax.ShapeDtypeStruct((2, modules, rank, tokens), jnp.bfloat16),
+                jax.ShapeDtypeStruct((8, tokens), jnp.float32),
+            ),
+            in_specs=[HBM] + [VMEM] * len(before),
+            out_specs=(VMEM, VMEM),
+            scratch_shapes=[
+                pltpu.VMEM((tokens * modules, doubled), jnp.bfloat16),
+                pltpu.VMEM((tokens * modules, doubled), jnp.float32),
+                pltpu.SemaphoreType.DMA,
+            ],
+            input_output_aliases={1 + i: i for i in range(len(before))},
+            compiler_params=PARAMS,
+            name="tokens",
+        )(pltpu.with_memory_space_constraint(token_rows, pltpu.HBM), *before)
 
     def swapped(x):
         return lax.ppermute(x, "proj", [(i, (i + 1) % proj) for i in range(proj)])
 
-    def bulk(blocks, ring):
+    def bulk(blocks, ring, factors, norm):
         count, parts = len(blocks), len(blocks[0])
         early = pl.pallas_call(
-            functools.partial(early_kernel, count, parts, modules, rank),
+            functools.partial(early_kernel, count - 1, parts, modules, rank),
+            out_shape=jax.ShapeDtypeStruct(((count - 1) * GROUP, wide), jnp.float32),
+            in_specs=[VMEM] * count,
+            out_specs=VMEM,
+            compiler_params=PARAMS,
+            cost_estimate=cover(0.81),
+            name="early",
+        )(*[block[0] for block in blocks[:-1]], factors)
+        late = pl.pallas_call(
+            functools.partial(late_kernel, count, parts, modules, rank),
             out_shape=jax.ShapeDtypeStruct((count * GROUP, wide), jnp.float32),
-            in_specs=[VMEM] * (count + 1),
+            in_specs=[VMEM] * (count + 2),
             out_specs=VMEM,
             compiler_params=PARAMS,
-            cost_estimate=COVER,
-            name="early",
-        )(*[block[-1] for block in blocks], factors)
+            cost_estimate=cover(0.58),
+            name="late",
+        )(*[block[-1] for block in blocks], factors, early)
         return pl.pallas_call(
-            functools.partial(late_kernel, count, parts, modules, rank, ring),
+            functools.partial(third_kernel, count, parts, modules, rank, ring),
             out_shape=(
                 jax.ShapeDtypeStruct((columns, wide), jnp.float32),
                 jax.ShapeDtypeStruct((columns + 8, wide), jnp.float32),
             ),
-            in_specs=[VMEM] * (count + 3),
+            in_specs=[VMEM] * 4,
             out_specs=(VMEM, VMEM),
-            scratch_shapes=[pltpu.VMEM((count * GROUP, wide), jnp.float32)],
-            compiler_params=PARAMS,
-            cost_estimate=COVER,
-            name="late",
-        )(*[block[0] for block in blocks], factors, norm, early)
-
-    def most(keep, far):
+            scratch_shapes=[pltpu.VMEM((GROUP, wide), jnp.float32)],
+            compiler_params=PARAMS,
+            cost_estimate=cover(0.23),
+            name="third",
+        )(blocks[-1][0], factors, norm, late)
+
+    def most(keep, far, norm):
         return pl.pallas_call(
             functools.partial(most_kernel, width),
             out_shape=(
@@ -288,7 +314,10 @@
             compiler_params=PARAMS,
             name="queries",
         )(pltpu.with_memory_space_constraint(rows, pltpu.HBM))
-        below, above = block, block
+        factors, norm = token_work(1)
+        later = lax.optimization_barrier((block[1], block[0], factors))
+        below, above, factors = (block[0], later[0]), (later[1], block[1]), later[2]
+        factors, norm = token_work(0, factors, norm)
         blocks, steps = [block], [0]
         for step in range(1, ex // 2):
             first = (up(below[0]), down(above[0]))
@@ -308,8 +337,8 @@
         def opposite():
             return index_at(place_of(lax.axis_index("ex"), ex) + ex // 2, ex)
 
-        keep, send = bulk(blocks, ring)
-        out, scale = most(keep, swapped(send))
+        keep, send = bulk(blocks, ring, factors, norm)
+        out, scale = most(keep, swapped(send), norm)
         mine = ()
         for part, chunk in enumerate(across):
             mine = (
@@ -319,7 +348,7 @@
                     in_specs=[VMEM] * (2 + len(mine)),
                     out_specs=VMEM,
                     compiler_params=PARAMS,
-                    cost_estimate=LONG if part else COVER,
+                    cost_estimate=LONG if part else cover(0.46),
                     name="last",
                 )(chunk, factors, *mine),
             )
@@ -340,8 +369,9 @@
         gathered = gathered.reshape(count, GROUP, modules, 2, pairs // 2, LANES)
         gathered = gathered.transpose(0, 3, 2, 4, 1, 5).reshape(count, 2, -1, GROUP, LANES)
         blocks = [(gathered[i, 0], gathered[i, 1]) for i in range(count)]
-        keep, send = bulk(blocks, lambda: [jnp.int32(i) for i in range(count)])
-        out, _ = most(keep, swapped(send))
+        factors, norm = token_work(None)
+        keep, send = bulk(blocks, lambda: [jnp.int32(i) for i in range(count)], factors, norm)
+        out, _ = most(keep, swapped(send), norm)
     return out.T
 
 

time: 30.2 us -> 29.6 us (0.980)
  starting transfers between devices: 16 us -> 14.3 us
  Pallas kernels: 8.48 us -> 9.25 us
  waiting for transfers between devices: 5.5 us -> 5.85 us
    ppermute x2, starting transfers between devices: 4.58 us -> 3.16 us  [swapped(): return lax.ppermute(x, 'proj', [(i, (i + 1) % proj) for i in range(proj)])]
    pallas_call x2 -> x4, Pallas kernels: 2.77 us -> 3.71 us  [the longest x1 1.48 us: bulk(): pl.pallas_call(functools.partial(early_kernel, count - 1, parts, modules,...]
    ppermute x7, waiting for transfers between devices: 5.37 us -> 5.71 us  [up(): return lax.ppermute(x, 'ex', up_pairs)]
  transfers between devices with their start and end apart: 16 -> 16, of which waited for: 7 -> 6; matrix products, arithmetic and copies ran while one was open for 0% -> 0% of each run, Pallas kernels for 22% -> 25%
where the time goes in v7:
time: 29.6 us; the launch traced here: 29.4 us
  starting transfers between devices  14.3 us (48%)
  Pallas kernels  9.25 us (31%)
  waiting for transfers between devices  5.85 us (20%)
    ppermute x7, starting transfers between devices, up(): return lax.ppermute(x, 'ex', up_pairs)  8.78 us
    ppermute x7, waiting for transfers between devices, up(): return lax.ppermute(x, 'ex', up_pairs)  5.71 us
    ppermute x2, starting transfers between devices, swapped(): return lax.ppermute(x, 'proj', [(i, (i + 1) % proj) for i in range(proj)])  3.16 us
    ppermute x7, starting transfers between devices, down(): return lax.ppermute(x, 'ex', down_pairs)  2.32 us
    pallas_call x1, Pallas kernels, bulk(): pl.pallas_call(functools.partial(early_kernel, count - 1, parts, modules,...  1.48 us
    pallas_call x2, Pallas kernels, token_work(): pl.pallas_call(functools.partial(token_kernel, modules, rank, core), out_...  1.42 us
    pallas_call x2, Pallas kernels, local(): pl.pallas_call(functools.partial(last_kernel, part, len(across), modules,...  1.39 us
    pallas_call x1, Pallas kernels, bulk(): pl.pallas_call(functools.partial(late_kernel, count, parts, modules, rank...  1.34 us
  transfers between devices with their start and end apart: 16, of which 6 were waited for; matrix products, arithmetic and copies ran while one was open for 0% of the time, Pallas kernels for 25%

profile of v7, /device:TPU:1, one launch (start us, length us, event | category | flops | bytes accessed | tf_op | source)
XLA Modules:
  0.0 29.4 jit_solution(9231832339914820484)
XLA Ops:
  0.0 1.3 %queries.1 = (bf16[32,16,128]{2,1,0:T(8,128)(2,1)S(1)}, bf16[32,16,128]{2,1,0:T(8,128)(2,1)S(1)}) custom-call(f32[16,64,128]{2,1,0:T(8,128)} %bitcast.9), custom_call_target="tpu_custom_call" | custom-call | tf_op jit(solution)/shard_map/queries/pallas_call | solution.py:305
  1.3 2.1 %collective-permute-start.4 = (bf16[32,16,128]{2,1,0:T(8,128)(2,1)S(1)}, bf16[32,16,128]{2,1,0:T(8,128)(2,1)S(1)}, u32[]{:S(2)}, u32[]{:S(2)}) collective-permute-start(bf16[32,16,128]{2,1,0:T(8,128)(2,1)S(1)} %get-tuple-element.28.refs_0_), channel_id=1, source_target_pairs={{0,2},{2,6},{6,10},{10,14},{14,12},{12,8},{8,4},{4,0},{1,3},{3,7},... | collective-permute-start | bytes 393224 | tf_op jit(solution)/shard_map/ppermute | solution.py:297
  3.4 0.2 collective-permute-start
  3.5 1.4 %tokens.2 = (bf16[2,2,64,1024]{3,2,1,0:T(8,128)(2,1)S(1)}, f32[8,1024]{1,0:T(8,128)S(1)}) custom-call(bf16[2048,128]{1,0:T(8,128)(2,1)} %bitcast.7), custom_call_target="tpu_custom_call" | custom-call | tf_op jit(solution)/shard_map/tokens/pallas_call | solution.py:221
  4.9 1.4 %collective-permute-start.12 = (bf16[32,16,128]{2,1,0:T(8,128)(2,1)S(1)}, bf16[32,16,128]{2,1,0:T(8,128)(2,1)S(1)}, u32[]{:S(2)}, u32[]{:S(2)}) collective-permute-start(bf16[32,16,128]{2,1,0:T(8,128)(2,1)S(1)} %get-tuple-element.30.refs_0_), channel_id=1, source_target_pairs={{0,2},{2,6},{6,10},{10,14},{14,12},{12,8},{8,4},{4,0},{1,3},{3,7},... | collective-permute-start | bytes 393224 | tf_op jit(solution)/shard_map/ppermute | solution.py:297
  6.3 0.2 collective-permute-start.9
  6.5 0.2 collective-permute-done.4.refs_1_
  6.7 1.2 %collective-permute-start.5 = (bf16[32,16,128]{2,1,0:T(8,128)(2,1)S(1)}, bf16[32,16,128]{2,1,0:T(8,128)(2,1)S(1)}, u32[]{:S(2)}, u32[]{:S(2)}) collective-permute-start(bf16[32,16,128]{2,1,0:T(8,128)(2,1)S(1)} %collective-permute-done.4.refs_1_), channel_id=1, source_target_pairs={{0,2},{2,6},{6,10},{10,14},{14,12},{12,8},{8,4},{4,0},{1,3},{3,7},... | collective-permute-start | bytes 393224 | tf_op jit(solution)/shard_map/ppermute | solution.py:297
  7.9 0.0 collective-permute-done.refs_2_
  7.9 0.3 collective-permute-start.1
  8.1 2.3 %collective-permute-done.12.refs_1_ = bf16[32,16,128]{2,1,0:T(8,128)(2,1)S(1)} collective-permute-done((bf16[32,16,128]{2,1,0:T(8,128)(2,1)S(1)}, bf16[32,16,128]{2,1,0:T(8,128)(2,1)S(1)}, u32[]{:S(2)}, u32[]{:S(2)}) %collective-permute-start.12) | collective-permute-done | bytes 131104 | tf_op jit(solution)/shard_map/ppermute | solution.py:297
  10.5 1.0 %collective-permute-start.13 = (bf16[32,16,128]{2,1,0:T(8,128)(2,1)S(1)}, bf16[32,16,128]{2,1,0:T(8,128)(2,1)S(1)}, u32[]{:S(2)}, u32[]{:S(2)}) collective-permute-start(bf16[32,16,128]{2,1,0:T(8,128)(2,1)S(1)} %collective-permute-done.12.refs_1_), channel_id=1, source_target_pairs={{0,2},{2,6},{6,10},{10,14},{14,12},{12,8},{8,4},{4,0},{1,3},{3,7},... | collective-permute-start | bytes 393224 | tf_op jit(solution)/shard_map/ppermute | solution.py:297
  11.5 0.0 collective-permute-done.9.refs_2_
  11.5 0.4 %collective-permute-start.10 = (bf16[32,16,128]{2,1,0:T(8,128)(2,1)S(1)}, bf16[32,16,128]{2,1,0:T(8,128)(2,1)S(1)}, u32[]{:S(2)}, u32[]{:S(2)}) collective-permute-start(bf16[32,16,128]{2,1,0:T(8,128)(2,1)S(1)} %collective-permute-done.9.refs_2_), channel_id=1, source_target_pairs={{2,0},{6,2},{10,6},{14,10},{12,14},{8,12},{4,8},{0,4},{3,1},{7,3},... | collective-permute-start | bytes 393224 | tf_op jit(solution)/shard_map/ppermute | solution.py:300
  12.0 0.6 %collective-permute-done.5.refs_3_ = bf16[32,16,128]{2,1,0:T(8,128)(2,1)S(1)} collective-permute-done((bf16[32,16,128]{2,1,0:T(8,128)(2,1)S(1)}, bf16[32,16,128]{2,1,0:T(8,128)(2,1)S(1)}, u32[]{:S(2)}, u32[]{:S(2)}) %collective-permute-start.5) | collective-permute-done | bytes 131104 | tf_op jit(solution)/shard_map/ppermute | solution.py:297
  12.5 1.0 %collective-permute-start.6 = (bf16[32,16,128]{2,1,0:T(8,128)(2,1)S(1)}, bf16[32,16,128]{2,1,0:T(8,128)(2,1)S(1)}, u32[]{:S(2)}, u32[]{:S(2)}) collective-permute-start(bf16[32,16,128]{2,1,0:T(8,128)(2,1)S(1)} %collective-permute-done.5.refs_3_), channel_id=1, source_target_pairs={{0,2},{2,6},{6,10},{10,14},{14,12},{12,8},{8,4},{4,0},{1,3},{3,7},... | collective-permute-start | bytes 393224 | tf_op jit(solution)/shard_map/ppermute | solution.py:297
  13.6 0.0 collective-permute-done.1.refs_4_
  13.6 0.4 %collective-permute-start.2 = (bf16[32,16,128]{2,1,0:T(8,128)(2,1)S(1)}, bf16[32,16,128]{2,1,0:T(8,128)(2,1)S(1)}, u32[]{:S(2)}, u32[]{:S(2)}) collective-permute-start(bf16[32,16,128]{2,1,0:T(8,128)(2,1)S(1)} %collective-permute-done.1.refs_4_), channel_id=1, source_target_pairs={{2,0},{6,2},{10,6},{14,10},{12,14},{8,12},{4,8},{0,4},{3,1},{7,3},... | collective-permute-start | bytes 393224 | tf_op jit(solution)/shard_map/ppermute | solution.py:300
  14.0 1.4 %collective-permute-done.13.refs_3_ = bf16[32,16,128]{2,1,0:T(8,128)(2,1)S(1)} collective-permute-done((bf16[32,16,128]{2,1,0:T(8,128)(2,1)S(1)}, bf16[32,16,128]{2,1,0:T(8,128)(2,1)S(1)}, u32[]{:S(2)}, u32[]{:S(2)}) %collective-permute-start.13) | collective-permute-done | bytes 131104 | tf_op jit(solution)/shard_map/ppermute | solution.py:297
  15.4 1.0 %collective-permute-start.14 = (bf16[32,16,128]{2,1,0:T(8,128)(2,1)S(1)}, bf16[32,16,128]{2,1,0:T(8,128)(2,1)S(1)}, u32[]{:S(2)}, u32[]{:S(2)}) collective-permute-start(bf16[32,16,128]{2,1,0:T(8,128)(2,1)S(1)} %collective-permute-done.13.refs_3_), channel_id=1, source_target_pairs={{0,2},{2,6},{6,10},{10,14},{14,12},{12,8},{8,4},{4,0},{1,3},{3,7},... | collective-permute-start | bytes 393224 | tf_op jit(solution)/shard_map/ppermute | solution.py:297
  16.3 0.0 collective-permute-done.10.refs_4_
  16.3 0.5 %collective-permute-start.11 = (bf16[32,16,128]{2,1,0:T(8,128)(2,1)S(1)}, bf16[32,16,128]{2,1,0:T(8,128)(2,1)S(1)}, u32[]{:S(2)}, u32[]{:S(2)}) collective-permute-start(bf16[32,16,128]{2,1,0:T(8,128)(2,1)S(1)} %collective-permute-done.10.refs_4_), channel_id=1, source_target_pairs={{2,0},{6,2},{10,6},{14,10},{12,14},{8,12},{4,8},{0,4},{3,1},{7,3},... | collective-permute-start | bytes 393224 | tf_op jit(solution)/shard_map/ppermute | solution.py:300
  16.8 1.2 %collective-permute-done.6.refs_5_ = bf16[32,16,128]{2,1,0:T(8,128)(2,1)S(1)} collective-permute-done((bf16[32,16,128]{2,1,0:T(8,128)(2,1)S(1)}, bf16[32,16,128]{2,1,0:T(8,128)(2,1)S(1)}, u32[]{:S(2)}, u32[]{:S(2)}) %collective-permute-start.6) | collective-permute-done | bytes 131104 | tf_op jit(solution)/shard_map/ppermute | solution.py:297
  18.1 1.1 %collective-permute-start.7 = (bf16[32,16,128]{2,1,0:T(8,128)(2,1)S(1)}, bf16[32,16,128]{2,1,0:T(8,128)(2,1)S(1)}, u32[]{:S(2)}, u32[]{:S(2)}) collective-permute-start(bf16[32,16,128]{2,1,0:T(8,128)(2,1)S(1)} %collective-permute-done.6.refs_5_), channel_id=1, source_target_pairs={{0,2},{2,6},{6,10},{10,14},{14,12},{12,8},{8,4},{4,0},{1,3},{3,7},... | collective-permute-start | bytes 393224 | tf_op jit(solution)/shard_map/ppermute | solution.py:297
  19.1 0.0 collective-permute-done.2.refs_6_
  19.1 0.4 %collective-permute-start.3 = (bf16[32,16,128]{2,1,0:T(8,128)(2,1)S(1)}, bf16[32,16,128]{2,1,0:T(8,128)(2,1)S(1)}, u32[]{:S(2)}, u32[]{:S(2)}) collective-permute-start(bf16[32,16,128]{2,1,0:T(8,128)(2,1)S(1)} %collective-permute-done.2.refs_6_), channel_id=1, source_target_pairs={{2,0},{6,2},{10,6},{14,10},{12,14},{8,12},{4,8},{0,4},{3,1},{7,3},... | collective-permute-start | bytes 393224 | tf_op jit(solution)/shard_map/ppermute | solution.py:300
  19.5 1.5 %early.1.refs_8_ = f32[96,1152]{1,0:T(8,128)S(1)} custom-call(bf16[32,16,128]{2,1,0:T(8,128)(2,1)S(1)} %get-tuple-element.28.refs_0_, bf16[32,16,128]{2,1,0:T(8,128)(2,1)S(1)} %collective-permute-done.4.refs_1_, bf16[32,16,128]{2,1,0:T(8,128)(2,1)S(1)} %collective-permute-done.9.refs_2_, bf16[32,16,128]{2,1,0:T(8,128)(2,1)S(1)} %collective-permute-done.5.refs_3_, ...), custom_call_target="tpu_custom_call" | custom-call | flops 810000000 | bytes 1024 | tf_op jit(solution)/shard_map/early/pallas_call | solution.py:244
  21.0 0.0 collective-permute-done.14.refs_5_
  21.0 1.3 %late.1.sum_ref = f32[112,1152]{1,0:T(8,128)S(1)} custom-call(bf16[32,16,128]{2,1,0:T(8,128)(2,1)S(1)} %get-tuple-element.30.refs_0_, bf16[32,16,128]{2,1,0:T(8,128)(2,1)S(1)} %collective-permute-done.12.refs_1_, bf16[32,16,128]{2,1,0:T(8,128)(2,1)S(1)} %collective-permute-done.refs_2_, bf16[32,16,128]{2,1,0:T(8,128)(2,1)S(1)} %collective-permute-done.13.refs_3_, ...), custom_call_target="tpu_custom_call" | custom-call | flops 580000000 | bytes 1024 | tf_op jit(solution)/shard_map/late/pallas_call | solution.py:253
  22.4 0.0 collective-permute-done.11.chunk
  22.4 0.8 %third.1 = (f32[64,1152]{1,0:T(8,128)S(1)}, f32[72,1152]{1,0:T(8,128)S(1)}) custom-call(bf16[32,16,128]{2,1,0:T(8,128)(2,1)S(1)} %collective-permute-done.11.chunk, bf16[2,2,64,1024]{3,2,1,0:T(8,128)(2,1)S(1)} %get-tuple-element.26.p_ref.refs_6_.refs_7_, f32[8,1024]{1,0:T(8,128)S(1)} %get-tuple-element.29.n_ref, f32[112,1152]{1,0:T(8,128)S(1)} %late.1.sum_ref), custom_call_target="tpu_custom_call" | custom-call | flops 230000000 | bytes 1024 | tf_op jit(solution)/shard_map/third/pallas_call | solution.py:262
  23.2 2.8 %collective-permute-start.15 = (f32[72,1152]{1,0:T(8,128)S(1)}, f32[72,1152]{1,0:T(8,128)S(1)}, u32[]{:S(2)}, u32[]{:S(2)}) collective-permute-start(f32[72,1152]{1,0:T(8,128)S(1)} %get-tuple-element.32), channel_id=1, source_target_pairs={{0,1},{1,0},{2,3},{3,2},{4,5},{5,4},{6,7},{7,6},{8,9},{9,8},{10,11... | collective-permute-start | bytes 995336 | tf_op jit(solution)/shard_map/ppermute | solution.py:240
  26.0 0.0 collective-permute-done.7.chunk
  26.0 0.7 %last.2.refs_0_ = f32[16,1152]{1,0:T(8,128)S(1)} custom-call(bf16[32,16,128]{2,1,0:T(8,128)(2,1)S(1)} %collective-permute-done.7.chunk, bf16[2,2,64,1024]{3,2,1,0:T(8,128)(2,1)S(1)} %get-tuple-element.26.p_ref.refs_6_.refs_7_), custom_call_target="tpu_custom_call" | custom-call | flops 460000000 | bytes 1024 | tf_op jit(solution)/shard_map/last/pallas_call | solution.py:345
  26.7 0.0 collective-permute-done.3.chunk
  26.7 0.7 %last.3.own_ref = f32[16,1152]{1,0:T(8,128)S(1)} custom-call(bf16[32,16,128]{2,1,0:T(8,128)(2,1)S(1)} %collective-permute-done.3.chunk, bf16[2,2,64,1024]{3,2,1,0:T(8,128)(2,1)S(1)} %get-tuple-element.26.p_ref.refs_6_.refs_7_, f32[16,1152]{1,0:T(8,128)S(1)} %last.2.refs_0_), custom_call_target="tpu_custom_call" | custom-call | flops 10000000000 | bytes 4194304 | tf_op jit(solution)/shard_map/last/pallas_call | solution.py:345
  27.4 0.4 %collective-permute-start.8 = (f32[16,1152]{1,0:T(8,128)S(1)}, f32[16,1152]{1,0:T(8,128)S(1)}, u32[]{:S(2)}, u32[]{:S(2)}) collective-permute-start(f32[16,1152]{1,0:T(8,128)S(1)} %last.3.own_ref), channel_id=1, source_target_pairs={{0,1},{1,0},{2,3},{3,2},{4,5},{5,4},{6,7},{7,6},{8,9},{9,8},{10,11... | collective-permute-start | bytes 221192 | tf_op jit(solution)/shard_map/ppermute | solution.py:240
  27.8 0.0 collective-permute-done.15.far_ref
  27.8 0.8 %most.1 = (f32[64,1024]{1,0:T(8,128)}, f32[8,1024]{1,0:T(8,128)S(1)}) custom-call(f32[64,1152]{1,0:T(8,128)S(1)} %get-tuple-element.31.keep_ref, f32[72,1152]{1,0:T(8,128)S(1)} %collective-permute-done.15.far_ref, f32[8,1024]{1,0:T(8,128)S(1)} %get-tuple-element.29.n_ref), custom_call_target="tpu_custom_call" | custom-call | flops 10000000000 | bytes 4194304 | tf_op jit(solution)/shard_map/most/pallas_call | solution.py:277
  28.6 0.1 collective-permute-done.8.far_ref
  28.7 0.7 %rest.1 = f32[64,1024]{1,0:T(8,128)} custom-call(f32[16,1152]{1,0:T(8,128)S(1)} %last.3.own_ref, f32[16,1152]{1,0:T(8,128)S(1)} %collective-permute-done.8.far_ref, f32[8,1024]{1,0:T(8,128)S(1)} %get-tuple-element.33.s_ref, f32[64,1024]{1,0:T(8,128)} %get-tuple-element.34.most_ref), custom_call_target="tpu_custom_call", output_to_operand_aliasing={{}: (3, {})} | custom-call | tf_op jit(solution)/shard_map/rest/pallas_call | solution.py:356
  (1 shorter events, 0.0 us)
Async XLA Ops:
  1.3 5.4 %collective-permute-start.4 = (bf16[32,16,128]{2,1,0:T(8,128)(2,1)S(1)}, bf16[32,16,128]{2,1,0:T(8,128)(2,1)S(1)}, u32[]{:S(2)}, u32[]{:S(2)}) collective-permute-start(bf16[32,16,128]{2,1,0:T(8,128)(2,1)S(1)} %get-tuple-element.28.refs_0_), channel_id=1, source_target_pairs={{0,2},{2,6},{6,10},{10,14},{14,12},{12,8},{8,4},{4,0},{1,3},{3,7},... | collective-permute-start | bytes 393224 | tf_op jit(solution)/shard_map/ppermute | solution.py:297
  3.4 4.5 %collective-permute-start = (bf16[32,16,128]{2,1,0:T(8,128)(2,1)S(1)}, bf16[32,16,128]{2,1,0:T(8,128)(2,1)S(1)}, u32[]{:S(2)}, u32[]{:S(2)}) collective-permute-start(bf16[32,16,128]{2,1,0:T(8,128)(2,1)S(1)} %get-tuple-element.30.refs_0_), channel_id=1, source_target_pairs={{2,0},{6,2},{10,6},{14,10},{12,14},{8,12},{4,8},{0,4},{3,1},{7,3},... | collective-permute-start | bytes 393224 | tf_op jit(solution)/shard_map/ppermute | solution.py:300
  4.9 5.6 %collective-permute-start.12 = (bf16[32,16,128]{2,1,0:T(8,128)(2,1)S(1)}, bf16[32,16,128]{2,1,0:T(8,128)(2,1)S(1)}, u32[]{:S(2)}, u32[]{:S(2)}) collective-permute-start(bf16[32,16,128]{2,1,0:T(8,128)(2,1)S(1)} %get-tuple-element.30.refs_0_), channel_id=1, source_target_pairs={{0,2},{2,6},{6,10},{10,14},{14,12},{12,8},{8,4},{4,0},{1,3},{3,7},... | collective-permute-start | bytes 393224 | tf_op jit(solution)/shard_map/ppermute | solution.py:297
  6.3 5.2 %collective-permute-start.9 = (bf16[32,16,128]{2,1,0:T(8,128)(2,1)S(1)}, bf16[32,16,128]{2,1,0:T(8,128)(2,1)S(1)}, u32[]{:S(2)}, u32[]{:S(2)}) collective-permute-start(bf16[32,16,128]{2,1,0:T(8,128)(2,1)S(1)} %get-tuple-element.28.refs_0_), channel_id=1, source_target_pairs={{2,0},{6,2},{10,6},{14,10},{12,14},{8,12},{4,8},{0,4},{3,1},{7,3},... | collective-permute-start | bytes 393224 | tf_op jit(solution)/shard_map/ppermute | solution.py:300
  6.7 5.9 %collective-permute-start.5 = (bf16[32,16,128]{2,1,0:T(8,128)(2,1)S(1)}, bf16[32,16,128]{2,1,0:T(8,128)(2,1)S(1)}, u32[]{:S(2)}, u32[]{:S(2)}) collective-permute-start(bf16[32,16,128]{2,1,0:T(8,128)(2,1)S(1)} %collective-permute-done.4.refs_1_), channel_id=1, source_target_pairs={{0,2},{2,6},{6,10},{10,14},{14,12},{12,8},{8,4},{4,0},{1,3},{3,7},... | collective-permute-start | bytes 393224 | tf_op jit(solution)/shard_map/ppermute | solution.py:297
  7.9 5.7 %collective-permute-start.1 = (bf16[32,16,128]{2,1,0:T(8,128)(2,1)S(1)}, bf16[32,16,128]{2,1,0:T(8,128)(2,1)S(1)}, u32[]{:S(2)}, u32[]{:S(2)}) collective-permute-start(bf16[32,16,128]{2,1,0:T(8,128)(2,1)S(1)} %collective-permute-done.refs_2_), channel_id=1, source_target_pairs={{2,0},{6,2},{10,6},{14,10},{12,14},{8,12},{4,8},{0,4},{3,1},{7,3},... | collective-permute-start | bytes 393224 | tf_op jit(solution)/shard_map/ppermute | solution.py:300
  10.5 4.9 %collective-permute-start.13 = (bf16[32,16,128]{2,1,0:T(8,128)(2,1)S(1)}, bf16[32,16,128]{2,1,0:T(8,128)(2,1)S(1)}, u32[]{:S(2)}, u32[]{:S(2)}) collective-permute-start(bf16[32,16,128]{2,1,0:T(8,128)(2,1)S(1)} %collective-permute-done.12.refs_1_), channel_id=1, source_target_pairs={{0,2},{2,6},{6,10},{10,14},{14,12},{12,8},{8,4},{4,0},{1,3},{3,7},... | collective-permute-start | bytes 393224 | tf_op jit(solution)/shard_map/ppermute | solution.py:297
  11.5 4.8 %collective-permute-start.10 = (bf16[32,16,128]{2,1,0:T(8,128)(2,1)S(1)}, bf16[32,16,128]{2,1,0:T(8,128)(2,1)S(1)}, u32[]{:S(2)}, u32[]{:S(2)}) collective-permute-start(bf16[32,16,128]{2,1,0:T(8,128)(2,1)S(1)} %collective-permute-done.9.refs_2_), channel_id=1, source_target_pairs={{2,0},{6,2},{10,6},{14,10},{12,14},{8,12},{4,8},{0,4},{3,1},{7,3},... | collective-permute-start | bytes 393224 | tf_op jit(solution)/shard_map/ppermute | solution.py:300
  12.5 5.5 %collective-permute-start.6 = (bf16[32,16,128]{2,1,0:T(8,128)(2,1)S(1)}, bf16[32,16,128]{2,1,0:T(8,128)(2,1)S(1)}, u32[]{:S(2)}, u32[]{:S(2)}) collective-permute-start(bf16[32,16,128]{2,1,0:T(8,128)(2,1)S(1)} %collective-permute-done.5.refs_3_), channel_id=1, source_target_pairs={{0,2},{2,6},{6,10},{10,14},{14,12},{12,8},{8,4},{4,0},{1,3},{3,7},... | collective-permute-start | bytes 393224 | tf_op jit(solution)/shard_map/ppermute | solution.py:297
  13.6 5.6 %collective-permute-start.2 = (bf16[32,16,128]{2,1,0:T(8,128)(2,1)S(1)}, bf16[32,16,128]{2,1,0:T(8,128)(2,1)S(1)}, u32[]{:S(2)}, u32[]{:S(2)}) collective-permute-start(bf16[32,16,128]{2,1,0:T(8,128)(2,1)S(1)} %collective-permute-done.1.refs_4_), channel_id=1, source_target_pairs={{2,0},{6,2},{10,6},{14,10},{12,14},{8,12},{4,8},{0,4},{3,1},{7,3},... | collective-permute-start | bytes 393224 | tf_op jit(solution)/shard_map/ppermute | solution.py:300
  15.4 5.6 %collective-permute-start.14 = (bf16[32,16,128]{2,1,0:T(8,128)(2,1)S(1)}, bf16[32,16,128]{2,1,0:T(8,128)(2,1)S(1)}, u32[]{:S(2)}, u32[]{:S(2)}) collective-permute-start(bf16[32,16,128]{2,1,0:T(8,128)(2,1)S(1)} %collective-permute-done.13.refs_3_), channel_id=1, source_target_pairs={{0,2},{2,6},{6,10},{10,14},{14,12},{12,8},{8,4},{4,0},{1,3},{3,7},... | collective-permute-start | bytes 393224 | tf_op jit(solution)/shard_map/ppermute | solution.py:297
  16.3 6.0 %collective-permute-start.11 = (bf16[32,16,128]{2,1,0:T(8,128)(2,1)S(1)}, bf16[32,16,128]{2,1,0:T(8,128)(2,1)S(1)}, u32[]{:S(2)}, u32[]{:S(2)}) collective-permute-start(bf16[32,16,128]{2,1,0:T(8,128)(2,1)S(1)} %collective-permute-done.10.refs_4_), channel_id=1, source_target_pairs={{2,0},{6,2},{10,6},{14,10},{12,14},{8,12},{4,8},{0,4},{3,1},{7,3},... | collective-permute-start | bytes 393224 | tf_op jit(solution)/shard_map/ppermute | solution.py:300
  18.1 7.9 %collective-permute-start.7 = (bf16[32,16,128]{2,1,0:T(8,128)(2,1)S(1)}, bf16[32,16,128]{2,1,0:T(8,128)(2,1)S(1)}, u32[]{:S(2)}, u32[]{:S(2)}) collective-permute-start(bf16[32,16,128]{2,1,0:T(8,128)(2,1)S(1)} %collective-permute-done.6.refs_5_), channel_id=1, source_target_pairs={{0,2},{2,6},{6,10},{10,14},{14,12},{12,8},{8,4},{4,0},{1,3},{3,7},... | collective-permute-start | bytes 393224 | tf_op jit(solution)/shard_map/ppermute | solution.py:297
  19.1 7.5 %collective-permute-start.3 = (bf16[32,16,128]{2,1,0:T(8,128)(2,1)S(1)}, bf16[32,16,128]{2,1,0:T(8,128)(2,1)S(1)}, u32[]{:S(2)}, u32[]{:S(2)}) collective-permute-start(bf16[32,16,128]{2,1,0:T(8,128)(2,1)S(1)} %collective-permute-done.2.refs_6_), channel_id=1, source_target_pairs={{2,0},{6,2},{10,6},{14,10},{12,14},{8,12},{4,8},{0,4},{3,1},{7,3},... | collective-permute-start | bytes 393224 | tf_op jit(solution)/shard_map/ppermute | solution.py:300
  23.2 4.6 %collective-permute-start.15 = (f32[72,1152]{1,0:T(8,128)S(1)}, f32[72,1152]{1,0:T(8,128)S(1)}, u32[]{:S(2)}, u32[]{:S(2)}) collective-permute-start(f32[72,1152]{1,0:T(8,128)S(1)} %get-tuple-element.32), channel_id=1, source_target_pairs={{0,1},{1,0},{2,3},{3,2},{4,5},{5,4},{6,7},{7,6},{8,9},{9,8},{10,11... | collective-permute-start | bytes 995336 | tf_op jit(solution)/shard_map/ppermute | solution.py:240
  27.4 1.3 %collective-permute-start.8 = (f32[16,1152]{1,0:T(8,128)S(1)}, f32[16,1152]{1,0:T(8,128)S(1)}, u32[]{:S(2)}, u32[]{:S(2)}) collective-permute-start(f32[16,1152]{1,0:T(8,128)S(1)} %last.3.own_ref), channel_id=1, source_target_pairs={{0,1},{1,0},{2,3},{3,2},{4,5},{5,4},{6,7},{7,6},{8,9},{9,8},{10,11... | collective-permute-start | bytes 221192 | tf_op jit(solution)/shard_map/ppermute | solution.py:240

commit v8 on v7

--- a/solution.py
+++ b/solution.py
@@ -12,6 +12,9 @@
 GROUP = 16
 VMEM = pl.BlockSpec(memory_space=pltpu.VMEM)
 HBM = pl.BlockSpec(memory_space=pltpu.HBM)
+
+
+SHORT = pl.CostEstimate(flops=10**6, bytes_accessed=1024, transcendentals=0)
 
 
 def cover(share):
@@ -111,9 +114,21 @@
         o_ref[:, lanes] = acc
 
 
+def core_kernel(core, kept, part, parts, modules, rank, chunk, p_ref, *refs):
+    def run():
+        last_kernel(part, parts, modules, rank, chunk, p_ref, *(refs[1:] if kept else refs))
+
+    if core is None:
+        run()
+    else:
+        pl.when((lax.axis_index("proj") == 0) == (core == 0))(run)
+
+
 def products(blocks, part, parts, modules, rank, p_ref, lanes):
     own = rank // 2 // parts
     step = min(4, own)
+    used = len(blocks) * GROUP
+    blocks = (list(blocks) * 8)[: -(-len(blocks) // 8) * 8]
     acc = jnp.zeros((len(blocks) * GROUP, lanes.stop - lanes.start), jnp.float32)
     for m in range(modules):
         grad = p_ref[1, m, :, lanes]
@@ -128,7 +143,7 @@
                 [grad * p_ref[0, m, row + s : row + s + 1, lanes] for s in range(2 * step)], axis=0
             )
             acc += jnp.dot(left, right, preferred_element_type=jnp.float32)
-    return acc
+    return acc[:used]
 
 
 def tiles(tokens):
@@ -322,9 +337,9 @@
         for step in range(1, ex // 2):
             first = (up(below[0]), down(above[0]))
             second = (up(below[1]), down(above[1]))
-            if step == 1:
-                arrived, factors = lax.optimization_barrier((first[0], factors))
-                first = (arrived, first[1])
+            if step == 2:
+                arrived, factors = lax.optimization_barrier((second[0], factors))
+                second = (arrived, second[1])
             below, above = (first[0], second[0]), (first[1], second[1])
             blocks += [below, above]
             steps += [-step, step]
@@ -338,21 +353,24 @@
             return index_at(place_of(lax.axis_index("ex"), ex) + ex // 2, ex)
 
         keep, send = bulk(blocks, ring, factors, norm)
+        def scored(part, core, cost, *before):
+            kept = part == 0 and bool(before)
+            return pl.pallas_call(
+                functools.partial(core_kernel, core, kept, part, 2, modules, rank),
+                out_shape=jax.ShapeDtypeStruct((GROUP, wide), jnp.float32),
+                in_specs=[VMEM] * (2 + len(before)),
+                out_specs=VMEM,
+                input_output_aliases={2: 0} if kept else {},
+                compiler_params=PARAMS,
+                cost_estimate=cost,
+                name="last",
+            )(across[part], factors, *before)
+
+        mine = scored(0, 1, SHORT)
+        send, mine = lax.optimization_barrier((send, mine))
         out, scale = most(keep, swapped(send), norm)
-        mine = ()
-        for part, chunk in enumerate(across):
-            mine = (
-                pl.pallas_call(
-                    functools.partial(last_kernel, part, len(across), modules, rank),
-                    out_shape=jax.ShapeDtypeStruct((GROUP, wide), jnp.float32),
-                    in_specs=[VMEM] * (2 + len(mine)),
-                    out_specs=VMEM,
-                    compiler_params=PARAMS,
-                    cost_estimate=LONG if part else cover(0.46),
-                    name="last",
-                )(chunk, factors, *mine),
-            )
-        (mine,) = mine
+        mine = scored(0, 0, cover(0.46), mine)
+        mine = scored(1, None, LONG, mine)
         out = pl.pallas_call(
             functools.partial(rest_kernel, width, opposite),
             out_shape=jax.ShapeDtypeStruct((columns, tokens), jnp.float32),

time: 29.6 us -> 29.6 us (level)
    ppermute x7, waiting for transfers between devices: 5.71 us -> 6.02 us  [up(): return lax.ppermute(x, 'ex', up_pairs)]
    pallas_call x2 -> x3, Pallas kernels: 1.39 us -> 1.38 us  [scored(): pl.pallas_call(functools.partial(core_kernel, core, kept, part, 2, module...]
  transfers between devices with their start and end apart: 16 -> 16, of which waited for: 6 -> 7; matrix products, arithmetic and copies ran while one was open for 0% -> 0% of each run, Pallas kernels for 25% -> 24%
where the time goes in v8:
time: 29.6 us; the launch traced here: 29.4 us
  starting transfers between devices  14.2 us (48%)
  Pallas kernels  8.97 us (30%)
  waiting for transfers between devices  6.13 us (21%)
    ppermute x7, starting transfers between devices, up(): return lax.ppermute(x, 'ex', up_pairs)  8.88 us
    ppermute x7, waiting for transfers between devices, up(): return lax.ppermute(x, 'ex', up_pairs)  6.02 us
    ppermute x2, starting transfers between devices, swapped(): return lax.ppermute(x, 'proj', [(i, (i + 1) % proj) for i in range(proj)])  3.16 us
    ppermute x7, starting transfers between devices, down(): return lax.ppermute(x, 'ex', down_pairs)  2.22 us
    pallas_call x2, Pallas kernels, token_work(): pl.pallas_call(functools.partial(token_kernel, modules, rank, core), out_...  1.42 us
    pallas_call x3, Pallas kernels, scored(): pl.pallas_call(functools.partial(core_kernel, core, kept, part, 2, module...  1.38 us
    pallas_call x1, Pallas kernels, bulk(): pl.pallas_call(functools.partial(late_kernel, count, parts, modules, rank...  1.27 us
    pallas_call x1, Pallas kernels, bulk(): pl.pallas_call(functools.partial(early_kernel, count - 1, parts, modules,...  1.27 us
  transfers between devices with their start and end apart: 16, of which 7 were waited for; matrix products, arithmetic and copies ran while one was open for 0% of the time, Pallas kernels for 24%

profile of v8, /device:TPU:1, one launch (start us, length us, event | category | flops | bytes accessed | tf_op | source)
XLA Modules:
  0.0 29.4 jit_solution(14193442716069817840)
XLA Ops:
  0.0 1.3 %queries.1 = (bf16[32,16,128]{2,1,0:T(8,128)(2,1)S(1)}, bf16[32,16,128]{2,1,0:T(8,128)(2,1)S(1)}) custom-call(f32[16,64,128]{2,1,0:T(8,128)} %bitcast.9), custom_call_target="tpu_custom_call" | custom-call | tf_op jit(solution)/shard_map/queries/pallas_call | solution.py:320
  1.3 2.1 %collective-permute-start.6 = (bf16[32,16,128]{2,1,0:T(8,128)(2,1)S(1)}, bf16[32,16,128]{2,1,0:T(8,128)(2,1)S(1)}, u32[]{:S(2)}, u32[]{:S(2)}) collective-permute-start(bf16[32,16,128]{2,1,0:T(8,128)(2,1)S(1)} %get-tuple-element.30.refs_0_), channel_id=1, source_target_pairs={{0,2},{2,6},{6,10},{10,14},{14,12},{12,8},{8,4},{4,0},{1,3},{3,7},... | collective-permute-start | bytes 393224 | tf_op jit(solution)/shard_map/ppermute | solution.py:312
  3.4 0.2 collective-permute-start
  3.5 1.4 %tokens.2 = (bf16[2,2,64,1024]{3,2,1,0:T(8,128)(2,1)S(1)}, f32[8,1024]{1,0:T(8,128)S(1)}) custom-call(bf16[2048,128]{1,0:T(8,128)(2,1)} %bitcast.7), custom_call_target="tpu_custom_call" | custom-call | tf_op jit(solution)/shard_map/tokens/pallas_call | solution.py:236
  4.9 1.4 %collective-permute-start.4 = (bf16[32,16,128]{2,1,0:T(8,128)(2,1)S(1)}, bf16[32,16,128]{2,1,0:T(8,128)(2,1)S(1)}, u32[]{:S(2)}, u32[]{:S(2)}) collective-permute-start(bf16[32,16,128]{2,1,0:T(8,128)(2,1)S(1)} %get-tuple-element.25.refs_0_), channel_id=1, source_target_pairs={{0,2},{2,6},{6,10},{10,14},{14,12},{12,8},{8,4},{4,0},{1,3},{3,7},... | collective-permute-start | bytes 393224 | tf_op jit(solution)/shard_map/ppermute | solution.py:312
  6.3 0.2 collective-permute-start.10
  6.5 0.2 collective-permute-done.6.refs_1_
  6.7 1.1 %collective-permute-start.7 = (bf16[32,16,128]{2,1,0:T(8,128)(2,1)S(1)}, bf16[32,16,128]{2,1,0:T(8,128)(2,1)S(1)}, u32[]{:S(2)}, u32[]{:S(2)}) collective-permute-start(bf16[32,16,128]{2,1,0:T(8,128)(2,1)S(1)} %collective-permute-done.6.refs_1_), channel_id=1, source_target_pairs={{0,2},{2,6},{6,10},{10,14},{14,12},{12,8},{8,4},{4,0},{1,3},{3,7},... | collective-permute-start | bytes 393224 | tf_op jit(solution)/shard_map/ppermute | solution.py:312
  7.8 0.0 collective-permute-done.refs_2_
  7.8 0.3 %collective-permute-start.1 = (bf16[32,16,128]{2,1,0:T(8,128)(2,1)S(1)}, bf16[32,16,128]{2,1,0:T(8,128)(2,1)S(1)}, u32[]{:S(2)}, u32[]{:S(2)}) collective-permute-start(bf16[32,16,128]{2,1,0:T(8,128)(2,1)S(1)} %collective-permute-done.refs_2_), channel_id=1, source_target_pairs={{2,0},{6,2},{10,6},{14,10},{12,14},{8,12},{4,8},{0,4},{3,1},{7,3},... | collective-permute-start | bytes 393224 | tf_op jit(solution)/shard_map/ppermute | solution.py:315
  8.1 2.3 %collective-permute-done.4.refs_1_ = bf16[32,16,128]{2,1,0:T(8,128)(2,1)S(1)} collective-permute-done((bf16[32,16,128]{2,1,0:T(8,128)(2,1)S(1)}, bf16[32,16,128]{2,1,0:T(8,128)(2,1)S(1)}, u32[]{:S(2)}, u32[]{:S(2)}) %collective-permute-start.4) | collective-permute-done | bytes 131104 | tf_op jit(solution)/shard_map/ppermute | solution.py:312
  10.5 1.0 %collective-permute-start.5 = (bf16[32,16,128]{2,1,0:T(8,128)(2,1)S(1)}, bf16[32,16,128]{2,1,0:T(8,128)(2,1)S(1)}, u32[]{:S(2)}, u32[]{:S(2)}) collective-permute-start(bf16[32,16,128]{2,1,0:T(8,128)(2,1)S(1)} %collective-permute-done.4.refs_1_), channel_id=1, source_target_pairs={{0,2},{2,6},{6,10},{10,14},{14,12},{12,8},{8,4},{4,0},{1,3},{3,7},... | collective-permute-start | bytes 393224 | tf_op jit(solution)/shard_map/ppermute | solution.py:312
  11.5 0.0 collective-permute-done.10.refs_2_
  11.5 0.4 %collective-permute-start.11 = (bf16[32,16,128]{2,1,0:T(8,128)(2,1)S(1)}, bf16[32,16,128]{2,1,0:T(8,128)(2,1)S(1)}, u32[]{:S(2)}, u32[]{:S(2)}) collective-permute-start(bf16[32,16,128]{2,1,0:T(8,128)(2,1)S(1)} %collective-permute-done.10.refs_2_), channel_id=1, source_target_pairs={{2,0},{6,2},{10,6},{14,10},{12,14},{8,12},{4,8},{0,4},{3,1},{7,3},... | collective-permute-start | bytes 393224 | tf_op jit(solution)/shard_map/ppermute | solution.py:315
  12.0 0.7 %collective-permute-done.7.refs_3_ = bf16[32,16,128]{2,1,0:T(8,128)(2,1)S(1)} collective-permute-done((bf16[32,16,128]{2,1,0:T(8,128)(2,1)S(1)}, bf16[32,16,128]{2,1,0:T(8,128)(2,1)S(1)}, u32[]{:S(2)}, u32[]{:S(2)}) %collective-permute-start.7) | collective-permute-done | bytes 131104 | tf_op jit(solution)/shard_map/ppermute | solution.py:312
  12.7 1.3 %collective-permute-start.8 = (bf16[32,16,128]{2,1,0:T(8,128)(2,1)S(1)}, bf16[32,16,128]{2,1,0:T(8,128)(2,1)S(1)}, u32[]{:S(2)}, u32[]{:S(2)}) collective-permute-start(bf16[32,16,128]{2,1,0:T(8,128)(2,1)S(1)} %collective-permute-done.7.refs_3_), channel_id=1, source_target_pairs={{0,2},{2,6},{6,10},{10,14},{14,12},{12,8},{8,4},{4,0},{1,3},{3,7},... | collective-permute-start | bytes 393224 | tf_op jit(solution)/shard_map/ppermute | solution.py:312
  13.9 0.0 collective-permute-done.1.refs_4_
  13.9 0.2 collective-permute-start.2
  14.2 1.2 %collective-permute-done.5.refs_3_ = bf16[32,16,128]{2,1,0:T(8,128)(2,1)S(1)} collective-permute-done((bf16[32,16,128]{2,1,0:T(8,128)(2,1)S(1)}, bf16[32,16,128]{2,1,0:T(8,128)(2,1)S(1)}, u32[]{:S(2)}, u32[]{:S(2)}) %collective-permute-start.5) | collective-permute-done | bytes 131104 | tf_op jit(solution)/shard_map/ppermute | solution.py:312
  15.4 1.0 %collective-permute-start.13 = (bf16[32,16,128]{2,1,0:T(8,128)(2,1)S(1)}, bf16[32,16,128]{2,1,0:T(8,128)(2,1)S(1)}, u32[]{:S(2)}, u32[]{:S(2)}) collective-permute-start(bf16[32,16,128]{2,1,0:T(8,128)(2,1)S(1)} %collective-permute-done.5.refs_3_), channel_id=1, source_target_pairs={{0,2},{2,6},{6,10},{10,14},{14,12},{12,8},{8,4},{4,0},{1,3},{3,7},... | collective-permute-start | bytes 393224 | tf_op jit(solution)/shard_map/ppermute | solution.py:312
  16.3 0.0 collective-permute-done.11.refs_4_
  16.3 0.5 %collective-permute-start.12 = (bf16[32,16,128]{2,1,0:T(8,128)(2,1)S(1)}, bf16[32,16,128]{2,1,0:T(8,128)(2,1)S(1)}, u32[]{:S(2)}, u32[]{:S(2)}) collective-permute-start(bf16[32,16,128]{2,1,0:T(8,128)(2,1)S(1)} %collective-permute-done.11.refs_4_), channel_id=1, source_target_pairs={{2,0},{6,2},{10,6},{14,10},{12,14},{8,12},{4,8},{0,4},{3,1},{7,3},... | collective-permute-start | bytes 393224 | tf_op jit(solution)/shard_map/ppermute | solution.py:315
  16.8 1.2 %collective-permute-done.8.refs_5_ = bf16[32,16,128]{2,1,0:T(8,128)(2,1)S(1)} collective-permute-done((bf16[32,16,128]{2,1,0:T(8,128)(2,1)S(1)}, bf16[32,16,128]{2,1,0:T(8,128)(2,1)S(1)}, u32[]{:S(2)}, u32[]{:S(2)}) %collective-permute-start.8) | collective-permute-done | bytes 131104 | tf_op jit(solution)/shard_map/ppermute | solution.py:312
  18.1 1.0 %collective-permute-start.9 = (bf16[32,16,128]{2,1,0:T(8,128)(2,1)S(1)}, bf16[32,16,128]{2,1,0:T(8,128)(2,1)S(1)}, u32[]{:S(2)}, u32[]{:S(2)}) collective-permute-start(bf16[32,16,128]{2,1,0:T(8,128)(2,1)S(1)} %collective-permute-done.8.refs_5_), channel_id=1, source_target_pairs={{0,2},{2,6},{6,10},{10,14},{14,12},{12,8},{8,4},{4,0},{1,3},{3,7},... | collective-permute-start | bytes 393224 | tf_op jit(solution)/shard_map/ppermute | solution.py:312
  19.1 0.0 collective-permute-done.2.refs_6_
  19.1 0.4 %collective-permute-start.3 = (bf16[32,16,128]{2,1,0:T(8,128)(2,1)S(1)}, bf16[32,16,128]{2,1,0:T(8,128)(2,1)S(1)}, u32[]{:S(2)}, u32[]{:S(2)}) collective-permute-start(bf16[32,16,128]{2,1,0:T(8,128)(2,1)S(1)} %collective-permute-done.2.refs_6_), channel_id=1, source_target_pairs={{2,0},{6,2},{10,6},{14,10},{12,14},{8,12},{4,8},{0,4},{3,1},{7,3},... | collective-permute-start | bytes 393224 | tf_op jit(solution)/shard_map/ppermute | solution.py:315
  19.5 1.3 %early.1.refs_8_ = f32[96,1152]{1,0:T(8,128)S(1)} custom-call(bf16[32,16,128]{2,1,0:T(8,128)(2,1)S(1)} %get-tuple-element.30.refs_0_, bf16[32,16,128]{2,1,0:T(8,128)(2,1)S(1)} %collective-permute-done.6.refs_1_, bf16[32,16,128]{2,1,0:T(8,128)(2,1)S(1)} %collective-permute-done.10.refs_2_, bf16[32,16,128]{2,1,0:T(8,128)(2,1)S(1)} %collective-permute-done.7.refs_3_, ...), custom_call_target="tpu_custom_call" | custom-call | flops 810000000 | bytes 1024 | tf_op jit(solution)/shard_map/early/pallas_call | solution.py:259
  20.8 0.0 collective-permute-done.13.refs_5_
  20.8 1.3 %late.1.sum_ref = f32[112,1152]{1,0:T(8,128)S(1)} custom-call(bf16[32,16,128]{2,1,0:T(8,128)(2,1)S(1)} %get-tuple-element.25.refs_0_, bf16[32,16,128]{2,1,0:T(8,128)(2,1)S(1)} %collective-permute-done.4.refs_1_, bf16[32,16,128]{2,1,0:T(8,128)(2,1)S(1)} %collective-permute-done.refs_2_, bf16[32,16,128]{2,1,0:T(8,128)(2,1)S(1)} %collective-permute-done.5.refs_3_, ...), custom_call_target="tpu_custom_call" | custom-call | flops 580000000 | bytes 1024 | tf_op jit(solution)/shard_map/late/pallas_call | solution.py:268
  22.1 0.0 collective-permute-done.12.chunk
  22.1 0.8 %third.1 = (f32[64,1152]{1,0:T(8,128)S(1)}, f32[72,1152]{1,0:T(8,128)S(1)}) custom-call(bf16[32,16,128]{2,1,0:T(8,128)(2,1)S(1)} %collective-permute-done.12.chunk, bf16[2,2,64,1024]{3,2,1,0:T(8,128)(2,1)S(1)} %get-tuple-element.29.refs_6_.refs_7_.p_ref, f32[8,1024]{1,0:T(8,128)S(1)} %get-tuple-element.31.n_ref, f32[112,1152]{1,0:T(8,128)S(1)} %late.1.sum_ref), custom_call_target="tpu_custom_call" | custom-call | flops 230000000 | bytes 1024 | tf_op jit(solution)/shard_map/third/pallas_call | solution.py:277
  22.9 0.3 %collective-permute-done.9.chunk = bf16[32,16,128]{2,1,0:T(8,128)(2,1)S(1)} collective-permute-done((bf16[32,16,128]{2,1,0:T(8,128)(2,1)S(1)}, bf16[32,16,128]{2,1,0:T(8,128)(2,1)S(1)}, u32[]{:S(2)}, u32[]{:S(2)}) %collective-permute-start.9) | collective-permute-done | bytes 131104 | tf_op jit(solution)/shard_map/ppermute | solution.py:312
  23.2 0.7 %last.3.refs_0_ = f32[16,1152]{1,0:T(8,128)S(1)} custom-call(bf16[32,16,128]{2,1,0:T(8,128)(2,1)S(1)} %collective-permute-done.9.chunk, bf16[2,2,64,1024]{3,2,1,0:T(8,128)(2,1)S(1)} %get-tuple-element.29.refs_6_.refs_7_.p_ref), custom_call_target="tpu_custom_call" | custom-call | flops 1000000 | bytes 1024 | tf_op jit(solution)/shard_map/last/pallas_call | solution.py:358
  23.9 2.0 %collective-permute-start.15 = (f32[72,1152]{1,0:T(8,128)S(1)}, f32[72,1152]{1,0:T(8,128)S(1)}, u32[]{:S(2)}, u32[]{:S(2)}) collective-permute-start(f32[72,1152]{1,0:T(8,128)S(1)} %get-tuple-element.36), channel_id=1, source_target_pairs={{0,1},{1,0},{2,3},{3,2},{4,5},{5,4},{6,7},{7,6},{8,9},{9,8},{10,11... | collective-permute-start | bytes 995336 | tf_op jit(solution)/shard_map/ppermute | solution.py:255
  25.9 0.0 collective-permute-done.3.chunk
  25.9 0.7 %last.5.own_ref = f32[16,1152]{1,0:T(8,128)S(1)} custom-call(bf16[32,16,128]{2,1,0:T(8,128)(2,1)S(1)} %collective-permute-done.3.chunk, bf16[2,2,64,1024]{3,2,1,0:T(8,128)(2,1)S(1)} %get-tuple-element.29.refs_6_.refs_7_.p_ref, f32[16,1152]{1,0:T(8,128)S(1)} %last.4.refs_0_), custom_call_target="tpu_custom_call" | custom-call | flops 10000000000 | bytes 4194304 | tf_op jit(solution)/shard_map/last/pallas_call | solution.py:358
  26.6 1.2 %collective-permute-start.14 = (f32[16,1152]{1,0:T(8,128)S(1)}, f32[16,1152]{1,0:T(8,128)S(1)}, u32[]{:S(2)}, u32[]{:S(2)}) collective-permute-start(f32[16,1152]{1,0:T(8,128)S(1)} %last.5.own_ref), channel_id=1, source_target_pairs={{0,1},{1,0},{2,3},{3,2},{4,5},{5,4},{6,7},{7,6},{8,9},{9,8},{10,11... | collective-permute-start | bytes 221192 | tf_op jit(solution)/shard_map/ppermute | solution.py:255
  27.8 0.0 collective-permute-done.15.far_ref
  27.8 0.8 %most.1 = (f32[64,1024]{1,0:T(8,128)}, f32[8,1024]{1,0:T(8,128)S(1)}) custom-call(f32[64,1152]{1,0:T(8,128)S(1)} %get-tuple-element.35.keep_ref, f32[72,1152]{1,0:T(8,128)S(1)} %collective-permute-done.15.far_ref, f32[8,1024]{1,0:T(8,128)S(1)} %get-tuple-element.31.n_ref), custom_call_target="tpu_custom_call" | custom-call | flops 10000000000 | bytes 4194304 | tf_op jit(solution)/shard_map/most/pallas_call | solution.py:292
  28.6 0.1 collective-permute-done.14.far_ref
  28.7 0.7 %rest.1 = f32[64,1024]{1,0:T(8,128)} custom-call(f32[16,1152]{1,0:T(8,128)S(1)} %last.5.own_ref, f32[16,1152]{1,0:T(8,128)S(1)} %collective-permute-done.14.far_ref, f32[8,1024]{1,0:T(8,128)S(1)} %get-tuple-element.37.s_ref, f32[64,1024]{1,0:T(8,128)} %get-tuple-element.38.most_ref), custom_call_target="tpu_custom_call", output_to_operand_aliasing={{}: (3, {})} | custom-call | tf_op jit(solution)/shard_map/rest/pallas_call | solution.py:374
  (2 shorter events, 0.0 us)
Async XLA Ops:
  1.3 5.4 %collective-permute-start.6 = (bf16[32,16,128]{2,1,0:T(8,128)(2,1)S(1)}, bf16[32,16,128]{2,1,0:T(8,128)(2,1)S(1)}, u32[]{:S(2)}, u32[]{:S(2)}) collective-permute-start(bf16[32,16,128]{2,1,0:T(8,128)(2,1)S(1)} %get-tuple-element.30.refs_0_), channel_id=1, source_target_pairs={{0,2},{2,6},{6,10},{10,14},{14,12},{12,8},{8,4},{4,0},{1,3},{3,7},... | collective-permute-start | bytes 393224 | tf_op jit(solution)/shard_map/ppermute | solution.py:312
  3.4 4.4 %collective-permute-start = (bf16[32,16,128]{2,1,0:T(8,128)(2,1)S(1)}, bf16[32,16,128]{2,1,0:T(8,128)(2,1)S(1)}, u32[]{:S(2)}, u32[]{:S(2)}) collective-permute-start(bf16[32,16,128]{2,1,0:T(8,128)(2,1)S(1)} %get-tuple-element.25.refs_0_), channel_id=1, source_target_pairs={{2,0},{6,2},{10,6},{14,10},{12,14},{8,12},{4,8},{0,4},{3,1},{7,3},... | collective-permute-start | bytes 393224 | tf_op jit(solution)/shard_map/ppermute | solution.py:315
  4.9 5.6 %collective-permute-start.4 = (bf16[32,16,128]{2,1,0:T(8,128)(2,1)S(1)}, bf16[32,16,128]{2,1,0:T(8,128)(2,1)S(1)}, u32[]{:S(2)}, u32[]{:S(2)}) collective-permute-start(bf16[32,16,128]{2,1,0:T(8,128)(2,1)S(1)} %get-tuple-element.25.refs_0_), channel_id=1, source_target_pairs={{0,2},{2,6},{6,10},{10,14},{14,12},{12,8},{8,4},{4,0},{1,3},{3,7},... | collective-permute-start | bytes 393224 | tf_op jit(solution)/shard_map/ppermute | solution.py:312
  6.3 5.2 %collective-permute-start.10 = (bf16[32,16,128]{2,1,0:T(8,128)(2,1)S(1)}, bf16[32,16,128]{2,1,0:T(8,128)(2,1)S(1)}, u32[]{:S(2)}, u32[]{:S(2)}) collective-permute-start(bf16[32,16,128]{2,1,0:T(8,128)(2,1)S(1)} %get-tuple-element.30.refs_0_), channel_id=1, source_target_pairs={{2,0},{6,2},{10,6},{14,10},{12,14},{8,12},{4,8},{0,4},{3,1},{7,3},... | collective-permute-start | bytes 393224 | tf_op jit(solution)/shard_map/ppermute | solution.py:315
  6.7 6.0 %collective-permute-start.7 = (bf16[32,16,128]{2,1,0:T(8,128)(2,1)S(1)}, bf16[32,16,128]{2,1,0:T(8,128)(2,1)S(1)}, u32[]{:S(2)}, u32[]{:S(2)}) collective-permute-start(bf16[32,16,128]{2,1,0:T(8,128)(2,1)S(1)} %collective-permute-done.6.refs_1_), channel_id=1, source_target_pairs={{0,2},{2,6},{6,10},{10,14},{14,12},{12,8},{8,4},{4,0},{1,3},{3,7},... | collective-permute-start | bytes 393224 | tf_op jit(solution)/shard_map/ppermute | solution.py:312
  7.8 6.1 %collective-permute-start.1 = (bf16[32,16,128]{2,1,0:T(8,128)(2,1)S(1)}, bf16[32,16,128]{2,1,0:T(8,128)(2,1)S(1)}, u32[]{:S(2)}, u32[]{:S(2)}) collective-permute-start(bf16[32,16,128]{2,1,0:T(8,128)(2,1)S(1)} %collective-permute-done.refs_2_), channel_id=1, source_target_pairs={{2,0},{6,2},{10,6},{14,10},{12,14},{8,12},{4,8},{0,4},{3,1},{7,3},... | collective-permute-start | bytes 393224 | tf_op jit(solution)/shard_map/ppermute | solution.py:315
  10.5 4.9 %collective-permute-start.5 = (bf16[32,16,128]{2,1,0:T(8,128)(2,1)S(1)}, bf16[32,16,128]{2,1,0:T(8,128)(2,1)S(1)}, u32[]{:S(2)}, u32[]{:S(2)}) collective-permute-start(bf16[32,16,128]{2,1,0:T(8,128)(2,1)S(1)} %collective-permute-done.4.refs_1_), channel_id=1, source_target_pairs={{0,2},{2,6},{6,10},{10,14},{14,12},{12,8},{8,4},{4,0},{1,3},{3,7},... | collective-permute-start | bytes 393224 | tf_op jit(solution)/shard_map/ppermute | solution.py:312
  11.5 4.8 %collective-permute-start.11 = (bf16[32,16,128]{2,1,0:T(8,128)(2,1)S(1)}, bf16[32,16,128]{2,1,0:T(8,128)(2,1)S(1)}, u32[]{:S(2)}, u32[]{:S(2)}) collective-permute-start(bf16[32,16,128]{2,1,0:T(8,128)(2,1)S(1)} %collective-permute-done.10.refs_2_), channel_id=1, source_target_pairs={{2,0},{6,2},{10,6},{14,10},{12,14},{8,12},{4,8},{0,4},{3,1},{7,3},... | collective-permute-start | bytes 393224 | tf_op jit(solution)/shard_map/ppermute | solution.py:315
  12.7 5.4 %collective-permute-start.8 = (bf16[32,16,128]{2,1,0:T(8,128)(2,1)S(1)}, bf16[32,16,128]{2,1,0:T(8,128)(2,1)S(1)}, u32[]{:S(2)}, u32[]{:S(2)}) collective-permute-start(bf16[32,16,128]{2,1,0:T(8,128)(2,1)S(1)} %collective-permute-done.7.refs_3_), channel_id=1, source_target_pairs={{0,2},{2,6},{6,10},{10,14},{14,12},{12,8},{8,4},{4,0},{1,3},{3,7},... | collective-permute-start | bytes 393224 | tf_op jit(solution)/shard_map/ppermute | solution.py:312
  13.9 5.2 %collective-permute-start.2 = (bf16[32,16,128]{2,1,0:T(8,128)(2,1)S(1)}, bf16[32,16,128]{2,1,0:T(8,128)(2,1)S(1)}, u32[]{:S(2)}, u32[]{:S(2)}) collective-permute-start(bf16[32,16,128]{2,1,0:T(8,128)(2,1)S(1)} %collective-permute-done.1.refs_4_), channel_id=1, source_target_pairs={{2,0},{6,2},{10,6},{14,10},{12,14},{8,12},{4,8},{0,4},{3,1},{7,3},... | collective-permute-start | bytes 393224 | tf_op jit(solution)/shard_map/ppermute | solution.py:315
  15.4 5.4 %collective-permute-start.13 = (bf16[32,16,128]{2,1,0:T(8,128)(2,1)S(1)}, bf16[32,16,128]{2,1,0:T(8,128)(2,1)S(1)}, u32[]{:S(2)}, u32[]{:S(2)}) collective-permute-start(bf16[32,16,128]{2,1,0:T(8,128)(2,1)S(1)} %collective-permute-done.5.refs_3_), channel_id=1, source_target_pairs={{0,2},{2,6},{6,10},{10,14},{14,12},{12,8},{8,4},{4,0},{1,3},{3,7},... | collective-permute-start | bytes 393224 | tf_op jit(solution)/shard_map/ppermute | solution.py:312
  16.3 5.8 %collective-permute-start.12 = (bf16[32,16,128]{2,1,0:T(8,128)(2,1)S(1)}, bf16[32,16,128]{2,1,0:T(8,128)(2,1)S(1)}, u32[]{:S(2)}, u32[]{:S(2)}) collective-permute-start(bf16[32,16,128]{2,1,0:T(8,128)(2,1)S(1)} %collective-permute-done.11.refs_4_), channel_id=1, source_target_pairs={{2,0},{6,2},{10,6},{14,10},{12,14},{8,12},{4,8},{0,4},{3,1},{7,3},... | collective-permute-start | bytes 393224 | tf_op jit(solution)/shard_map/ppermute | solution.py:315
  18.1 5.2 %collective-permute-start.9 = (bf16[32,16,128]{2,1,0:T(8,128)(2,1)S(1)}, bf16[32,16,128]{2,1,0:T(8,128)(2,1)S(1)}, u32[]{:S(2)}, u32[]{:S(2)}) collective-permute-start(bf16[32,16,128]{2,1,0:T(8,128)(2,1)S(1)} %collective-permute-done.8.refs_5_), channel_id=1, source_target_pairs={{0,2},{2,6},{6,10},{10,14},{14,12},{12,8},{8,4},{4,0},{1,3},{3,7},... | collective-permute-start | bytes 393224 | tf_op jit(solution)/shard_map/ppermute | solution.py:312
  19.1 6.8 %collective-permute-start.3 = (bf16[32,16,128]{2,1,0:T(8,128)(2,1)S(1)}, bf16[32,16,128]{2,1,0:T(8,128)(2,1)S(1)}, u32[]{:S(2)}, u32[]{:S(2)}) collective-permute-start(bf16[32,16,128]{2,1,0:T(8,128)(2,1)S(1)} %collective-permute-done.2.refs_6_), channel_id=1, source_target_pairs={{2,0},{6,2},{10,6},{14,10},{12,14},{8,12},{4,8},{0,4},{3,1},{7,3},... | collective-permute-start | bytes 393224 | tf_op jit(solution)/shard_map/ppermute | solution.py:315
  23.9 3.9 %collective-permute-start.15 = (f32[72,1152]{1,0:T(8,128)S(1)}, f32[72,1152]{1,0:T(8,128)S(1)}, u32[]{:S(2)}, u32[]{:S(2)}) collective-permute-start(f32[72,1152]{1,0:T(8,128)S(1)} %get-tuple-element.36), channel_id=1, source_target_pairs={{0,1},{1,0},{2,3},{3,2},{4,5},{5,4},{6,7},{7,6},{8,9},{9,8},{10,11... | collective-permute-start | bytes 995336 | tf_op jit(solution)/shard_map/ppermute | solution.py:255
  26.6 2.1 %collective-permute-start.14 = (f32[16,1152]{1,0:T(8,128)S(1)}, f32[16,1152]{1,0:T(8,128)S(1)}, u32[]{:S(2)}, u32[]{:S(2)}) collective-permute-start(f32[16,1152]{1,0:T(8,128)S(1)} %last.5.own_ref), channel_id=1, source_target_pairs={{0,1},{1,0},{2,3},{3,2},{4,5},{5,4},{6,7},{7,6},{8,9},{9,8},{10,11... | collective-permute-start | bytes 221192 | tf_op jit(solution)/shard_map/ppermute | solution.py:255

commit v9 on v8

--- a/solution.py
+++ b/solution.py
@@ -40,18 +40,14 @@
     queries = chunks[0].shape[1]
     own = pairs // len(chunks)
     span = own * modules
-    copies = [
-        pltpu.make_async_copy(x_ref.at[:, pl.ds(c * span, span), :], rows.at[c], sems.at[c])
-        for c in range(len(chunks))
-    ]
-    for copy in copies:
-        copy.start()
+    copy = pltpu.make_async_copy(x_ref, rows, sems)
+    copy.start()
+    copy.wait()
+    flat = rows.reshape(queries * span * len(chunks), LANES)
     for c, o_ref in enumerate(chunks):
-        copies[c].wait()
-        flat = rows.at[c].reshape(queries * span, LANES)
         for m in range(modules):
             for i in range(own):
-                got = flat[pl.ds(i * modules + m, queries, stride=span), :]
+                got = flat[pl.ds(c * span + i * modules + m, queries, stride=span * len(chunks)), :]
                 o_ref[m * own + i] = got.astype(jnp.bfloat16)
 
 
@@ -323,8 +319,8 @@
             in_specs=[HBM],
             out_specs=(VMEM, VMEM),
             scratch_shapes=[
-                pltpu.VMEM((2, queries, pairs * modules // 2, LANES), jnp.float32),
-                pltpu.SemaphoreType.DMA((2,)),
+                pltpu.VMEM((queries, pairs * modules, LANES), jnp.float32),
+                pltpu.SemaphoreType.DMA,
             ],
             compiler_params=PARAMS,
             name="queries",

time: 29.6 us -> 29.7 us (level)
  no operation moved by 1% of the time
where the time goes in v9:
time: 29.7 us; the launch traced here: 29.5 us
  starting transfers between devices  14.2 us (48%)
  Pallas kernels  9.04 us (30%)
  waiting for transfers between devices  6.13 us (21%)
    ppermute x7, starting transfers between devices, up(): return lax.ppermute(x, 'ex', up_pairs)  8.88 us
    ppermute x7, waiting for transfers between devices, up(): return lax.ppermute(x, 'ex', up_pairs)  6.02 us
    ppermute x2, starting transfers between devices, swapped(): return lax.ppermute(x, 'proj', [(i, (i + 1) % proj) for i in range(proj)])  3.16 us
    ppermute x7, starting transfers between devices, down(): return lax.ppermute(x, 'ex', down_pairs)  2.22 us
    pallas_call x2, Pallas kernels, token_work(): pl.pallas_call(functools.partial(token_kernel, modules, rank, core), out_...  1.42 us
    pallas_call x3, Pallas kernels, scored(): pl.pallas_call(functools.partial(core_kernel, core, kept, part, 2, module...  1.38 us
    pallas_call x1, Pallas kernels, local(): pl.pallas_call(functools.partial(query_kernel, modules, pairs), out_shape...  1.34 us
    pallas_call x1, Pallas kernels, bulk(): pl.pallas_call(functools.partial(late_kernel, count, parts, modules, rank...  1.28 us
  transfers between devices with their start and end apart: 16, of which 7 were waited for; matrix products, arithmetic and copies ran while one was open for 0% of the time, Pallas kernels for 24%

profile of v9, /device:TPU:1, one launch (start us, length us, event | category | flops | bytes accessed | tf_op | source)
XLA Modules:
  0.0 29.5 jit_solution(5161693494809821783)
XLA Ops:
  0.0 1.3 %queries.1 = (bf16[32,16,128]{2,1,0:T(8,128)(2,1)S(1)}, bf16[32,16,128]{2,1,0:T(8,128)(2,1)S(1)}) custom-call(f32[16,64,128]{2,1,0:T(8,128)} %bitcast.9), custom_call_target="tpu_custom_call" | custom-call | tf_op jit(solution)/shard_map/queries/pallas_call | solution.py:316
  1.3 2.1 %collective-permute-start.6 = (bf16[32,16,128]{2,1,0:T(8,128)(2,1)S(1)}, bf16[32,16,128]{2,1,0:T(8,128)(2,1)S(1)}, u32[]{:S(2)}, u32[]{:S(2)}) collective-permute-start(bf16[32,16,128]{2,1,0:T(8,128)(2,1)S(1)} %get-tuple-element.30.refs_0_), channel_id=1, source_target_pairs={{0,2},{2,6},{6,10},{10,14},{14,12},{12,8},{8,4},{4,0},{1,3},{3,7},... | collective-permute-start | bytes 393224 | tf_op jit(solution)/shard_map/ppermute | solution.py:308
  3.4 0.2 collective-permute-start
  3.6 1.4 %tokens.2 = (bf16[2,2,64,1024]{3,2,1,0:T(8,128)(2,1)S(1)}, f32[8,1024]{1,0:T(8,128)S(1)}) custom-call(bf16[2048,128]{1,0:T(8,128)(2,1)} %bitcast.7), custom_call_target="tpu_custom_call" | custom-call | tf_op jit(solution)/shard_map/tokens/pallas_call | solution.py:232
  5.0 1.4 %collective-permute-start.4 = (bf16[32,16,128]{2,1,0:T(8,128)(2,1)S(1)}, bf16[32,16,128]{2,1,0:T(8,128)(2,1)S(1)}, u32[]{:S(2)}, u32[]{:S(2)}) collective-permute-start(bf16[32,16,128]{2,1,0:T(8,128)(2,1)S(1)} %get-tuple-element.25.refs_0_), channel_id=1, source_target_pairs={{0,2},{2,6},{6,10},{10,14},{14,12},{12,8},{8,4},{4,0},{1,3},{3,7},... | collective-permute-start | bytes 393224 | tf_op jit(solution)/shard_map/ppermute | solution.py:308
  6.4 0.2 collective-permute-start.10
  6.5 0.2 collective-permute-done.6.refs_1_
  6.8 1.1 %collective-permute-start.7 = (bf16[32,16,128]{2,1,0:T(8,128)(2,1)S(1)}, bf16[32,16,128]{2,1,0:T(8,128)(2,1)S(1)}, u32[]{:S(2)}, u32[]{:S(2)}) collective-permute-start(bf16[32,16,128]{2,1,0:T(8,128)(2,1)S(1)} %collective-permute-done.6.refs_1_), channel_id=1, source_target_pairs={{0,2},{2,6},{6,10},{10,14},{14,12},{12,8},{8,4},{4,0},{1,3},{3,7},... | collective-permute-start | bytes 393224 | tf_op jit(solution)/shard_map/ppermute | solution.py:308
  7.9 0.0 collective-permute-done.refs_2_
  7.9 0.3 %collective-permute-start.1 = (bf16[32,16,128]{2,1,0:T(8,128)(2,1)S(1)}, bf16[32,16,128]{2,1,0:T(8,128)(2,1)S(1)}, u32[]{:S(2)}, u32[]{:S(2)}) collective-permute-start(bf16[32,16,128]{2,1,0:T(8,128)(2,1)S(1)} %collective-permute-done.refs_2_), channel_id=1, source_target_pairs={{2,0},{6,2},{10,6},{14,10},{12,14},{8,12},{4,8},{0,4},{3,1},{7,3},... | collective-permute-start | bytes 393224 | tf_op jit(solution)/shard_map/ppermute | solution.py:311
  8.2 2.3 %collective-permute-done.4.refs_1_ = bf16[32,16,128]{2,1,0:T(8,128)(2,1)S(1)} collective-permute-done((bf16[32,16,128]{2,1,0:T(8,128)(2,1)S(1)}, bf16[32,16,128]{2,1,0:T(8,128)(2,1)S(1)}, u32[]{:S(2)}, u32[]{:S(2)}) %collective-permute-start.4) | collective-permute-done | bytes 131104 | tf_op jit(solution)/shard_map/ppermute | solution.py:308
  10.6 1.0 %collective-permute-start.5 = (bf16[32,16,128]{2,1,0:T(8,128)(2,1)S(1)}, bf16[32,16,128]{2,1,0:T(8,128)(2,1)S(1)}, u32[]{:S(2)}, u32[]{:S(2)}) collective-permute-start(bf16[32,16,128]{2,1,0:T(8,128)(2,1)S(1)} %collective-permute-done.4.refs_1_), channel_id=1, source_target_pairs={{0,2},{2,6},{6,10},{10,14},{14,12},{12,8},{8,4},{4,0},{1,3},{3,7},... | collective-permute-start | bytes 393224 | tf_op jit(solution)/shard_map/ppermute | solution.py:308
  11.6 0.0 collective-permute-done.10.refs_2_
  11.6 0.4 %collective-permute-start.11 = (bf16[32,16,128]{2,1,0:T(8,128)(2,1)S(1)}, bf16[32,16,128]{2,1,0:T(8,128)(2,1)S(1)}, u32[]{:S(2)}, u32[]{:S(2)}) collective-permute-start(bf16[32,16,128]{2,1,0:T(8,128)(2,1)S(1)} %collective-permute-done.10.refs_2_), channel_id=1, source_target_pairs={{2,0},{6,2},{10,6},{14,10},{12,14},{8,12},{4,8},{0,4},{3,1},{7,3},... | collective-permute-start | bytes 393224 | tf_op jit(solution)/shard_map/ppermute | solution.py:311
  12.0 0.7 %collective-permute-done.7.refs_3_ = bf16[32,16,128]{2,1,0:T(8,128)(2,1)S(1)} collective-permute-done((bf16[32,16,128]{2,1,0:T(8,128)(2,1)S(1)}, bf16[32,16,128]{2,1,0:T(8,128)(2,1)S(1)}, u32[]{:S(2)}, u32[]{:S(2)}) %collective-permute-start.7) | collective-permute-done | bytes 131104 | tf_op jit(solution)/shard_map/ppermute | solution.py:308
  12.8 1.3 %collective-permute-start.8 = (bf16[32,16,128]{2,1,0:T(8,128)(2,1)S(1)}, bf16[32,16,128]{2,1,0:T(8,128)(2,1)S(1)}, u32[]{:S(2)}, u32[]{:S(2)}) collective-permute-start(bf16[32,16,128]{2,1,0:T(8,128)(2,1)S(1)} %collective-permute-done.7.refs_3_), channel_id=1, source_target_pairs={{0,2},{2,6},{6,10},{10,14},{14,12},{12,8},{8,4},{4,0},{1,3},{3,7},... | collective-permute-start | bytes 393224 | tf_op jit(solution)/shard_map/ppermute | solution.py:308
  14.0 0.0 collective-permute-done.1.refs_4_
  14.0 0.2 collective-permute-start.2
  14.2 1.2 %collective-permute-done.5.refs_3_ = bf16[32,16,128]{2,1,0:T(8,128)(2,1)S(1)} collective-permute-done((bf16[32,16,128]{2,1,0:T(8,128)(2,1)S(1)}, bf16[32,16,128]{2,1,0:T(8,128)(2,1)S(1)}, u32[]{:S(2)}, u32[]{:S(2)}) %collective-permute-start.5) | collective-permute-done | bytes 131104 | tf_op jit(solution)/shard_map/ppermute | solution.py:308
  15.4 1.0 %collective-permute-start.13 = (bf16[32,16,128]{2,1,0:T(8,128)(2,1)S(1)}, bf16[32,16,128]{2,1,0:T(8,128)(2,1)S(1)}, u32[]{:S(2)}, u32[]{:S(2)}) collective-permute-start(bf16[32,16,128]{2,1,0:T(8,128)(2,1)S(1)} %collective-permute-done.5.refs_3_), channel_id=1, source_target_pairs={{0,2},{2,6},{6,10},{10,14},{14,12},{12,8},{8,4},{4,0},{1,3},{3,7},... | collective-permute-start | bytes 393224 | tf_op jit(solution)/shard_map/ppermute | solution.py:308
  16.4 0.0 collective-permute-done.11.refs_4_
  16.4 0.5 %collective-permute-start.12 = (bf16[32,16,128]{2,1,0:T(8,128)(2,1)S(1)}, bf16[32,16,128]{2,1,0:T(8,128)(2,1)S(1)}, u32[]{:S(2)}, u32[]{:S(2)}) collective-permute-start(bf16[32,16,128]{2,1,0:T(8,128)(2,1)S(1)} %collective-permute-done.11.refs_4_), channel_id=1, source_target_pairs={{2,0},{6,2},{10,6},{14,10},{12,14},{8,12},{4,8},{0,4},{3,1},{7,3},... | collective-permute-start | bytes 393224 | tf_op jit(solution)/shard_map/ppermute | solution.py:311
  16.9 1.2 %collective-permute-done.8.refs_5_ = bf16[32,16,128]{2,1,0:T(8,128)(2,1)S(1)} collective-permute-done((bf16[32,16,128]{2,1,0:T(8,128)(2,1)S(1)}, bf16[32,16,128]{2,1,0:T(8,128)(2,1)S(1)}, u32[]{:S(2)}, u32[]{:S(2)}) %collective-permute-start.8) | collective-permute-done | bytes 131104 | tf_op jit(solution)/shard_map/ppermute | solution.py:308
  18.1 1.0 %collective-permute-start.9 = (bf16[32,16,128]{2,1,0:T(8,128)(2,1)S(1)}, bf16[32,16,128]{2,1,0:T(8,128)(2,1)S(1)}, u32[]{:S(2)}, u32[]{:S(2)}) collective-permute-start(bf16[32,16,128]{2,1,0:T(8,128)(2,1)S(1)} %collective-permute-done.8.refs_5_), channel_id=1, source_target_pairs={{0,2},{2,6},{6,10},{10,14},{14,12},{12,8},{8,4},{4,0},{1,3},{3,7},... | collective-permute-start | bytes 393224 | tf_op jit(solution)/shard_map/ppermute | solution.py:308
  19.2 0.0 collective-permute-done.2.refs_6_
  19.2 0.4 %collective-permute-start.3 = (bf16[32,16,128]{2,1,0:T(8,128)(2,1)S(1)}, bf16[32,16,128]{2,1,0:T(8,128)(2,1)S(1)}, u32[]{:S(2)}, u32[]{:S(2)}) collective-permute-start(bf16[32,16,128]{2,1,0:T(8,128)(2,1)S(1)} %collective-permute-done.2.refs_6_), channel_id=1, source_target_pairs={{2,0},{6,2},{10,6},{14,10},{12,14},{8,12},{4,8},{0,4},{3,1},{7,3},... | collective-permute-start | bytes 393224 | tf_op jit(solution)/shard_map/ppermute | solution.py:311
  19.6 1.3 %early.1.refs_8_ = f32[96,1152]{1,0:T(8,128)S(1)} custom-call(bf16[32,16,128]{2,1,0:T(8,128)(2,1)S(1)} %get-tuple-element.30.refs_0_, bf16[32,16,128]{2,1,0:T(8,128)(2,1)S(1)} %collective-permute-done.6.refs_1_, bf16[32,16,128]{2,1,0:T(8,128)(2,1)S(1)} %collective-permute-done.10.refs_2_, bf16[32,16,128]{2,1,0:T(8,128)(2,1)S(1)} %collective-permute-done.7.refs_3_, ...), custom_call_target="tpu_custom_call" | custom-call | flops 810000000 | bytes 1024 | tf_op jit(solution)/shard_map/early/pallas_call | solution.py:255
  20.9 0.0 collective-permute-done.13.refs_5_
  20.9 1.3 %late.1.sum_ref = f32[112,1152]{1,0:T(8,128)S(1)} custom-call(bf16[32,16,128]{2,1,0:T(8,128)(2,1)S(1)} %get-tuple-element.25.refs_0_, bf16[32,16,128]{2,1,0:T(8,128)(2,1)S(1)} %collective-permute-done.4.refs_1_, bf16[32,16,128]{2,1,0:T(8,128)(2,1)S(1)} %collective-permute-done.refs_2_, bf16[32,16,128]{2,1,0:T(8,128)(2,1)S(1)} %collective-permute-done.5.refs_3_, ...), custom_call_target="tpu_custom_call" | custom-call | flops 580000000 | bytes 1024 | tf_op jit(solution)/shard_map/late/pallas_call | solution.py:264
  22.2 0.0 collective-permute-done.12.chunk
  22.2 0.8 %third.1 = (f32[64,1152]{1,0:T(8,128)S(1)}, f32[72,1152]{1,0:T(8,128)S(1)}) custom-call(bf16[32,16,128]{2,1,0:T(8,128)(2,1)S(1)} %collective-permute-done.12.chunk, bf16[2,2,64,1024]{3,2,1,0:T(8,128)(2,1)S(1)} %get-tuple-element.29.refs_6_.refs_7_.p_ref, f32[8,1024]{1,0:T(8,128)S(1)} %get-tuple-element.31.n_ref, f32[112,1152]{1,0:T(8,128)S(1)} %late.1.sum_ref), custom_call_target="tpu_custom_call" | custom-call | flops 230000000 | bytes 1024 | tf_op jit(solution)/shard_map/third/pallas_call | solution.py:273
  23.0 0.3 %collective-permute-done.9.chunk = bf16[32,16,128]{2,1,0:T(8,128)(2,1)S(1)} collective-permute-done((bf16[32,16,128]{2,1,0:T(8,128)(2,1)S(1)}, bf16[32,16,128]{2,1,0:T(8,128)(2,1)S(1)}, u32[]{:S(2)}, u32[]{:S(2)}) %collective-permute-start.9) | collective-permute-done | bytes 131104 | tf_op jit(solution)/shard_map/ppermute | solution.py:308
  23.3 0.7 %last.3.refs_0_ = f32[16,1152]{1,0:T(8,128)S(1)} custom-call(bf16[32,16,128]{2,1,0:T(8,128)(2,1)S(1)} %collective-permute-done.9.chunk, bf16[2,2,64,1024]{3,2,1,0:T(8,128)(2,1)S(1)} %get-tuple-element.29.refs_6_.refs_7_.p_ref), custom_call_target="tpu_custom_call" | custom-call | flops 1000000 | bytes 1024 | tf_op jit(solution)/shard_map/last/pallas_call | solution.py:354
  24.0 2.0 %collective-permute-start.15 = (f32[72,1152]{1,0:T(8,128)S(1)}, f32[72,1152]{1,0:T(8,128)S(1)}, u32[]{:S(2)}, u32[]{:S(2)}) collective-permute-start(f32[72,1152]{1,0:T(8,128)S(1)} %get-tuple-element.36), channel_id=1, source_target_pairs={{0,1},{1,0},{2,3},{3,2},{4,5},{5,4},{6,7},{7,6},{8,9},{9,8},{10,11... | collective-permute-start | bytes 995336 | tf_op jit(solution)/shard_map/ppermute | solution.py:251
  26.0 0.0 collective-permute-done.3.chunk
  26.0 0.7 %last.5.own_ref = f32[16,1152]{1,0:T(8,128)S(1)} custom-call(bf16[32,16,128]{2,1,0:T(8,128)(2,1)S(1)} %collective-permute-done.3.chunk, bf16[2,2,64,1024]{3,2,1,0:T(8,128)(2,1)S(1)} %get-tuple-element.29.refs_6_.refs_7_.p_ref, f32[16,1152]{1,0:T(8,128)S(1)} %last.4.refs_0_), custom_call_target="tpu_custom_call" | custom-call | flops 10000000000 | bytes 4194304 | tf_op jit(solution)/shard_map/last/pallas_call | solution.py:354
  26.7 1.2 %collective-permute-start.14 = (f32[16,1152]{1,0:T(8,128)S(1)}, f32[16,1152]{1,0:T(8,128)S(1)}, u32[]{:S(2)}, u32[]{:S(2)}) collective-permute-start(f32[16,1152]{1,0:T(8,128)S(1)} %last.5.own_ref), channel_id=1, source_target_pairs={{0,1},{1,0},{2,3},{3,2},{4,5},{5,4},{6,7},{7,6},{8,9},{9,8},{10,11... | collective-permute-start | bytes 221192 | tf_op jit(solution)/shard_map/ppermute | solution.py:251
  27.9 0.0 collective-permute-done.15.far_ref
  27.9 0.8 %most.1 = (f32[64,1024]{1,0:T(8,128)}, f32[8,1024]{1,0:T(8,128)S(1)}) custom-call(f32[64,1152]{1,0:T(8,128)S(1)} %get-tuple-element.35.keep_ref, f32[72,1152]{1,0:T(8,128)S(1)} %collective-permute-done.15.far_ref, f32[8,1024]{1,0:T(8,128)S(1)} %get-tuple-element.31.n_ref), custom_call_target="tpu_custom_call" | custom-call | flops 10000000000 | bytes 4194304 | tf_op jit(solution)/shard_map/most/pallas_call | solution.py:288
  28.7 0.1 collective-permute-done.14.far_ref
  28.8 0.7 %rest.1 = f32[64,1024]{1,0:T(8,128)} custom-call(f32[16,1152]{1,0:T(8,128)S(1)} %last.5.own_ref, f32[16,1152]{1,0:T(8,128)S(1)} %collective-permute-done.14.far_ref, f32[8,1024]{1,0:T(8,128)S(1)} %get-tuple-element.37.s_ref, f32[64,1024]{1,0:T(8,128)} %get-tuple-element.38.most_ref), custom_call_target="tpu_custom_call", output_to_operand_aliasing={{}: (3, {})} | custom-call | tf_op jit(solution)/shard_map/rest/pallas_call | solution.py:370
  (2 shorter events, 0.0 us)
Async XLA Ops:
  1.3 5.4 %collective-permute-start.6 = (bf16[32,16,128]{2,1,0:T(8,128)(2,1)S(1)}, bf16[32,16,128]{2,1,0:T(8,128)(2,1)S(1)}, u32[]{:S(2)}, u32[]{:S(2)}) collective-permute-start(bf16[32,16,128]{2,1,0:T(8,128)(2,1)S(1)} %get-tuple-element.30.refs_0_), channel_id=1, source_target_pairs={{0,2},{2,6},{6,10},{10,14},{14,12},{12,8},{8,4},{4,0},{1,3},{3,7},... | collective-permute-start | bytes 393224 | tf_op jit(solution)/shard_map/ppermute | solution.py:308
  3.4 4.4 %collective-permute-start = (bf16[32,16,128]{2,1,0:T(8,128)(2,1)S(1)}, bf16[32,16,128]{2,1,0:T(8,128)(2,1)S(1)}, u32[]{:S(2)}, u32[]{:S(2)}) collective-permute-start(bf16[32,16,128]{2,1,0:T(8,128)(2,1)S(1)} %get-tuple-element.25.refs_0_), channel_id=1, source_target_pairs={{2,0},{6,2},{10,6},{14,10},{12,14},{8,12},{4,8},{0,4},{3,1},{7,3},... | collective-permute-start | bytes 393224 | tf_op jit(solution)/shard_map/ppermute | solution.py:311
  5.0 5.6 %collective-permute-start.4 = (bf16[32,16,128]{2,1,0:T(8,128)(2,1)S(1)}, bf16[32,16,128]{2,1,0:T(8,128)(2,1)S(1)}, u32[]{:S(2)}, u32[]{:S(2)}) collective-permute-start(bf16[32,16,128]{2,1,0:T(8,128)(2,1)S(1)} %get-tuple-element.25.refs_0_), channel_id=1, source_target_pairs={{0,2},{2,6},{6,10},{10,14},{14,12},{12,8},{8,4},{4,0},{1,3},{3,7},... | collective-permute-start | bytes 393224 | tf_op jit(solution)/shard_map/ppermute | solution.py:308
  6.4 5.2 %collective-permute-start.10 = (bf16[32,16,128]{2,1,0:T(8,128)(2,1)S(1)}, bf16[32,16,128]{2,1,0:T(8,128)(2,1)S(1)}, u32[]{:S(2)}, u32[]{:S(2)}) collective-permute-start(bf16[32,16,128]{2,1,0:T(8,128)(2,1)S(1)} %get-tuple-element.30.refs_0_), channel_id=1, source_target_pairs={{2,0},{6,2},{10,6},{14,10},{12,14},{8,12},{4,8},{0,4},{3,1},{7,3},... | collective-permute-start | bytes 393224 | tf_op jit(solution)/shard_map/ppermute | solution.py:311
  6.8 6.0 %collective-permute-start.7 = (bf16[32,16,128]{2,1,0:T(8,128)(2,1)S(1)}, bf16[32,16,128]{2,1,0:T(8,128)(2,1)S(1)}, u32[]{:S(2)}, u32[]{:S(2)}) collective-permute-start(bf16[32,16,128]{2,1,0:T(8,128)(2,1)S(1)} %collective-permute-done.6.refs_1_), channel_id=1, source_target_pairs={{0,2},{2,6},{6,10},{10,14},{14,12},{12,8},{8,4},{4,0},{1,3},{3,7},... | collective-permute-start | bytes 393224 | tf_op jit(solution)/shard_map/ppermute | solution.py:308
  7.9 6.1 %collective-permute-start.1 = (bf16[32,16,128]{2,1,0:T(8,128)(2,1)S(1)}, bf16[32,16,128]{2,1,0:T(8,128)(2,1)S(1)}, u32[]{:S(2)}, u32[]{:S(2)}) collective-permute-start(bf16[32,16,128]{2,1,0:T(8,128)(2,1)S(1)} %collective-permute-done.refs_2_), channel_id=1, source_target_pairs={{2,0},{6,2},{10,6},{14,10},{12,14},{8,12},{4,8},{0,4},{3,1},{7,3},... | collective-permute-start | bytes 393224 | tf_op jit(solution)/shard_map/ppermute | solution.py:311
  10.6 4.9 %collective-permute-start.5 = (bf16[32,16,128]{2,1,0:T(8,128)(2,1)S(1)}, bf16[32,16,128]{2,1,0:T(8,128)(2,1)S(1)}, u32[]{:S(2)}, u32[]{:S(2)}) collective-permute-start(bf16[32,16,128]{2,1,0:T(8,128)(2,1)S(1)} %collective-permute-done.4.refs_1_), channel_id=1, source_target_pairs={{0,2},{2,6},{6,10},{10,14},{14,12},{12,8},{8,4},{4,0},{1,3},{3,7},... | collective-permute-start | bytes 393224 | tf_op jit(solution)/shard_map/ppermute | solution.py:308
  11.6 4.8 %collective-permute-start.11 = (bf16[32,16,128]{2,1,0:T(8,128)(2,1)S(1)}, bf16[32,16,128]{2,1,0:T(8,128)(2,1)S(1)}, u32[]{:S(2)}, u32[]{:S(2)}) collective-permute-start(bf16[32,16,128]{2,1,0:T(8,128)(2,1)S(1)} %collective-permute-done.10.refs_2_), channel_id=1, source_target_pairs={{2,0},{6,2},{10,6},{14,10},{12,14},{8,12},{4,8},{0,4},{3,1},{7,3},... | collective-permute-start | bytes 393224 | tf_op jit(solution)/shard_map/ppermute | solution.py:311
  12.8 5.4 %collective-permute-start.8 = (bf16[32,16,128]{2,1,0:T(8,128)(2,1)S(1)}, bf16[32,16,128]{2,1,0:T(8,128)(2,1)S(1)}, u32[]{:S(2)}, u32[]{:S(2)}) collective-permute-start(bf16[32,16,128]{2,1,0:T(8,128)(2,1)S(1)} %collective-permute-done.7.refs_3_), channel_id=1, source_target_pairs={{0,2},{2,6},{6,10},{10,14},{14,12},{12,8},{8,4},{4,0},{1,3},{3,7},... | collective-permute-start | bytes 393224 | tf_op jit(solution)/shard_map/ppermute | solution.py:308
  14.0 5.2 %collective-permute-start.2 = (bf16[32,16,128]{2,1,0:T(8,128)(2,1)S(1)}, bf16[32,16,128]{2,1,0:T(8,128)(2,1)S(1)}, u32[]{:S(2)}, u32[]{:S(2)}) collective-permute-start(bf16[32,16,128]{2,1,0:T(8,128)(2,1)S(1)} %collective-permute-done.1.refs_4_), channel_id=1, source_target_pairs={{2,0},{6,2},{10,6},{14,10},{12,14},{8,12},{4,8},{0,4},{3,1},{7,3},... | collective-permute-start | bytes 393224 | tf_op jit(solution)/shard_map/ppermute | solution.py:311
  15.4 5.4 %collective-permute-start.13 = (bf16[32,16,128]{2,1,0:T(8,128)(2,1)S(1)}, bf16[32,16,128]{2,1,0:T(8,128)(2,1)S(1)}, u32[]{:S(2)}, u32[]{:S(2)}) collective-permute-start(bf16[32,16,128]{2,1,0:T(8,128)(2,1)S(1)} %collective-permute-done.5.refs_3_), channel_id=1, source_target_pairs={{0,2},{2,6},{6,10},{10,14},{14,12},{12,8},{8,4},{4,0},{1,3},{3,7},... | collective-permute-start | bytes 393224 | tf_op jit(solution)/shard_map/ppermute | solution.py:308
  16.4 5.8 %collective-permute-start.12 = (bf16[32,16,128]{2,1,0:T(8,128)(2,1)S(1)}, bf16[32,16,128]{2,1,0:T(8,128)(2,1)S(1)}, u32[]{:S(2)}, u32[]{:S(2)}) collective-permute-start(bf16[32,16,128]{2,1,0:T(8,128)(2,1)S(1)} %collective-permute-done.11.refs_4_), channel_id=1, source_target_pairs={{2,0},{6,2},{10,6},{14,10},{12,14},{8,12},{4,8},{0,4},{3,1},{7,3},... | collective-permute-start | bytes 393224 | tf_op jit(solution)/shard_map/ppermute | solution.py:311
  18.1 5.2 %collective-permute-start.9 = (bf16[32,16,128]{2,1,0:T(8,128)(2,1)S(1)}, bf16[32,16,128]{2,1,0:T(8,128)(2,1)S(1)}, u32[]{:S(2)}, u32[]{:S(2)}) collective-permute-start(bf16[32,16,128]{2,1,0:T(8,128)(2,1)S(1)} %collective-permute-done.8.refs_5_), channel_id=1, source_target_pairs={{0,2},{2,6},{6,10},{10,14},{14,12},{12,8},{8,4},{4,0},{1,3},{3,7},... | collective-permute-start | bytes 393224 | tf_op jit(solution)/shard_map/ppermute | solution.py:308
  19.2 6.8 %collective-permute-start.3 = (bf16[32,16,128]{2,1,0:T(8,128)(2,1)S(1)}, bf16[32,16,128]{2,1,0:T(8,128)(2,1)S(1)}, u32[]{:S(2)}, u32[]{:S(2)}) collective-permute-start(bf16[32,16,128]{2,1,0:T(8,128)(2,1)S(1)} %collective-permute-done.2.refs_6_), channel_id=1, source_target_pairs={{2,0},{6,2},{10,6},{14,10},{12,14},{8,12},{4,8},{0,4},{3,1},{7,3},... | collective-permute-start | bytes 393224 | tf_op jit(solution)/shard_map/ppermute | solution.py:311
  24.0 3.9 %collective-permute-start.15 = (f32[72,1152]{1,0:T(8,128)S(1)}, f32[72,1152]{1,0:T(8,128)S(1)}, u32[]{:S(2)}, u32[]{:S(2)}) collective-permute-start(f32[72,1152]{1,0:T(8,128)S(1)} %get-tuple-element.36), channel_id=1, source_target_pairs={{0,1},{1,0},{2,3},{3,2},{4,5},{5,4},{6,7},{7,6},{8,9},{9,8},{10,11... | collective-permute-start | bytes 995336 | tf_op jit(solution)/shard_map/ppermute | solution.py:251
  26.7 2.1 %collective-permute-start.14 = (f32[16,1152]{1,0:T(8,128)S(1)}, f32[16,1152]{1,0:T(8,128)S(1)}, u32[]{:S(2)}, u32[]{:S(2)}) collective-permute-start(f32[16,1152]{1,0:T(8,128)S(1)} %last.5.own_ref), channel_id=1, source_target_pairs={{0,1},{1,0},{2,3},{3,2},{4,5},{5,4},{6,7},{7,6},{8,9},{9,8},{10,11... | collective-permute-start | bytes 221192 | tf_op jit(solution)/shard_map/ppermute | solution.py:251
